TPU v7x, 32 devices: a whole 2x2x4 slice. The times are simulated.
32 devices in a mesh: cell: 8 (over z, core), vel: 4 (over y, x).
Axes of the slice: x: 2, y: 2, z: 4, core: 2. Of those that a mesh axis runs over, the one named last changes fastest.
Arguments:
- distribution: float32 [64, 64, 4096], P(None, 'cell', 'vel'), may hold values from 0.2 to 2
- cell_type: int32 [64, 64], P(None, 'cell'), may hold values from 0 to 2, as said below
- first_kernel: float32 [16, 4096], replicated, may hold values from -1.5 to 1.5
- second_kernel: float32 [16, 4096], replicated, may hold values from -1.5 to 1.5
- loss_kernel: float32 [4096], replicated, may hold values from -4 to 4
Outputs:
- updated: float32 [64, 64, 4096], P(None, 'cell', 'vel')
Inputs may be any that keep to these rules, and one draw needn't show every extreme that they name: `cell_type`: cells with x = 0, x = 63 or y = 0 are 1, the other cells with y = 63 are 2, and every other cell is 1 with probability 1/40, else 0.
All inputs are finite; a program needn't handle non-finite values.
Results may differ from a plain program's by a relative error of at most 0.0004.
Values sent between devices are 32-bit elements; how exact they have to be, the bound alone decides.
No kernel may reach another device: no remote copies, remote signals or barrier semaphores. Data moves between devices by JAX's collectives and lax.ppermute only.
A program may use at most 128 MiB of HBM per device.

v0:
```python
import math

import jax
import jax.numpy as jnp
from jax import lax
from jax.sharding import PartitionSpec as P

NVEL = 16
DIRS = 16


courant = 0.45
collision_timestep = 0.1
pass_forms = ("ai,ijkc->ajkc", "aj,ijkc->iakc", "ak,ijkc->ijac")


def padded_2(cells, sides, width):
    for axis, dim in sides:
        count = lax.axis_size(axis)
        ends = count - 1
        head = lax.slice_in_dim(cells, 0, width, axis=dim)
        tail = lax.slice_in_dim(cells, cells.shape[dim] - width, cells.shape[dim], axis=dim)
        cells = jnp.concatenate(
            [
                lax.ppermute(tail, axis, [(i, (i + 1) % count) for i in range(ends)]),
                cells,
                lax.ppermute(head, axis, [((i + 1) % count, i) for i in range(ends)]),
            ],
            axis=dim,
        )
    return cells


def components(nvel):
    levels = (2.0 * jnp.arange(nvel, dtype=jnp.float32) - (nvel - 1)) / (nvel - 1)
    along_x = jnp.repeat(levels, nvel * nvel)
    along_y = jnp.tile(jnp.repeat(levels, nvel), nvel)
    along_z = jnp.tile(levels, nvel * nvel)
    return (along_x, along_y, along_z)


def wall_tables(along_x, along_y, along_z):
    still_wall = jnp.exp(-4.5 * (along_x * along_x + along_y * along_y + along_z * along_z))
    still_wall = still_wall / jnp.sum(still_wall)
    moving = jnp.exp(
        -0.5 * ((3.0 * along_x - 1.0) ** 2 + 9.0 * along_y * along_y + 9.0 * along_z * along_z)
    )
    moving = moving / jnp.sum(moving)
    return (still_wall, moving)


def fourier_tables(nvel):
    indices = jnp.arange(nvel, dtype=jnp.int32)
    angles = 2.0 * math.pi * (indices[:, None] * indices[None, :] % nvel).astype(jnp.float32) / nvel
    cosine = jnp.cos(angles)
    sine_part = jnp.sin(angles)
    return (
        cosine.astype(jnp.bfloat16),
        (-sine_part).astype(jnp.bfloat16),
        (cosine / nvel).astype(jnp.bfloat16),
        (sine_part / nvel).astype(jnp.bfloat16),
    )


def apply_table(matrix, operand, pattern):
    return jnp.einsum(pattern, matrix, operand, preferred_element_type=jnp.float32)


def real_pass(operand, cos_table, sin_table, pattern):
    return (
        apply_table(cos_table, operand, pattern).astype(jnp.bfloat16),
        apply_table(sin_table, operand, pattern).astype(jnp.bfloat16),
    )


def complex_pass(real_part, imag_part, cos_table, sin_table, pattern):
    new_real = apply_table(cos_table, real_part, pattern) - apply_table(
        sin_table, imag_part, pattern
    )
    new_imag = apply_table(cos_table, imag_part, pattern) + apply_table(
        sin_table, real_part, pattern
    )
    return (new_real.astype(jnp.bfloat16), new_imag.astype(jnp.bfloat16))


def last_pass(real_part, imag_part, cos_table, sin_table, pattern):
    return apply_table(cos_table, real_part, pattern) - apply_table(sin_table, imag_part, pattern)


def spectrum_of(rounded, tables):
    real_part, imag_part = real_pass(rounded, tables[0], tables[1], pass_forms[0])
    real_part, imag_part = complex_pass(real_part, imag_part, tables[0], tables[1], pass_forms[1])
    return complex_pass(real_part, imag_part, tables[0], tables[1], pass_forms[2])


def inverse_of(kernel, spec_real, spec_imag, tables):
    weight = kernel[..., None]
    real_part = (weight * spec_real).astype(jnp.bfloat16)
    imag_part = (weight * spec_imag).astype(jnp.bfloat16)
    real_part, imag_part = complex_pass(real_part, imag_part, tables[2], tables[3], pass_forms[0])
    real_part, imag_part = complex_pass(real_part, imag_part, tables[2], tables[3], pass_forms[1])
    return last_pass(real_part, imag_part, tables[2], tables[3], pass_forms[2])


def collide(moved_block, kern_first, kern_second, kern_loss, tables):
    rounded = moved_block.astype(jnp.bfloat16)
    spec_real, spec_imag = spectrum_of(rounded, tables)

    def add_direction(direction, running):
        return running + inverse_of(
            kern_first[direction], spec_real, spec_imag, tables
        ) * inverse_of(kern_second[direction], spec_real, spec_imag, tables)

    gain = lax.fori_loop(
        0, kern_first.shape[0], add_direction, jnp.zeros(moved_block.shape, jnp.float32)
    )
    return gain - moved_block * inverse_of(kern_loss, spec_real, spec_imag, tables)


def transport(padded, along_x, along_y):
    center = padded[1:-1, 1:-1]
    back_x = center - padded[:-2, 1:-1]
    front_x = padded[2:, 1:-1] - center
    back_y = center - padded[1:-1, :-2]
    front_y = padded[1:-1, 2:] - center
    plus_x = jnp.maximum(along_x, 0.0)[None, None, :]
    minus_x = jnp.minimum(along_x, 0.0)[None, None, :]
    plus_y = jnp.maximum(along_y, 0.0)[None, None, :]
    minus_y = jnp.minimum(along_y, 0.0)[None, None, :]
    return -courant * (plus_x * back_x + minus_x * front_x + plus_y * back_y + minus_y * front_y)


def on_device(distribution, cell_type, first_kernel, second_kernel, loss_kernel):
    all_rows, cell_cols, block_vel = distribution.shape
    groups = lax.axis_size("vel")
    rank = lax.axis_index("vel")
    sub_rows = all_rows // groups
    along_x, along_y, along_z = components(NVEL)
    still_wall, moving = wall_tables(along_x, along_y, along_z)
    sub_type = lax.dynamic_slice_in_dim(cell_type, rank * sub_rows, sub_rows, 0)
    local_fluid_cells = sub_type == 0
    first_vel = rank * block_vel
    here_x = lax.dynamic_slice_in_dim(along_x, first_vel, block_vel)
    here_y = lax.dynamic_slice_in_dim(along_y, first_vel, block_vel)
    still_here = lax.dynamic_slice_in_dim(still_wall, first_vel, block_vel)
    moving_here = lax.dynamic_slice_in_dim(moving, first_vel, block_vel)
    density = lax.psum(jnp.sum(distribution, axis=2), "vel")
    fluid_cell_mask = cell_type == 0
    thermal = density[:, :, None] * jnp.where(
        cell_type[:, :, None] == 1, still_here[None, None, :], moving_here[None, None, :]
    )
    walled = jnp.where(fluid_cell_mask[:, :, None], distribution, thermal)
    rimmed = padded_2(walled, (("cell", 1),), 1)
    padded = jnp.pad(rimmed, ((1, 1), (0, 0), (0, 0)))
    increment = transport(padded, here_x, here_y)
    moved = jnp.where(fluid_cell_mask[:, :, None], walled + increment, walled)
    velocity_grids = lax.all_to_all(moved, "vel", split_axis=0, concat_axis=2, tiled=True)
    vel_count = velocity_grids.shape[2]
    tables = fourier_tables(NVEL)
    cell_block = velocity_grids.transpose(2, 0, 1).reshape(NVEL, NVEL, NVEL, sub_rows * cell_cols)
    kern_first = first_kernel.reshape(DIRS, NVEL, NVEL, NVEL)
    kern_second = second_kernel.reshape(DIRS, NVEL, NVEL, NVEL)
    kern_loss = loss_kernel.reshape(NVEL, NVEL, NVEL)
    collision_operator = collide(cell_block, kern_first, kern_second, kern_loss, tables)
    collision_operator = collision_operator.reshape(vel_count, sub_rows, cell_cols).transpose(
        1, 2, 0
    )
    completed_state = jnp.where(
        local_fluid_cells[:, :, None],
        velocity_grids + collision_timestep * collision_operator,
        velocity_grids,
    )
    return lax.all_to_all(completed_state, "vel", split_axis=2, concat_axis=0, tiled=True)


def solution(mesh):
    return jax.shard_map(
        on_device,
        mesh=mesh,
        in_specs=(P(None, "cell", "vel"), P(None, "cell"), P(), P(), P()),
        out_specs=P(None, "cell", "vel"),
        check_vma=False,
    )
```

profile of v0, /device:TPU:0, one launch (start us, length us, event | category | flops | bytes accessed | tf_op | source)
XLA Modules:
  0.0 624.3 jit_solution(11724081583912681703)
XLA Ops:
  1.2 1.8 reduce_sum.27
  3.0 17.8 %psum.7 = f32[64,8]{1,0:T(8,128)S(1)} all-reduce(f32[64,8]{1,0:T(8,128)S(1)} %reduce_sum.27), channel_id=1, replica_groups=mesh['cell'=8,'vel'=4] {'vel'}, use_global_device_ids=true, to_apply=%region_1.0 | all-reduce | flops 512 | bytes 4096 | tf_op jit(solution)/shard_map/psum | solution.py:147
  26.9 3.9 collective-permute-done.1
  31.4 1.4 add_select_fusion.2
  32.8 2.5 copy.194
  35.4 4.0 all-to-all-start
  40.9 2.0 reshape.45
  43.0 2.1 reshape.47
  45.0 19.5 %all-to-all-done = f32[64,8,1024]{2,1,0:T(8,128)S(1)} async-done(((f32[64,8,1024]{2,1,0:T(8,128)}), f32[64,8,1024]{2,1,0:T(8,128)S(1)}, u32[]{:S(2)}, u32[]{:S(2)}) %all-to-all-start) | async-done | bytes 2097184 | tf_op jit(solution)/shard_map/all_to_all | solution.py:157
  64.6 2.7 copy.299
  67.3 2.7 all_to_all.29
  70.0 8.9 %reshape.46 = f32[16,16,16,128]{2,1,0,3:T(8,128)} reshape(f32[4096,16,8]{0,2,1:T(8,128)S(1)} %bitcast.206) | data formatting | bytes 4194304 | tf_op jit(solution)/shard_map/reshape | solution.py:160
  78.9 11.1 %copy.196 = bf16[16,16,16,128]{3,0,2,1:T(8,128)(2,1)S(1)} copy(f32[16,16,16,128]{2,1,0,3:T(8,128)} %reshape.46) | data formatting | bytes 3145728 | tf_op jit(solution)/shard_map/reshape | solution.py:160
  90.0 13.7 %copy.219 = f32[16,16,16,128]{3,2,1,0:T(8,128)} copy(f32[16,16,16,128]{2,1,0,3:T(8,128)} %reshape.46) | data formatting | bytes 4194304 | tf_op jit(solution)/shard_map/reshape | solution.py:160
  108.6 1.4 fusion.189
  112.3 1.7 multiply_convert_fusion.2
  114.8 384.8 %while.15 = (s32[]{:T(128)}, f32[16,16,16,128]{3,2,1,0:T(8,128)}, f32[16,16,16,16]{3,2,1,0:T(8,128)}, bf16[16,16,16,128]{3,0,2,1:T(8,128)(2,1)S(1)}, bf16[16,16,...) while((s32[]{:T(128)}, f32[16,16,16,128]{3,2,1,0:T(8,128)}, ...), condition=%wide.region_5.6_spmd.clone.clone, body=%wide.region_4.5_spmd.clone.clone.sunk | while | flops 359219200 | bytes 96731296 | solution.py:114
  373.8 1.4 fusion.464
  397.8 1.4 fusion.464
  445.7 1.4 fusion.464
  459.9 1.4 fusion.471
  469.6 1.4 fusion.464
  510.9 13.4 %copy.220 = f32[16,16,16,128]{2,1,0,3:T(8,128)} copy(f32[16,16,16,128]{3,2,1,0:T(8,128)S(1)} %fusion.187) | data formatting | bytes 4194304 | tf_op jit(solution)/shard_map/mul | solution.py:170
  524.3 15.4 %mul.561 = f32[4096,16,8]{0,2,1:T(8,128)} reshape(f32[16,16,16,128]{2,1,0,3:T(8,128)} %copy.220) | data formatting | bytes 4194304 | tf_op jit(solution)/shard_map/mul | solution.py:170
  539.7 3.2 add_select_fusion.1
  543.0 9.5 %copy.221 = f32[16,8,4096]{0,1,2:T(8,128)} copy(f32[16,8,4096]{2,1,0:T(8,128)} %add_select_fusion.1) | data formatting | bytes 4194304 | tf_op jit(solution)/shard_map/jit(_where)/select_n | solution.py:168
  552.5 9.1 %reshape.54 = f32[4,1,131072]{2,1,0:T(1,128)S(1)} reshape(f32[4096,8,16]{2,1,0:T(8,128)} %bitcast.204) | data formatting | bytes 4194304
  561.6 29.8 %all_to_all.36 = f32[4,1,131072]{2,1,0:T(1,128)} all-to-all(f32[4,1,131072]{2,1,0:T(1,128)S(1)} %reshape.54), channel_id=1, replica_groups=mesh['cell'=8,'vel'=4] {'vel'}, dimensions={0} | all-to-all | bytes 4194304 | tf_op jit(solution)/shard_map/all_to_all | solution.py:173
  591.9 7.7 %reduce.2 = f32[4,131072]{1,0:T(4,128)S(1)} reduce(f32[4,1,131072]{2,1,0:T(1,128)} %all_to_all.36, f32[]{:T(128)} %broadcast.260), dimensions={1}, to_apply=%all_to_all.30.reduce_sub_computation | reduce | bytes 4194308 | tf_op jit(solution)/shard_map/all_to_all | solution.py:173
  599.6 11.5 %reshape.55 = f32[4096,8,16]{2,1,0:T(8,128)} reshape(f32[4,131072]{1,0:T(4,128)S(1)} %reduce.2) | data formatting | bytes 4194304
  611.2 10.4 %copy.230 = f32[16,8,4,1024]{3,2,1,0:T(4,128)S(1)} copy(f32[16,8,4,1024]{0,1,3,2:T(8,128)} %bitcast.205) | data formatting | bytes 4194304 | tf_op jit(solution)/shard_map/all_to_all | solution.py:173
  621.6 2.5 copy.223
  (502 shorter events, 404.1 us)
Async XLA Ops:
  0.0 22.9 %copy-start.6 = (f32[64,8,1024]{2,1,0:T(8,128)S(1)}, f32[64,8,1024]{2,1,0:T(8,128)}, u32[]{:S(2)}) copy-start(f32[64,8,1024]{2,1,0:T(8,128)} %param.7) | copy-start | bytes 6291460
  24.3 2.6 collective-permute-start
  25.6 5.2 collective-permute-start.1
  35.4 4.1 copy-start.12
  35.4 4.8 copy-start.11
  35.4 5.6 copy-start.9
  35.4 29.2 %all-to-all-start = ((f32[64,8,1024]{2,1,0:T(8,128)}), f32[64,8,1024]{2,1,0:T(8,128)S(1)}, u32[]{:S(2)}, u32[]{:S(2)}) async-start(f32[64,8,1024]{2,1,0:T(8,128)} %copy.194), calls=%async_computation | async-start | bytes 4194304 | tf_op jit(solution)/shard_map/all_to_all | solution.py:157
  39.4 3.6 copy-start.10
  70.0 9.0 %copy-start.3 = (f32[16,8,4096]{2,1,0:T(8,128)}, f32[16,8,4096]{2,1,0:T(8,128)S(1)}, u32[]{:S(2)}) copy-start(f32[16,8,4096]{2,1,0:T(8,128)S(1)} %all_to_all.29) | copy-start | bytes 6291460
  135.8 1.6 copy-start
  138.7 1.3 copy-start.1
  159.7 1.6 copy-start
  162.7 1.3 copy-start.1
  183.7 1.6 copy-start
  186.6 1.3 copy-start.1
  207.6 1.6 copy-start
  231.5 1.6 copy-start
  255.5 1.6 copy-start
  279.4 1.6 copy-start
  303.4 1.6 copy-start
  327.3 1.6 copy-start
  351.3 1.6 copy-start
  375.2 1.6 copy-start
  399.2 1.6 copy-start
  423.1 1.6 copy-start
  447.0 1.6 copy-start
  471.0 1.6 copy-start
  494.9 1.6 copy-start
  507.2 1.9 copy-start.7
  508.6 1.6 copy-start.2
  524.3 15.4 %copy-start.4 = (f32[16,8,4096]{2,1,0:T(8,128)S(1)}, f32[16,8,4096]{2,1,0:T(8,128)}, u32[]{:S(2)}) copy-start(f32[16,8,4096]{2,1,0:T(8,128)} %copy-done.3) | copy-start | bytes 6291460
  524.3 15.4 %copy-start.13 = (pred[16,8]{1,0:T(8,128)(4,1)S(1)}, pred[16,8]{1,0:T(8,128)(4,1)}, u32[]{:S(2)}) copy-start(pred[16,8]{1,0:T(8,128)(4,1)} %copy.191) | copy-start | bytes 388
  (15 other events, 19.6 us)
where the time goes:
time: 632 us; the launch traced here: 624 us
  matrix products  342 us (54%)
  local copies, waits for them, and re-layouts  182 us (29%)
  blocking collectives  47.6 us (8%)
  waiting for transfers between devices  23.4 us (4%)
  other arithmetic  18.9 us (3%)
  starting transfers between devices  6.63 us (1%)
    dot_general x340, matrix products, apply_table(): jnp.einsum(pattern, matrix, operand, preferred_element_type=jnp.float32)  342 us
    while x64, local copies, waits for them, and re-layouts  39 us
    reshape x3, local copies, waits for them, and re-layouts, on_device(): velocity_grids.transpose(2, 0, 1)  33.7 us
    all_to_all x1, blocking collectives, on_device(): lax.all_to_all(completed_state, 'vel', split_axis=2, concat_axis=0, tiled...  29.8 us
    mul x2, local copies, waits for them, and re-layouts, on_device(): collision_timestep * collision_operator  28.8 us
    unnamed x32, local copies, waits for them, and re-layouts  23.9 us
    all_to_all x1, waiting for transfers between devices, on_device(): lax.all_to_all(moved, 'vel', split_axis=0, concat_axis=2, tiled=True)  19.5 us
    psum x1, blocking collectives, on_device(): density = lax.psum(jnp.sum(distribution, axis=2), 'vel')  17.8 us
  transfers between devices with their start and end apart: 3, of which 2 were waited for; matrix products, arithmetic and copies ran while one was open for 1% of the time, Pallas kernels for 0%

commit v1 on v0

v1 whole, which is shorter than its diff:
```python
import functools
import math

import jax
import jax.numpy as jnp
import numpy as np
from jax import lax
from jax.experimental import pallas as pl
from jax.experimental.pallas import tpu as pltpu
from jax.sharding import PartitionSpec as P

N = 16
HALF = N // 2
PLANE = N * N
TILE = N * HALF
CELLS = 8
CHUNKS = 4
UNROLL = 16
courant = 0.45
collision_timestep = 0.1
bf16 = jnp.bfloat16
f32 = jnp.float32


def velocity_tables():
    levels = ((2.0 * np.arange(N, dtype=np.float32) - (N - 1)) / (N - 1)).astype(np.float64)
    cx = np.repeat(levels, PLANE)
    cy = np.tile(np.repeat(levels, N), N)
    cz = np.tile(levels, PLANE)
    still = np.exp(-4.5 * (cx * cx + cy * cy + cz * cz))
    moving = np.exp(-0.5 * ((3.0 * cx - 1.0) ** 2 + 9.0 * cy * cy + 9.0 * cz * cz))
    zero = np.zeros_like(cx)
    rows = [np.maximum(cx, 0), np.minimum(cx, 0), np.maximum(cy, 0), np.minimum(cy, 0),
            still / still.sum(), moving / moving.sum(), zero, zero]
    return np.stack(rows).astype(np.float32)


def fourier_matrices():
    n = np.arange(N)
    angles = 2.0 * math.pi * ((n[:, None] * n[None, :]) % N) / N
    rounded = lambda t: t.astype(np.float32).astype(jnp.bfloat16).astype(np.float64)
    c, s = rounded(np.cos(angles)), rounded(np.sin(angles))
    by_cell, by_line = np.eye(CELLS), np.eye(N)
    forward_i = np.concatenate([np.kron(c, by_cell), np.kron(-s, by_cell)], 0)
    cj, sj = np.kron(c, by_line), np.kron(s, by_line)
    forward_j = np.block([[cj, -sj], [sj, cj]])
    ck, sk = np.kron(by_line, c), np.kron(by_line, s)
    whole = np.block([[ck, -sk], [sk, ck]]).reshape(2 * PLANE, 2, N, N)
    low = whole[..., :HALF]
    top = np.zeros_like(low)
    top[..., 0] = whole[..., HALF]
    forward_k = np.concatenate([low.reshape(2 * PLANE, PLANE), top.reshape(2 * PLANE, PLANE)], 1)
    turn = np.stack([np.stack([c, -s], -1), np.stack([s, c], -1)], 0) / N
    inverse_i = np.kron(turn.reshape(2 * N, 2 * N), by_cell)
    c, s = c / N, s / N
    spread = lambda left, right: np.einsum("bj,d->jbd", left, right)
    last = np.zeros((2, N, HALF, N, N))
    for k in range(1, HALF):
        last[0, :, k] = 2.0 * (spread(c, c[:, k]) - spread(s, s[:, k]))
        last[1, :, k] = -2.0 * (spread(c, s[:, k]) + spread(s, c[:, k]))
    last[0, :, 0] = spread(c, c[:, 0]) + spread(s, c[:, HALF])
    last[1, :, 0] = spread(c, c[:, HALF]) - spread(s, c[:, 0])
    inverse_jk = last.reshape(PLANE, PLANE)
    return [t.astype(np.float32).astype(jnp.bfloat16) for t in (forward_i, forward_j, forward_k, inverse_i, inverse_jk)]


def half_selection():
    eye = np.eye(PLANE, dtype=np.float32).reshape(PLANE, N, N)
    low = eye[..., :HALF]
    top = np.zeros_like(low)
    top[..., 0] = eye[..., HALF]
    straight = np.concatenate([low.reshape(PLANE, TILE), top.reshape(PLANE, TILE)], 1)
    flip = (-np.arange(N)) % N
    mirrored = straight.reshape(N, N, PLANE)[flip][:, flip].reshape(PLANE, PLANE)
    return np.concatenate([straight, mirrored], 1).astype(jnp.bfloat16)


def dot(left, right):
    return jnp.dot(left, right, preferred_element_type=f32)


def call(kernel, out_shape, operands, flops=0, scratch=(), **options):
    moved = sum(a.size * a.dtype.itemsize for a in list(operands) + jax.tree.leaves(out_shape))
    return pl.pallas_call(
        kernel, out_shape=out_shape, scratch_shapes=list(scratch),
        compiler_params=pltpu.CompilerParams(vmem_limit_bytes=40 * 2 ** 20),
        cost_estimate=pl.CostEstimate(flops=flops, bytes_accessed=moved, transcendentals=0),
        **options,
    )(*operands)


def kernels_body(first_ref, second_ref, loss_ref, pick_ref, low_ref, top_ref):
    pick = pick_ref[...]
    start = 0
    for source in (first_ref, second_ref, loss_ref):
        count = source.shape[0]
        picked = []
        for i in range(N):
            value = source[:, PLANE * i:PLANE * (i + 1)]
            total = 0.0
            for _ in range(3):
                part = value.astype(bf16)
                value = value - part.astype(f32)
                total = total + dot(part, pick)
            picked.append(total)
        for i in range(N):
            here, there = picked[i], picked[-i % N]
            even = 0.5 * (here[:, :PLANE] + there[:, PLANE:])
            low_ref[i, start:start + count, :] = even[:, :TILE]
            top_ref[i, start:start + count, :] = even[:, TILE:]
        start += count


def half_kernels(first_kernel, second_kernel, loss_kernel):
    total = first_kernel.shape[0] + second_kernel.shape[0] + 1
    shape = jax.ShapeDtypeStruct((N, total, TILE), f32)
    operands = (first_kernel, second_kernel, loss_kernel[None, :], jnp.asarray(half_selection()))
    return call(kernels_body, (shape, shape), operands, flops=6 * total * N * PLANE * 2 * PLANE)


def column_of(table, lane, row):
    return jnp.sum(jnp.where(lane == row, table, 0.0), axis=1, keepdims=True)


def density_body(cells_ref, sum_ref):
    rows, cols, _ = cells_ref.shape
    lane = lax.broadcasted_iota(jnp.int32, (cols, rows), 1)

    def add(row, total):
        return jnp.where(lane == row, jnp.sum(cells_ref[row], axis=1, keepdims=True), total)

    sum_ref[...] = lax.fori_loop(0, rows, add, jnp.zeros((cols, rows), f32), unroll=8)


def walled_row(cells_ref, kind, density, tables_ref, lane, row):
    here = column_of(kind, lane, row)
    wall = jnp.where(here == 1.0, tables_ref[4:5, :], tables_ref[5:6, :]) * column_of(density, lane, row)
    return jnp.where(here == 0.0, cells_ref[row], wall), here


def rim_body(groups, *refs):
    cells_ref, kind_ref, tables_ref = refs[:3]
    sums = refs[3:3 + groups]
    density_ref, first_ref, last_ref = refs[3 + groups:]
    rows, cols, width = cells_ref.shape
    density = sums[0][...]
    for other in sums[1:]:
        density = density + other[...]
    density_ref[...] = density
    kind = kind_ref[...]
    lane = lax.broadcasted_iota(jnp.int32, (cols, rows), 1)

    def one_row(row, _):
        walled, _ = walled_row(cells_ref, kind, density, tables_ref, lane, row)
        for block in range(width // PLANE):
            to = slice(TILE * block, TILE * (block + 1))
            at = PLANE * block
            first_ref[row, :, to] = walled[:1, at:at + TILE]
            last_ref[row, :, to] = walled[cols - 1:, at + TILE:at + PLANE]
        return 0

    lax.fori_loop(0, rows, one_row, 0, unroll=4)


def transport_body(groups, chunks, rank_ref, cells_ref, kind_ref, tables_ref, density_ref, before_ref, after_ref, *outs):
    rows, cols, width = cells_ref.shape
    per_chunk = rows // groups // chunks
    rank = rank_ref[0]
    kind, density = kind_ref[...], density_ref[...]
    lane = lax.broadcasted_iota(jnp.int32, (cols, rows), 1)
    sub = lax.broadcasted_iota(jnp.int32, (cols, TILE), 0)
    row_of = lambda row: walled_row(cells_ref, kind, density, tables_ref, lane, row)
    for chunk in range(chunks):
        for flip in range(groups):
            out_ref = outs[chunk * groups + flip]
            top = lax.bitwise_xor(rank, flip) * (rows // groups) + chunk * per_chunk

            def one_row(step, carry):
                past, here, kind_here = carry
                row = top + step
                ahead, kind_ahead = row_of(jnp.minimum(row + 1, rows - 1))
                back_x = here - past
                front_x = ahead - here
                parts = []
                for tile in range(width // TILE):
                    at = slice(TILE * tile, TILE * (tile + 1))
                    rim = slice(TILE * (tile // 2), TILE * (tile // 2 + 1))
                    now = here[:, at]
                    drift = tables_ref[0:1, at] * back_x[:, at] + tables_ref[1:2, at] * front_x[:, at]
                    if tile % 2:
                        near = jnp.where(sub == 0, before_ref[row, :, rim], pltpu.roll(now, 1, 0))
                        drift = drift + tables_ref[2:3, at] * (now - near)
                    else:
                        near = jnp.where(sub == cols - 1, after_ref[row, :, rim], pltpu.roll(now, cols - 1, 0))
                        drift = drift + tables_ref[3:4, at] * (near - now)
                    out_ref[step, :, at] = jnp.where(kind_here == 0.0, now + -courant * drift, now)
                return here, ahead, kind_ahead

            start = row_of(jnp.maximum(top - 1, 0))[0], *row_of(top)
            lax.fori_loop(0, per_chunk, one_row, start)


def collide_body(groups, dirs, *refs):
    rank_ref = refs[0]
    sources = refs[1:1 + groups]
    kind_ref, low_ref, top_ref, fi_ref, fj_ref, fk_ref, ii_ref, ijk_ref = refs[1 + groups:9 + groups]
    outs = refs[9 + groups:9 + 2 * groups]
    moved_ref, spec_ref, gain_ref = refs[9 + 2 * groups:]
    rows = N * CELLS
    per = N // groups
    rank = rank_ref[0]
    for flip, source in enumerate(sources):
        at = lax.bitwise_xor(rank, flip) * per
        for i in range(per):
            moved_ref[at + i] = source[0, :, PLANE * i:PLANE * (i + 1)]
    moved = moved_ref[...].reshape(rows, PLANE)
    value = dot(fi_ref[...], moved.astype(bf16)).astype(bf16)
    value = jnp.concatenate([value[:rows], value[rows:]], 1)
    value = dot(value, fj_ref[...]).astype(bf16)
    spec_ref[...] = dot(value, fk_ref[...]).astype(bf16).astype(f32)

    def weighted(p):
        parts = []
        for i in range(N):
            at = slice(CELLS * i, CELLS * (i + 1))
            low_re, low_im, top_re, top_im = (spec_ref[at, TILE * t:TILE * (t + 1)] for t in range(4))
            low, top = low_ref[i, p:p + 1, :], top_ref[i, p:p + 1, :]
            parts.append(low * low_re - top * top_im)
            parts.append(low * low_im + top * top_re)
        return jnp.concatenate(parts, 0).astype(bf16)

    def back(one, other):
        value = dot(ii_ref[...], jnp.concatenate([weighted(one), weighted(other)], 1)).astype(bf16)
        value = jnp.concatenate([
            jnp.concatenate([value[:rows, :TILE], value[rows:, :TILE]], 1),
            jnp.concatenate([value[:rows, TILE:], value[rows:, TILE:]], 1)], 0)
        value = dot(value, ijk_ref[...])
        return value[:rows], value[rows:]

    loss, other = back(2 * dirs, 0)
    gain_ref[...] = -moved * loss
    for p in range(dirs):
        one, other = back(p, dirs + p)
        gain_ref[...] += one * other
    fluid = kind_ref[0] == 0.0
    now = moved_ref[...]
    updated = jnp.where(fluid, now + collision_timestep * gain_ref[...].reshape(N, CELLS, PLANE), now)
    moved_ref[...] = updated
    for flip, out_ref in enumerate(outs):
        at = lax.bitwise_xor(rank, flip) * per
        for i in range(per):
            out_ref[0, :, PLANE * i:PLANE * (i + 1)] = moved_ref[at + i]


def collide(rank, blocks, kinds, low, top):
    groups = len(blocks)
    dirs = low.shape[1] // 2
    steps, cols, width = blocks[0].shape
    tables = [jnp.asarray(m) for m in fourier_matrices()]
    block = pl.BlockSpec((1, cols, width), lambda g: (g, 0, 0))
    whole = lambda a: pl.BlockSpec(a.shape, lambda g: (0,) * a.ndim)
    shape = jax.ShapeDtypeStruct(blocks[0].shape, f32)
    return call(
        functools.partial(collide_body, groups, dirs), (shape,) * groups,
        (rank, *blocks, kinds, low, top, *tables),
        flops=steps * 2 * PLANE ** 3 * (2 * dirs + 6),
        scratch=[pltpu.VMEM((N, CELLS, PLANE), f32), pltpu.VMEM((N * CELLS, 2 * PLANE), f32), pltpu.VMEM((N * CELLS, PLANE), f32)],
        grid=(steps,),
        in_specs=[pl.BlockSpec(memory_space=pltpu.SMEM)] + [block] * groups
        + [pl.BlockSpec((1, cols, 1), lambda g: (g, 0, 0))] + [whole(a) for a in (low, top, *tables)],
        out_specs=(block,) * groups,
    )


def on_device(distribution, cell_type, first_kernel, second_kernel, loss_kernel):
    rows, cols, width = distribution.shape
    groups = lax.axis_size("vel")
    rank = lax.axis_index("vel")
    spots = lax.axis_size("cell")
    own_rows = rows // groups
    per_chunk = own_rows // CHUNKS
    rank_word = rank.astype(jnp.int32)[None]
    tables = lax.dynamic_slice_in_dim(jnp.asarray(velocity_tables()), rank * width, width, 1)
    kind = cell_type.astype(f32)
    kind_by_col = kind.T
    own_kind = lax.dynamic_slice_in_dim(kind, rank * own_rows, own_rows, 0)[:, :, None]

    def swap(value, flip):
        return lax.ppermute(value, "vel", [(i, i ^ flip) for i in range(groups)])

    partial = call(density_body, jax.ShapeDtypeStruct((cols, rows), f32), (distribution,))
    sums = [partial] + [swap(partial, flip) for flip in range(1, groups)]
    low, top = half_kernels(first_kernel, second_kernel, loss_kernel)
    rim = jax.ShapeDtypeStruct((rows, 1, width // 2), f32)
    density, first, last = call(
        functools.partial(rim_body, groups), (jax.ShapeDtypeStruct((cols, rows), f32), rim, rim),
        (distribution, kind_by_col, tables, *sums))
    before = lax.ppermute(last, "cell", [(i, i + 1) for i in range(spots - 1)])
    after = lax.ppermute(first, "cell", [(i + 1, i) for i in range(spots - 1)])
    vmem = pl.BlockSpec(memory_space=pltpu.VMEM)
    piece = jax.ShapeDtypeStruct((per_chunk, cols, width), f32)
    pieces = call(
        functools.partial(transport_body, groups, CHUNKS), (piece,) * (CHUNKS * groups),
        (rank_word, distribution, kind_by_col, tables, density, before, after),
        in_specs=[pl.BlockSpec(memory_space=pltpu.SMEM)] + [vmem] * 6, out_specs=(vmem,) * (CHUNKS * groups))
    updated = jnp.zeros((rows, cols, width), f32)
    arrived = []
    for chunk in range(CHUNKS):
        mine = pieces[chunk * groups:(chunk + 1) * groups]
        arrived.append([mine[0]] + [swap(mine[flip], flip) for flip in range(1, groups)])
    for chunk in range(CHUNKS):
        done = collide(rank_word, arrived[chunk], own_kind[chunk * per_chunk:(chunk + 1) * per_chunk], low, top)
        for flip in range(groups):
            home = done[0] if flip == 0 else swap(done[flip], flip)
            updated = lax.dynamic_update_slice_in_dim(updated, home, (rank ^ flip) * own_rows + chunk * per_chunk, 0)
    return updated


def solution(mesh):
    return jax.shard_map(
        on_device,
        mesh=mesh,
        in_specs=(P(None, "cell", "vel"), P(None, "cell"), P(), P(), P()),
        out_specs=P(None, "cell", "vel"),
        check_vma=False,
    )
```

time: 632 us -> 116 us (0.18); the launches traced: 624 us -> 116 us
  matrix products: 342 us -> 0 us
  local copies, waits for them, and re-layouts: 182 us -> 15.8 us
  Pallas kernels: 0 us -> 50.5 us
  blocking collectives: 47.6 us -> 0 us
  starting transfers between devices: 6.63 us -> 35.6 us
  other arithmetic: 18.9 us -> 0.01 us
  waiting for transfers between devices: 23.4 us -> 13.8 us
    dot_general x340 -> x0, matrix products: 342 us -> none  [apply_table(): jnp.einsum(pattern, matrix, operand, preferred_element_type=jnp.float32)]
    pallas_call x0 -> x8, Pallas kernels: none -> 50.5 us  [call(): pl.pallas_call(kernel, out_shape=out_shape, scratch_shapes=list(scratch),...]
    while x64 -> x0, local copies, waits for them, and re-layouts: 39 us -> none
    reshape x5 -> x0, local copies, waits for them, and re-layouts: 37.8 us -> none  [the longest x3 33.7 us: on_device(): velocity_grids.transpose(2, 0, 1)]
    ppermute x2 -> x29, starting transfers between devices: 2.6 us -> 35.6 us  [the longest x27 33 us: swap(): return lax.ppermute(value, 'vel', [(i, i ^ flip) for i in range(groups)])]
    all_to_all x1 -> x0, blocking collectives: 29.8 us -> none  [on_device(): lax.all_to_all(completed_state, 'vel', split_axis=2, concat_axis=0, tiled...]
    mul x3 -> x0, local copies, waits for them, and re-layouts: 29.6 us -> none  [the longest x2 28.8 us: on_device(): collision_timestep * collision_operator]
    all_to_all x1 -> x0, waiting for transfers between devices: 19.5 us -> none  [on_device(): lax.all_to_all(moved, 'vel', split_axis=0, concat_axis=2, tiled=True)]
  transfers between devices with their start and end apart: 3 -> 29, of which waited for: 2 -> 10; matrix products, arithmetic and copies ran while one was open for 1% -> 2% of each run, Pallas kernels for 0% -> 34%
where the time goes in v1:
time: 116 us
  Pallas kernels  50.5 us (44%)
  starting transfers between devices  35.6 us (31%)
  local copies, waits for them, and re-layouts  15.8 us (14%)
  waiting for transfers between devices  13.8 us (12%)
    pallas_call x8, Pallas kernels, call(): pl.pallas_call(kernel, out_shape=out_shape, scratch_shapes=list(scratch),...  50.5 us
    ppermute x27, starting transfers between devices, swap(): return lax.ppermute(value, 'vel', [(i, i ^ flip) for i in range(groups)])  33 us
    unnamed x58, local copies, waits for them, and re-layouts  13.3 us
    ppermute x27, waiting for transfers between devices, swap(): return lax.ppermute(value, 'vel', [(i, i ^ flip) for i in range(groups)])  10.1 us
    ppermute x1, waiting for transfers between devices, on_device(): after = lax.ppermute(first, 'cell', [(i + 1, i) for i in range(spots - 1)])  3.67 us
  transfers between devices with their start and end apart: 29, of which 10 were waited for; matrix products, arithmetic and copies ran while one was open for 2% of the time, Pallas kernels for 34%

profile of v1, /device:TPU:0, one launch (start us, length us, event | category | flops | bytes accessed | tf_op | source)
XLA Modules:
  0.0 116.1 jit_solution(7566252209304251466)
XLA Ops:
  0.0 1.6 %copy-done = f32[64,8,1024]{2,1,0:T(8,128)S(1)} copy-done((f32[64,8,1024]{2,1,0:T(8,128)S(1)}, f32[64,8,1024]{2,1,0:T(8,128)}, u32[]{:S(2)}) %copy-start) | copy-done | bytes 2097176
  2.3 3.9 %collective-permute-start.2 = (f32[8,64]{1,0:T(8,128)S(1)}, f32[8,64]{1,0:T(8,128)S(1)}, u32[]{:S(2)}, u32[]{:S(2)}) collective-permute-start(f32[8,64]{1,0:T(8,128)S(1)} %shard_map.253.refs_3_), channel_id=1, source_target_pairs={{0,3},{1,2},{2,1},{3,0},{4,7},{5,6},{6,5},{7,4},{8,11},{9,10},{10,... | collective-permute-start | bytes 6152 | tf_op jit(solution)/shard_map/ppermute | solution.py:289
  7.8 2.0 %collective-permute-done.1.refs_5_ = f32[8,64]{1,0:T(8,128)S(1)} collective-permute-done((f32[8,64]{1,0:T(8,128)S(1)}, f32[8,64]{1,0:T(8,128)S(1)}, u32[]{:S(2)}, u32[]{:S(2)}) %collective-permute-start.1) | collective-permute-done | bytes 2080 | tf_op jit(solution)/shard_map/ppermute | solution.py:289
  10.4 1.7 %shard_map.254 = (f32[8,64]{1,0:T(8,128)S(1)}, f32[64,1,512]{2,1,0:T(1,128)S(1)}, f32[64,1,512]{2,1,0:T(1,128)S(1)}) custom-call(f32[64,8,1024]{2,1,0:T(8,128)S(1)} %copy-done.1, f32[8,64]{1,0:T(8,128)S(1)} %get-tuple-element.84.refs_1_.kind_ref, f32[8,1024]{1,0:T(8,128)S(1)} %constant_dynamic-slice_fusion.1.refs_2_.tables_ref, ...), custom_call_target="tpu_custom_call" | custom-call | bytes 2404352 | tf_op jit(solution)/shard_map/pallas_call | solution.py:84
  12.1 1.3 %collective-permute-start.3 = (f32[64,1,512]{2,1,0:T(1,128)S(1)}, f32[64,1,512]{2,1,0:T(1,128)S(1)}, u32[]{:S(2)}, u32[]{:S(2)}) collective-permute-start(f32[64,1,512]{2,1,0:T(1,128)S(1)} %get-tuple-element.43), channel_id=1, source_target_pairs={{0,4},{4,8},{8,12},{12,16},{16,20},{20,24},{24,28},{1,5},{5,9},{9,... | collective-permute-start | bytes 393224 | tf_op jit(solution)/shard_map/ppermute | solution.py:298
  13.4 1.3 %collective-permute-start.4 = (f32[64,1,512]{2,1,0:T(1,128)S(1)}, f32[64,1,512]{2,1,0:T(1,128)S(1)}, u32[]{:S(2)}, u32[]{:S(2)}) collective-permute-start(f32[64,1,512]{2,1,0:T(1,128)S(1)} %get-tuple-element.44), channel_id=1, source_target_pairs={{4,0},{8,4},{12,8},{16,12},{20,16},{24,20},{28,24},{5,1},{9,5},{13... | collective-permute-start | bytes 393224 | tf_op jit(solution)/shard_map/ppermute | solution.py:299
  14.8 3.7 %collective-permute-done.4.after_ref = f32[64,1,512]{2,1,0:T(1,128)S(1)} collective-permute-done((f32[64,1,512]{2,1,0:T(1,128)S(1)}, f32[64,1,512]{2,1,0:T(1,128)S(1)}, u32[]{:S(2)}, u32[]{:S(2)}) %collective-permute-start.4) | collective-permute-done | bytes 131104 | tf_op jit(solution)/shard_map/ppermute | solution.py:299
  18.4 8.1 %shard_map.255 = (f32[4,8,1024]{2,1,0:T(8,128)S(1)}, f32[4,8,1024]{2,1,0:T(8,128)}, f32[4,8,1024]{2,1,0:T(8,128)}, f32[4,8,1024]{2,1,0:T(8,128)}, f32[4,8,1024]{...) custom-call(s32[1]{0:T(128)} %bitcast.rank_ref.refs_0_, ...), custom_call_target="tpu_custom_call" | custom-call | bytes 4493316 | tf_op jit(solution)/shard_map/pallas_call | solution.py:84
  32.9 1.5 %collective-permute-start.6 = (f32[4,8,1024]{2,1,0:T(8,128)}, f32[4,8,1024]{2,1,0:T(8,128)S(1)}, u32[]{:S(2)}, u32[]{:S(2)}) collective-permute-start(f32[4,8,1024]{2,1,0:T(8,128)} %get-tuple-element.47), channel_id=1, source_target_pairs={{0,2},{1,3},{2,0},{3,1},{4,6},{5,7},{6,4},{7,5},{8,10},{9,11},{10,... | collective-permute-start | bytes 393224 | tf_op jit(solution)/shard_map/ppermute | solution.py:289
  34.4 1.4 %collective-permute-start.7 = (f32[4,8,1024]{2,1,0:T(8,128)}, f32[4,8,1024]{2,1,0:T(8,128)S(1)}, u32[]{:S(2)}, u32[]{:S(2)}) collective-permute-start(f32[4,8,1024]{2,1,0:T(8,128)} %get-tuple-element.48), channel_id=1, source_target_pairs={{0,3},{1,2},{2,1},{3,0},{4,7},{5,6},{6,5},{7,4},{8,11},{9,10},{10,... | collective-permute-start | bytes 393224 | tf_op jit(solution)/shard_map/ppermute | solution.py:289
  37.5 5.0 %shard_map.256 = (f32[16,33,128]{2,1,0:T(8,128)S(1)}, f32[16,33,128]{2,1,0:T(8,128)S(1)}) custom-call(f32[16,4096]{1,0:T(8,128)S(1)} %copy-done.2, f32[16,4096]{1,0:T(8,128)S(1)} %copy-done.3, f32[1,4096]{1,0:T(1,128)S(1)} %bitcast.12, bf16[256,512]{1,0:T(8,128)(2,1)S(1)} %copy-done.21), custom_call_target="tpu_custom_call" | custom-call | flops 415236096 | bytes 1343488 | tf_op jit(solution)/shard_map/pallas_call | solution.py:84
  43.0 1.5 %collective-permute-start.12 = (f32[4,8,1024]{2,1,0:T(8,128)}, f32[4,8,1024]{2,1,0:T(8,128)S(1)}, u32[]{:S(2)}, u32[]{:S(2)}) collective-permute-start(f32[4,8,1024]{2,1,0:T(8,128)} %copy-done.13), channel_id=1, source_target_pairs={{0,2},{1,3},{2,0},{3,1},{4,6},{5,7},{6,4},{7,5},{8,10},{9,11},{10,... | collective-permute-start | bytes 393224 | tf_op jit(solution)/shard_map/ppermute | solution.py:289
  44.6 1.4 %collective-permute-start.13 = (f32[4,8,1024]{2,1,0:T(8,128)}, f32[4,8,1024]{2,1,0:T(8,128)S(1)}, u32[]{:S(2)}, u32[]{:S(2)}) collective-permute-start(f32[4,8,1024]{2,1,0:T(8,128)} %copy-done.12), channel_id=1, source_target_pairs={{0,3},{1,2},{2,1},{3,0},{4,7},{5,6},{6,5},{7,4},{8,11},{9,10},{10,... | collective-permute-start | bytes 393224 | tf_op jit(solution)/shard_map/ppermute | solution.py:289
  46.5 1.5 %collective-permute-start.18 = (f32[4,8,1024]{2,1,0:T(8,128)}, f32[4,8,1024]{2,1,0:T(8,128)S(1)}, u32[]{:S(2)}, u32[]{:S(2)}) collective-permute-start(f32[4,8,1024]{2,1,0:T(8,128)} %copy-done.8), channel_id=1, source_target_pairs={{0,2},{1,3},{2,0},{3,1},{4,6},{5,7},{6,4},{7,5},{8,10},{9,11},{10,... | collective-permute-start | bytes 393224 | tf_op jit(solution)/shard_map/ppermute | solution.py:289
  52.9 8.7 %shard_map.257 = (f32[4,8,1024]{2,1,0:T(8,128)S(1)}, f32[4,8,1024]{2,1,0:T(8,128)S(1)}, f32[4,8,1024]{2,1,0:T(8,128)S(1)}, f32[4,8,1024]{2,1,0:T(8,128)S(1)}) custom-call(s32[1]{0:T(128)} %bitcast.rank_ref.refs_0_, f32[4,8,1024]{2,1,0:T(8,128)S(1)} %copy-done.16, f32[4,8,1024]{2,1,0:T(8,128)S(1)} %collective-permute-done.5.refs_2_, ...), custom_call_target="tpu_custom_call" | custom-call | flops 5100273664 | bytes 2965636 | tf_op jit(solution)/shard_map/pallas_call | solution.py:84
  61.6 1.5 %collective-permute-start.19 = (f32[4,8,1024]{2,1,0:T(8,128)S(1)}, f32[4,8,1024]{2,1,0:T(8,128)S(1)}, u32[]{:S(2)}, u32[]{:S(2)}) collective-permute-start(f32[4,8,1024]{2,1,0:T(8,128)S(1)} %copy-done.7), channel_id=1, source_target_pairs={{0,3},{1,2},{2,1},{3,0},{4,7},{5,6},{6,5},{7,4},{8,11},{9,10},{10,... | collective-permute-start | bytes 393224 | tf_op jit(solution)/shard_map/ppermute | solution.py:289
  63.6 1.5 %collective-permute-start.24 = (f32[4,8,1024]{2,1,0:T(8,128)S(1)}, f32[4,8,1024]{2,1,0:T(8,128)S(1)}, u32[]{:S(2)}, u32[]{:S(2)}) collective-permute-start(f32[4,8,1024]{2,1,0:T(8,128)S(1)} %get-tuple-element.73), channel_id=1, source_target_pairs={{0,2},{1,3},{2,0},{3,1},{4,6},{5,7},{6,4},{7,5},{8,10},{9,11},{10,... | collective-permute-start | bytes 393224 | tf_op jit(solution)/shard_map/ppermute | solution.py:289
  65.2 8.8 %shard_map.258 = (f32[4,8,1024]{2,1,0:T(8,128)S(1)}, f32[4,8,1024]{2,1,0:T(8,128)S(1)}, f32[4,8,1024]{2,1,0:T(8,128)S(1)}, f32[4,8,1024]{2,1,0:T(8,128)S(1)}) custom-call(s32[1]{0:T(128)} %bitcast.rank_ref.refs_0_, f32[4,8,1024]{2,1,0:T(8,128)S(1)} %copy-done.11, f32[4,8,1024]{2,1,0:T(8,128)S(1)} %collective-permute-done.11.refs_2_, ...), custom_call_target="tpu_custom_call" | custom-call | flops 5100273664 | bytes 2965636 | tf_op jit(solution)/shard_map/pallas_call | solution.py:84
  74.0 1.5 %collective-permute-start.25 = (f32[4,8,1024]{2,1,0:T(8,128)S(1)}, f32[4,8,1024]{2,1,0:T(8,128)S(1)}, u32[]{:S(2)}, u32[]{:S(2)}) collective-permute-start(f32[4,8,1024]{2,1,0:T(8,128)S(1)} %get-tuple-element.74), channel_id=1, source_target_pairs={{0,3},{1,2},{2,1},{3,0},{4,7},{5,6},{6,5},{7,4},{8,11},{9,10},{10,... | collective-permute-start | bytes 393224 | tf_op jit(solution)/shard_map/ppermute | solution.py:289
  76.1 1.5 %collective-permute-start.9 = (f32[4,8,1024]{2,1,0:T(8,128)S(1)}, f32[4,8,1024]{2,1,0:T(8,128)S(1)}, u32[]{:S(2)}, u32[]{:S(2)}) collective-permute-start(f32[4,8,1024]{2,1,0:T(8,128)S(1)} %get-tuple-element.53), channel_id=1, source_target_pairs={{0,2},{1,3},{2,0},{3,1},{4,6},{5,7},{6,4},{7,5},{8,10},{9,11},{10,... | collective-permute-start | bytes 393224 | tf_op jit(solution)/shard_map/ppermute | solution.py:289
  77.5 8.8 %shard_map.259 = (f32[4,8,1024]{2,1,0:T(8,128)S(1)}, f32[4,8,1024]{2,1,0:T(8,128)S(1)}, f32[4,8,1024]{2,1,0:T(8,128)S(1)}, f32[4,8,1024]{2,1,0:T(8,128)S(1)}) custom-call(s32[1]{0:T(128)} %bitcast.rank_ref.refs_0_, f32[4,8,1024]{2,1,0:T(8,128)S(1)} %copy-done.5, f32[4,8,1024]{2,1,0:T(8,128)S(1)} %collective-permute-done.17.refs_2_, ...), custom_call_target="tpu_custom_call" | custom-call | flops 5100273664 | bytes 2965636 | tf_op jit(solution)/shard_map/pallas_call | solution.py:84
  86.3 1.6 %collective-permute-start.10 = (f32[4,8,1024]{2,1,0:T(8,128)S(1)}, f32[4,8,1024]{2,1,0:T(8,128)S(1)}, u32[]{:S(2)}, u32[]{:S(2)}) collective-permute-start(f32[4,8,1024]{2,1,0:T(8,128)S(1)} %get-tuple-element.54), channel_id=1, source_target_pairs={{0,3},{1,2},{2,1},{3,0},{4,7},{5,6},{6,5},{7,4},{8,11},{9,10},{10,... | collective-permute-start | bytes 393224 | tf_op jit(solution)/shard_map/ppermute | solution.py:289
  88.4 1.5 %collective-permute-start.15 = (f32[4,8,1024]{2,1,0:T(8,128)S(1)}, f32[4,8,1024]{2,1,0:T(8,128)S(1)}, u32[]{:S(2)}, u32[]{:S(2)}) collective-permute-start(f32[4,8,1024]{2,1,0:T(8,128)S(1)} %get-tuple-element.61), channel_id=1, source_target_pairs={{0,2},{1,3},{2,0},{3,1},{4,6},{5,7},{6,4},{7,5},{8,10},{9,11},{10,... | collective-permute-start | bytes 393224 | tf_op jit(solution)/shard_map/ppermute | solution.py:289
  89.9 8.8 %shard_map.260 = (f32[4,8,1024]{2,1,0:T(8,128)S(1)}, f32[4,8,1024]{2,1,0:T(8,128)S(1)}, f32[4,8,1024]{2,1,0:T(8,128)S(1)}, f32[4,8,1024]{2,1,0:T(8,128)S(1)}) custom-call(s32[1]{0:T(128)} %bitcast.rank_ref.refs_0_, f32[4,8,1024]{2,1,0:T(8,128)S(1)} %get-tuple-element.71.refs_1_, f32[4,8,1024]{2,1,0:T(8,128)S(1)} %collective-permute-done.23.refs_2_, ...), custom_call_target="tpu_custom_call" | custom-call | flops 5100273664 | bytes 2965636 | tf_op jit(solution)/shard_map/pallas_call | solution.py:84
  99.0 1.6 %collective-permute-start.16 = (f32[4,8,1024]{2,1,0:T(8,128)S(1)}, f32[4,8,1024]{2,1,0:T(8,128)S(1)}, u32[]{:S(2)}, u32[]{:S(2)}) collective-permute-start(f32[4,8,1024]{2,1,0:T(8,128)S(1)} %get-tuple-element.62), channel_id=1, source_target_pairs={{0,3},{1,2},{2,1},{3,0},{4,7},{5,6},{6,5},{7,4},{8,11},{9,10},{10,... | collective-permute-start | bytes 393224 | tf_op jit(solution)/shard_map/ppermute | solution.py:289
  101.2 1.5 %collective-permute-start.21 = (f32[4,8,1024]{2,1,0:T(8,128)S(1)}, f32[4,8,1024]{2,1,0:T(8,128)S(1)}, u32[]{:S(2)}, u32[]{:S(2)}) collective-permute-start(f32[4,8,1024]{2,1,0:T(8,128)S(1)} %get-tuple-element.69), channel_id=1, source_target_pairs={{0,2},{1,3},{2,0},{3,1},{4,6},{5,7},{6,4},{7,5},{8,10},{9,11},{10,... | collective-permute-start | bytes 393224 | tf_op jit(solution)/shard_map/ppermute | solution.py:289
  102.7 1.6 %collective-permute-start.22 = (f32[4,8,1024]{2,1,0:T(8,128)S(1)}, f32[4,8,1024]{2,1,0:T(8,128)S(1)}, u32[]{:S(2)}, u32[]{:S(2)}) collective-permute-start(f32[4,8,1024]{2,1,0:T(8,128)S(1)} %get-tuple-element.70), channel_id=1, source_target_pairs={{0,3},{1,2},{2,1},{3,0},{4,7},{5,6},{6,5},{7,4},{8,11},{9,10},{10,... | collective-permute-start | bytes 393224 | tf_op jit(solution)/shard_map/ppermute | solution.py:289
  104.9 1.5 %collective-permute-done.16 = f32[4,8,1024]{2,1,0:T(8,128)S(1)} collective-permute-done((f32[4,8,1024]{2,1,0:T(8,128)S(1)}, f32[4,8,1024]{2,1,0:T(8,128)S(1)}, u32[]{:S(2)}, u32[]{:S(2)}) %collective-permute-start.16) | collective-permute-done | bytes 131104 | tf_op jit(solution)/shard_map/ppermute | solution.py:289
  107.1 1.2 %collective-permute-done.20 = f32[4,8,1024]{2,1,0:T(8,128)S(1)} collective-permute-done((f32[4,8,1024]{2,1,0:T(8,128)S(1)}, f32[4,8,1024]{2,1,0:T(8,128)S(1)}, u32[]{:S(2)}, u32[]{:S(2)}) %collective-permute-start.20) | collective-permute-done | bytes 131104 | tf_op jit(solution)/shard_map/ppermute | solution.py:289
  108.3 2.4 %collective-permute-start.28 = (f32[4,8,1024]{2,1,0:T(8,128)S(1)}, f32[4,8,1024]{2,1,0:T(8,128)S(1)}, u32[]{:S(2)}, u32[]{:S(2)}) collective-permute-start(f32[4,8,1024]{2,1,0:T(8,128)S(1)} %get-tuple-element.78), channel_id=1, source_target_pairs={{0,3},{1,2},{2,1},{3,0},{4,7},{5,6},{6,5},{7,4},{8,11},{9,10},{10,... | collective-permute-start | bytes 393224 | tf_op jit(solution)/shard_map/ppermute | solution.py:289
  110.7 1.3 %collective-permute-done.22 = f32[4,8,1024]{2,1,0:T(8,128)S(1)} collective-permute-done((f32[4,8,1024]{2,1,0:T(8,128)S(1)}, f32[4,8,1024]{2,1,0:T(8,128)S(1)}, u32[]{:S(2)}, u32[]{:S(2)}) %collective-permute-start.22) | collective-permute-done | bytes 131104 | tf_op jit(solution)/shard_map/ppermute | solution.py:289
  114.0 1.4 %collective-permute-done.28 = f32[4,8,1024]{2,1,0:T(8,128)S(1)} collective-permute-done((f32[4,8,1024]{2,1,0:T(8,128)S(1)}, f32[4,8,1024]{2,1,0:T(8,128)S(1)}, u32[]{:S(2)}, u32[]{:S(2)}) %collective-permute-start.28) | collective-permute-done | bytes 131104 | tf_op jit(solution)/shard_map/ppermute | solution.py:289
  (117 shorter events, 23.1 us)
Async XLA Ops:
  2.3 5.5 %collective-permute-start.2 = (f32[8,64]{1,0:T(8,128)S(1)}, f32[8,64]{1,0:T(8,128)S(1)}, u32[]{:S(2)}, u32[]{:S(2)}) collective-permute-start(f32[8,64]{1,0:T(8,128)S(1)} %shard_map.253.refs_3_), channel_id=1, source_target_pairs={{0,3},{1,2},{2,1},{3,0},{4,7},{5,6},{6,5},{7,4},{8,11},{9,10},{10,... | collective-permute-start | bytes 6152 | tf_op jit(solution)/shard_map/ppermute | solution.py:289
  6.2 3.6 %collective-permute-start.1 = (f32[8,64]{1,0:T(8,128)S(1)}, f32[8,64]{1,0:T(8,128)S(1)}, u32[]{:S(2)}, u32[]{:S(2)}) collective-permute-start(f32[8,64]{1,0:T(8,128)S(1)} %shard_map.253.refs_3_), channel_id=1, source_target_pairs={{0,2},{1,3},{2,0},{3,1},{4,6},{5,7},{6,4},{7,5},{8,10},{9,11},{10,... | collective-permute-start | bytes 6152 | tf_op jit(solution)/shard_map/ppermute | solution.py:289
  6.8 3.6 %collective-permute-start = (f32[8,64]{1,0:T(8,128)S(1)}, f32[8,64]{1,0:T(8,128)S(1)}, u32[]{:S(2)}, u32[]{:S(2)}) collective-permute-start(f32[8,64]{1,0:T(8,128)S(1)} %shard_map.253.refs_3_), channel_id=1, source_target_pairs={{0,1},{1,0},{2,3},{3,2},{4,5},{5,4},{6,7},{7,6},{8,9},{9,8},{10,11... | collective-permute-start | bytes 6152 | tf_op jit(solution)/shard_map/ppermute | solution.py:289
  10.4 26.2 %copy-start.3 = (f32[16,4096]{1,0:T(8,128)S(1)}, f32[16,4096]{1,0:T(8,128)}, u32[]{:S(2)}) copy-start(f32[16,4096]{1,0:T(8,128)} %second_ref.1) | copy-start | bytes 786436
  10.4 26.2 %copy-start.17 = (f32[4096]{0:T(1024)S(1)}, f32[4096]{0:T(1024)}, u32[]{:S(2)}) copy-start(f32[4096]{0:T(1024)} %param.31) | copy-start | bytes 49156
  12.1 2.7 %collective-permute-start.3 = (f32[64,1,512]{2,1,0:T(1,128)S(1)}, f32[64,1,512]{2,1,0:T(1,128)S(1)}, u32[]{:S(2)}, u32[]{:S(2)}) collective-permute-start(f32[64,1,512]{2,1,0:T(1,128)S(1)} %get-tuple-element.43), channel_id=1, source_target_pairs={{0,4},{4,8},{8,12},{12,16},{16,20},{20,24},{24,28},{1,5},{5,9},{9,... | collective-permute-start | bytes 393224 | tf_op jit(solution)/shard_map/ppermute | solution.py:298
  13.4 5.0 %collective-permute-start.4 = (f32[64,1,512]{2,1,0:T(1,128)S(1)}, f32[64,1,512]{2,1,0:T(1,128)S(1)}, u32[]{:S(2)}, u32[]{:S(2)}) collective-permute-start(f32[64,1,512]{2,1,0:T(1,128)S(1)} %get-tuple-element.44), channel_id=1, source_target_pairs={{4,0},{8,4},{12,8},{16,12},{20,16},{24,20},{28,24},{5,1},{9,5},{13... | collective-permute-start | bytes 393224 | tf_op jit(solution)/shard_map/ppermute | solution.py:299
  18.4 29.6 %copy-start.26 = (bf16[256,128]{1,0:T(8,128)(2,1)S(1)}, bf16[256,128]{1,0:T(8,128)(2,1)}, u32[]{:S(2)}) copy-start(bf16[256,128]{1,0:T(8,128)(2,1)} %constant.59.clone.refs_8_) | copy-start | bytes 196612
  32.4 12.2 %collective-permute-start.5 = (f32[4,8,1024]{2,1,0:T(8,128)}, f32[4,8,1024]{2,1,0:T(8,128)S(1)}, u32[]{:S(2)}, u32[]{:S(2)}) collective-permute-start(f32[4,8,1024]{2,1,0:T(8,128)} %get-tuple-element.46), channel_id=1, source_target_pairs={{0,1},{1,0},{2,3},{3,2},{4,5},{5,4},{6,7},{7,6},{8,9},{9,8},{10,11... | collective-permute-start | bytes 393224 | tf_op jit(solution)/shard_map/ppermute | solution.py:289
  32.9 13.1 %collective-permute-start.6 = (f32[4,8,1024]{2,1,0:T(8,128)}, f32[4,8,1024]{2,1,0:T(8,128)S(1)}, u32[]{:S(2)}, u32[]{:S(2)}) collective-permute-start(f32[4,8,1024]{2,1,0:T(8,128)} %get-tuple-element.47), channel_id=1, source_target_pairs={{0,2},{1,3},{2,0},{3,1},{4,6},{5,7},{6,4},{7,5},{8,10},{9,11},{10,... | collective-permute-start | bytes 393224 | tf_op jit(solution)/shard_map/ppermute | solution.py:289
  34.4 12.1 %collective-permute-start.7 = (f32[4,8,1024]{2,1,0:T(8,128)}, f32[4,8,1024]{2,1,0:T(8,128)S(1)}, u32[]{:S(2)}, u32[]{:S(2)}) collective-permute-start(f32[4,8,1024]{2,1,0:T(8,128)} %get-tuple-element.48), channel_id=1, source_target_pairs={{0,3},{1,2},{2,1},{3,0},{4,7},{5,6},{6,5},{7,4},{8,11},{9,10},{10,... | collective-permute-start | bytes 393224 | tf_op jit(solution)/shard_map/ppermute | solution.py:289
  42.5 19.1 %collective-permute-start.11 = (f32[4,8,1024]{2,1,0:T(8,128)}, f32[4,8,1024]{2,1,0:T(8,128)S(1)}, u32[]{:S(2)}, u32[]{:S(2)}) collective-permute-start(f32[4,8,1024]{2,1,0:T(8,128)} %copy-done.14), channel_id=1, source_target_pairs={{0,1},{1,0},{2,3},{3,2},{4,5},{5,4},{6,7},{7,6},{8,9},{9,8},{10,11... | collective-permute-start | bytes 393224 | tf_op jit(solution)/shard_map/ppermute | solution.py:289
  43.0 20.1 %collective-permute-start.12 = (f32[4,8,1024]{2,1,0:T(8,128)}, f32[4,8,1024]{2,1,0:T(8,128)S(1)}, u32[]{:S(2)}, u32[]{:S(2)}) collective-permute-start(f32[4,8,1024]{2,1,0:T(8,128)} %copy-done.13), channel_id=1, source_target_pairs={{0,2},{1,3},{2,0},{3,1},{4,6},{5,7},{6,4},{7,5},{8,10},{9,11},{10,... | collective-permute-start | bytes 393224 | tf_op jit(solution)/shard_map/ppermute | solution.py:289
  44.6 19.1 %collective-permute-start.13 = (f32[4,8,1024]{2,1,0:T(8,128)}, f32[4,8,1024]{2,1,0:T(8,128)S(1)}, u32[]{:S(2)}, u32[]{:S(2)}) collective-permute-start(f32[4,8,1024]{2,1,0:T(8,128)} %copy-done.12), channel_id=1, source_target_pairs={{0,3},{1,2},{2,1},{3,0},{4,7},{5,6},{6,5},{7,4},{8,11},{9,10},{10,... | collective-permute-start | bytes 393224 | tf_op jit(solution)/shard_map/ppermute | solution.py:289
  46.0 28.0 %collective-permute-start.17 = (f32[4,8,1024]{2,1,0:T(8,128)}, f32[4,8,1024]{2,1,0:T(8,128)S(1)}, u32[]{:S(2)}, u32[]{:S(2)}) collective-permute-start(f32[4,8,1024]{2,1,0:T(8,128)} %copy-done.9), channel_id=1, source_target_pairs={{0,1},{1,0},{2,3},{3,2},{4,5},{5,4},{6,7},{7,6},{8,9},{9,8},{10,11... | collective-permute-start | bytes 393224 | tf_op jit(solution)/shard_map/ppermute | solution.py:289
  46.5 29.0 %collective-permute-start.18 = (f32[4,8,1024]{2,1,0:T(8,128)}, f32[4,8,1024]{2,1,0:T(8,128)S(1)}, u32[]{:S(2)}, u32[]{:S(2)}) collective-permute-start(f32[4,8,1024]{2,1,0:T(8,128)} %copy-done.8), channel_id=1, source_target_pairs={{0,2},{1,3},{2,0},{3,1},{4,6},{5,7},{6,4},{7,5},{8,10},{9,11},{10,... | collective-permute-start | bytes 393224 | tf_op jit(solution)/shard_map/ppermute | solution.py:289
  61.6 14.5 %collective-permute-start.19 = (f32[4,8,1024]{2,1,0:T(8,128)S(1)}, f32[4,8,1024]{2,1,0:T(8,128)S(1)}, u32[]{:S(2)}, u32[]{:S(2)}) collective-permute-start(f32[4,8,1024]{2,1,0:T(8,128)S(1)} %copy-done.7), channel_id=1, source_target_pairs={{0,3},{1,2},{2,1},{3,0},{4,7},{5,6},{6,5},{7,4},{8,11},{9,10},{10,... | collective-permute-start | bytes 393224 | tf_op jit(solution)/shard_map/ppermute | solution.py:289
  63.1 23.2 %collective-permute-start.23 = (f32[4,8,1024]{2,1,0:T(8,128)S(1)}, f32[4,8,1024]{2,1,0:T(8,128)S(1)}, u32[]{:S(2)}, u32[]{:S(2)}) collective-permute-start(f32[4,8,1024]{2,1,0:T(8,128)S(1)} %get-tuple-element.72), channel_id=1, source_target_pairs={{0,1},{1,0},{2,3},{3,2},{4,5},{5,4},{6,7},{7,6},{8,9},{9,8},{10,11... | collective-permute-start | bytes 393224 | tf_op jit(solution)/shard_map/ppermute | solution.py:289
  63.6 24.3 %collective-permute-start.24 = (f32[4,8,1024]{2,1,0:T(8,128)S(1)}, f32[4,8,1024]{2,1,0:T(8,128)S(1)}, u32[]{:S(2)}, u32[]{:S(2)}) collective-permute-start(f32[4,8,1024]{2,1,0:T(8,128)S(1)} %get-tuple-element.73), channel_id=1, source_target_pairs={{0,2},{1,3},{2,0},{3,1},{4,6},{5,7},{6,4},{7,5},{8,10},{9,11},{10,... | collective-permute-start | bytes 393224 | tf_op jit(solution)/shard_map/ppermute | solution.py:289
  74.0 14.4 %collective-permute-start.25 = (f32[4,8,1024]{2,1,0:T(8,128)S(1)}, f32[4,8,1024]{2,1,0:T(8,128)S(1)}, u32[]{:S(2)}, u32[]{:S(2)}) collective-permute-start(f32[4,8,1024]{2,1,0:T(8,128)S(1)} %get-tuple-element.74), channel_id=1, source_target_pairs={{0,3},{1,2},{2,1},{3,0},{4,7},{5,6},{6,5},{7,4},{8,11},{9,10},{10,... | collective-permute-start | bytes 393224 | tf_op jit(solution)/shard_map/ppermute | solution.py:289
  75.5 23.4 %collective-permute-start.8 = (f32[4,8,1024]{2,1,0:T(8,128)S(1)}, f32[4,8,1024]{2,1,0:T(8,128)S(1)}, u32[]{:S(2)}, u32[]{:S(2)}) collective-permute-start(f32[4,8,1024]{2,1,0:T(8,128)S(1)} %get-tuple-element.52), channel_id=1, source_target_pairs={{0,1},{1,0},{2,3},{3,2},{4,5},{5,4},{6,7},{7,6},{8,9},{9,8},{10,11... | collective-permute-start | bytes 393224 | tf_op jit(solution)/shard_map/ppermute | solution.py:289
  76.1 24.5 %collective-permute-start.9 = (f32[4,8,1024]{2,1,0:T(8,128)S(1)}, f32[4,8,1024]{2,1,0:T(8,128)S(1)}, u32[]{:S(2)}, u32[]{:S(2)}) collective-permute-start(f32[4,8,1024]{2,1,0:T(8,128)S(1)} %get-tuple-element.53), channel_id=1, source_target_pairs={{0,2},{1,3},{2,0},{3,1},{4,6},{5,7},{6,4},{7,5},{8,10},{9,11},{10,... | collective-permute-start | bytes 393224 | tf_op jit(solution)/shard_map/ppermute | solution.py:289
  86.3 14.8 %collective-permute-start.10 = (f32[4,8,1024]{2,1,0:T(8,128)S(1)}, f32[4,8,1024]{2,1,0:T(8,128)S(1)}, u32[]{:S(2)}, u32[]{:S(2)}) collective-permute-start(f32[4,8,1024]{2,1,0:T(8,128)S(1)} %get-tuple-element.54), channel_id=1, source_target_pairs={{0,3},{1,2},{2,1},{3,0},{4,7},{5,6},{6,5},{7,4},{8,11},{9,10},{10,... | collective-permute-start | bytes 393224 | tf_op jit(solution)/shard_map/ppermute | solution.py:289
  87.9 14.8 %collective-permute-start.14 = (f32[4,8,1024]{2,1,0:T(8,128)S(1)}, f32[4,8,1024]{2,1,0:T(8,128)S(1)}, u32[]{:S(2)}, u32[]{:S(2)}) collective-permute-start(f32[4,8,1024]{2,1,0:T(8,128)S(1)} %get-tuple-element.60), channel_id=1, source_target_pairs={{0,1},{1,0},{2,3},{3,2},{4,5},{5,4},{6,7},{7,6},{8,9},{9,8},{10,11... | collective-permute-start | bytes 393224 | tf_op jit(solution)/shard_map/ppermute | solution.py:289
  88.4 15.9 %collective-permute-start.15 = (f32[4,8,1024]{2,1,0:T(8,128)S(1)}, f32[4,8,1024]{2,1,0:T(8,128)S(1)}, u32[]{:S(2)}, u32[]{:S(2)}) collective-permute-start(f32[4,8,1024]{2,1,0:T(8,128)S(1)} %get-tuple-element.61), channel_id=1, source_target_pairs={{0,2},{1,3},{2,0},{3,1},{4,6},{5,7},{6,4},{7,5},{8,10},{9,11},{10,... | collective-permute-start | bytes 393224 | tf_op jit(solution)/shard_map/ppermute | solution.py:289
  99.0 7.5 %collective-permute-start.16 = (f32[4,8,1024]{2,1,0:T(8,128)S(1)}, f32[4,8,1024]{2,1,0:T(8,128)S(1)}, u32[]{:S(2)}, u32[]{:S(2)}) collective-permute-start(f32[4,8,1024]{2,1,0:T(8,128)S(1)} %get-tuple-element.62), channel_id=1, source_target_pairs={{0,3},{1,2},{2,1},{3,0},{4,7},{5,6},{6,5},{7,4},{8,11},{9,10},{10,... | collective-permute-start | bytes 393224 | tf_op jit(solution)/shard_map/ppermute | solution.py:289
  100.6 7.7 %collective-permute-start.20 = (f32[4,8,1024]{2,1,0:T(8,128)S(1)}, f32[4,8,1024]{2,1,0:T(8,128)S(1)}, u32[]{:S(2)}, u32[]{:S(2)}) collective-permute-start(f32[4,8,1024]{2,1,0:T(8,128)S(1)} %get-tuple-element.68), channel_id=1, source_target_pairs={{0,1},{1,0},{2,3},{3,2},{4,5},{5,4},{6,7},{7,6},{8,9},{9,8},{10,11... | collective-permute-start | bytes 393224 | tf_op jit(solution)/shard_map/ppermute | solution.py:289
  101.2 9.5 %collective-permute-start.21 = (f32[4,8,1024]{2,1,0:T(8,128)S(1)}, f32[4,8,1024]{2,1,0:T(8,128)S(1)}, u32[]{:S(2)}, u32[]{:S(2)}) collective-permute-start(f32[4,8,1024]{2,1,0:T(8,128)S(1)} %get-tuple-element.69), channel_id=1, source_target_pairs={{0,2},{1,3},{2,0},{3,1},{4,6},{5,7},{6,4},{7,5},{8,10},{9,11},{10,... | collective-permute-start | bytes 393224 | tf_op jit(solution)/shard_map/ppermute | solution.py:289
  102.7 9.3 %collective-permute-start.22 = (f32[4,8,1024]{2,1,0:T(8,128)S(1)}, f32[4,8,1024]{2,1,0:T(8,128)S(1)}, u32[]{:S(2)}, u32[]{:S(2)}) collective-permute-start(f32[4,8,1024]{2,1,0:T(8,128)S(1)} %get-tuple-element.70), channel_id=1, source_target_pairs={{0,3},{1,2},{2,1},{3,0},{4,7},{5,6},{6,5},{7,4},{8,11},{9,10},{10,... | collective-permute-start | bytes 393224 | tf_op jit(solution)/shard_map/ppermute | solution.py:289
  104.4 8.8 %collective-permute-start.26 = (f32[4,8,1024]{2,1,0:T(8,128)S(1)}, f32[4,8,1024]{2,1,0:T(8,128)S(1)}, u32[]{:S(2)}, u32[]{:S(2)}) collective-permute-start(f32[4,8,1024]{2,1,0:T(8,128)S(1)} %get-tuple-element.76), channel_id=1, source_target_pairs={{0,1},{1,0},{2,3},{3,2},{4,5},{5,4},{6,7},{7,6},{8,9},{9,8},{10,11... | collective-permute-start | bytes 393224 | tf_op jit(solution)/shard_map/ppermute | solution.py:289
  106.5 7.5 %collective-permute-start.27 = (f32[4,8,1024]{2,1,0:T(8,128)S(1)}, f32[4,8,1024]{2,1,0:T(8,128)S(1)}, u32[]{:S(2)}, u32[]{:S(2)}) collective-permute-start(f32[4,8,1024]{2,1,0:T(8,128)S(1)} %get-tuple-element.77), channel_id=1, source_target_pairs={{0,2},{1,3},{2,0},{3,1},{4,6},{5,7},{6,4},{7,5},{8,10},{9,11},{10,... | collective-permute-start | bytes 393224 | tf_op jit(solution)/shard_map/ppermute | solution.py:289
  108.3 7.1 %collective-permute-start.28 = (f32[4,8,1024]{2,1,0:T(8,128)S(1)}, f32[4,8,1024]{2,1,0:T(8,128)S(1)}, u32[]{:S(2)}, u32[]{:S(2)}) collective-permute-start(f32[4,8,1024]{2,1,0:T(8,128)S(1)} %get-tuple-element.78), channel_id=1, source_target_pairs={{0,3},{1,2},{2,1},{3,0},{4,7},{5,6},{6,5},{7,4},{8,11},{9,10},{10,... | collective-permute-start | bytes 393224 | tf_op jit(solution)/shard_map/ppermute | solution.py:289
  (26 other events, 125.1 us)

commit v2 on v1

v2 whole, which is shorter than its diff:
```python
import functools
import math

import jax
import jax.numpy as jnp
import numpy as np
from jax import lax
from jax.experimental import pallas as pl
from jax.experimental.pallas import tpu as pltpu
from jax.sharding import PartitionSpec as P

N = 16
HALF = N // 2
PLANE = N * N
TILE = N * HALF
CELLS = 8
courant = 0.45
collision_timestep = 0.1
bf16 = jnp.bfloat16
f32 = jnp.float32


def velocity_tables():
    levels = ((2.0 * np.arange(N, dtype=np.float32) - (N - 1)) / (N - 1)).astype(np.float64)
    cx = np.repeat(levels, PLANE)
    cy = np.tile(np.repeat(levels, N), N)
    cz = np.tile(levels, PLANE)
    still = np.exp(-4.5 * (cx * cx + cy * cy + cz * cz))
    moving = np.exp(-0.5 * ((3.0 * cx - 1.0) ** 2 + 9.0 * cy * cy + 9.0 * cz * cz))
    rows = [np.abs(cx), np.abs(cy), still / still.sum(), moving / moving.sum()]
    rows += [np.zeros_like(cx)] * (8 - len(rows))
    return np.stack(rows).astype(np.float32).reshape(8, N, PLANE).transpose(1, 0, 2)


def fourier_matrices():
    n = np.arange(N)
    angles = 2.0 * math.pi * ((n[:, None] * n[None, :]) % N) / N
    rounded = lambda t: t.astype(np.float32).astype(jnp.bfloat16).astype(np.float64)
    c, s = rounded(np.cos(angles)), rounded(np.sin(angles))
    by_cell, by_line = np.eye(CELLS), np.eye(N)
    forward_i = np.concatenate([np.kron(c, by_cell), np.kron(-s, by_cell)], 0)
    cj, sj = np.kron(c, by_line), np.kron(s, by_line)
    pick = half_selection()[:, :PLANE]
    ck, sk = np.kron(by_line, c) @ pick, np.kron(by_line, s) @ pick
    turn = np.stack([np.stack([c, -s], -1), np.stack([s, c], -1)], 0) / N
    inverse_i = np.kron(turn.reshape(2 * N, 2 * N), by_cell)
    c, s = c / N, s / N
    spread = lambda left, right: np.einsum("bj,d->jbd", left, right)
    last = np.zeros((2, N, HALF, N, N))
    for k in range(1, HALF):
        last[0, :, k] = 2.0 * (spread(c, c[:, k]) - spread(s, s[:, k]))
        last[1, :, k] = -2.0 * (spread(c, s[:, k]) + spread(s, c[:, k]))
    last[0, :, 0] = spread(c, c[:, 0]) + spread(s, c[:, HALF])
    last[1, :, 0] = spread(c, c[:, HALF]) - spread(s, c[:, 0])
    inverse_jk = last.reshape(PLANE, PLANE)
    forward_i = np.concatenate([forward_i, np.zeros_like(forward_i)], 1)
    return np.stack([forward_i, cj, sj, ck, sk, inverse_i, inverse_jk]).astype(np.float32)


def half_selection():
    eye = np.eye(PLANE, dtype=np.float32).reshape(PLANE, N, N)
    low = eye[..., :HALF]
    top = np.zeros_like(low)
    top[..., 0] = eye[..., HALF]
    straight = np.concatenate([low.reshape(PLANE, TILE), top.reshape(PLANE, TILE)], 1)
    flip = (-np.arange(N)) % N
    mirrored = straight.reshape(N, N, PLANE)[flip][:, flip].reshape(PLANE, PLANE)
    return np.concatenate([straight, mirrored], 1)


def dot(left, right):
    return jnp.dot(left, right, preferred_element_type=f32)


def call(kernel, out_shape, operands, flops=0, scratch=(), limit=24, **options):
    moved = sum(a.size * a.dtype.itemsize for a in list(operands) + jax.tree.leaves(out_shape))
    return pl.pallas_call(
        kernel, out_shape=out_shape, scratch_shapes=list(scratch),
        compiler_params=pltpu.CompilerParams(vmem_limit_bytes=limit * 2 ** 20),
        cost_estimate=pl.CostEstimate(flops=flops, bytes_accessed=moved, transcendentals=0),
        **options,
    )(*operands)


def setup_body(first_ref, second_ref, loss_ref, pick_ref, table_ref, low_ref, top_ref, matrix_ref):
    dirs = first_ref.shape[0]
    matrix_ref[...] = table_ref[...].astype(bf16)
    parts = []
    for i in range(N):
        at = slice(PLANE * i, PLANE * (i + 1))
        value = jnp.concatenate([first_ref[:, at], second_ref[:, at], jnp.broadcast_to(loss_ref[:, at], (dirs, PLANE))], 0)
        for _ in range(3):
            part = value.astype(bf16)
            value = value - part.astype(f32)
            parts.append(part)
    picked = dot(jnp.concatenate(parts, 0), pick_ref[...].astype(bf16)).reshape(N, 3, 3 * dirs, 2 * PLANE)
    picked = picked[:, 0] + picked[:, 1] + picked[:, 2]
    for i in range(N):
        even = 0.5 * (picked[i, :, :PLANE] + picked[-i % N, :, PLANE:])
        low_ref[i] = even[:, :TILE]
        top_ref[i] = even[:, TILE:]


def setup(first_kernel, second_kernel, loss_kernel):
    total = 3 * first_kernel.shape[0]
    shape = jax.ShapeDtypeStruct((N, total, TILE), f32)
    matrices = fourier_matrices()
    operands = (first_kernel, second_kernel, loss_kernel[None, :], jnp.asarray(half_selection()), jnp.asarray(matrices))
    return call(setup_body, (shape, shape, jax.ShapeDtypeStruct(matrices.shape, bf16)), operands,
                flops=6 * total * N * PLANE * 2 * PLANE)


def column_of(table, lane, row):
    return jnp.sum(jnp.where(lane == row, table, 0.0), axis=1, keepdims=True)


def walled(kind, density, raw, table, at):
    return jnp.where(kind == 0.0, raw, jnp.where(kind == 1.0, table[2:3, at], table[3:4, at]) * density)


def window(rank, own_rows, total_rows, first_row, count):
    return jnp.clip(rank * own_rows + first_row - 1, 0, total_rows - count - 2)


def columns_body(cells_ref, kind_ref, after_ref, first_ref, last_ref):
    del after_ref
    rows, cols, width = cells_ref.shape
    half = width // 2
    lane = lax.broadcasted_iota(jnp.int32, (cols, TILE), 1)
    place = lax.broadcasted_iota(jnp.int32, (cols, rows), 1)
    kinds = kind_ref[...]

    def one_row(row, _):
        values = cells_ref[row]
        total = jnp.sum(values, axis=1, keepdims=True)
        tail = jnp.where(lane == 0, total, jnp.where(lane == 1, column_of(kinds, place, row), 0.0))
        for block in range(width // PLANE):
            to = slice(TILE * block, TILE * (block + 1))
            at = PLANE * block
            first_ref[row, :, to] = values[:1, at:at + TILE]
            last_ref[row, :, to] = values[cols - 1:, at + TILE:at + PLANE]
        first_ref[row, :, half:] = tail[:1]
        last_ref[row, :, half:] = tail[cols - 1:]
        return 0

    lax.fori_loop(0, rows, one_row, 0, unroll=8)


def cut_body(groups, first_row, rank_ref, cells_ref, after_ref, *refs):
    del after_ref
    columns, outs, sems = refs[:-1 - groups], refs[-1 - groups:-1], refs[-1]
    rows = cells_ref.shape[0]
    extra = 2 if columns else 0
    copies = []
    for flip, out_ref in enumerate(outs):
        count = out_ref.shape[0] - extra
        taker = lax.bitwise_xor(rank_ref[0], flip)
        top = window(taker, rows // groups, rows, first_row, count - 2)
        copies.append(pltpu.make_async_copy(cells_ref.at[pl.ds(top, count)], out_ref.at[pl.ds(0, count)], sems.at[flip]))
    for copy in copies:
        copy.start()
    for flip, out_ref in enumerate(outs):
        count = out_ref.shape[0] - extra
        top = lax.bitwise_xor(rank_ref[0], flip) * (rows // groups) + first_row
        for side, column in enumerate(columns):
            half = column.shape[2] - TILE
            for step in range(count - 2):
                out_ref[count, step:step + 1, half * side:half * (side + 1)] = column[top + step, :, :half]
                out_ref[count + 1, step:step + 1, TILE * side:TILE * (side + 1)] = column[top + step, :, half:]
    for copy in copies:
        copy.wait()


def edges_body(groups, first_row, passing, rank_ref, *refs):
    sources, refs = refs[:groups], refs[groups:]
    kind_ref, tables_ref = refs[1:3]
    first_ref, last_ref, density_ref = refs[3 + passing:6 + passing]
    cols, total_rows = kind_ref.shape
    count = first_ref.shape[0] // N
    carried = sources[0].shape[0] > count + 2
    half = sources[0].shape[2] // 2
    per = N // groups
    rank = rank_ref[0]
    kinds = kind_ref[...]
    place = lax.broadcasted_iota(jnp.int32, kinds.shape, 1)
    lane = lax.broadcasted_iota(jnp.int32, density_ref.shape, 1)
    start = window(rank, total_rows // groups, total_rows, first_row, count)
    densities = jnp.zeros(density_ref.shape, f32)
    for step in range(count + 2):
        row = jnp.clip(rank * (total_rows // groups) + first_row - 1 + step, 0, total_rows - 1)
        values = [source[row - start] for source in sources]
        density = jnp.sum(sum(values), axis=1, keepdims=True)
        densities = jnp.where(lane == step, density, densities)
        if 0 < step <= count:
            kind = column_of(kinds, place, row)
            at = slice(step - 1, step)
            tails = [[source[count + 3, at, TILE * side:TILE * (side + 1)] for source in sources] for side in range(2) if carried]
            known = [(column_of(tail[0], lane[:1], 1), column_of(sum(tail), lane[:1], 0)) for tail in tails]
            for flip, (value, source) in enumerate(zip(values, sources)):
                for i in range(per):
                    at = lax.bitwise_xor(rank, flip) * per + i
                    table = tables_ref[at]
                    for tile, cell, out_ref in ((0, 0, first_ref), (1, cols - 1, last_ref)):
                        of = slice(TILE * tile, TILE * (tile + 1))
                        if carried:
                            raw = source[count + 2, step - 1:step, half * (1 - tile) + TILE * i:half * (1 - tile) + TILE * (i + 1)]
                            out_ref[(step - 1) * N + at] = walled(*known[1 - tile], raw, table, of)
                        else:
                            edge = walled(kind, density, value[:, PLANE * i + TILE * tile:PLANE * i + TILE * (tile + 1)], table, of)
                            out_ref[(step - 1) * N + at] = edge[cell:cell + 1]
    density_ref[...] = densities


def collide_body(groups, dirs, batch, first_row, rank_ref, *refs):
    sources, refs = refs[:groups], refs[groups:]
    before_ref, after_ref, density_ref, kind_ref, tables_ref, low_ref, top_ref, matrix_ref, _ = refs[:9]
    outs, refs = refs[9:9 + groups], refs[9 + groups:]
    moved_refs, spec_refs, gain_ref = refs[:2], refs[2:4], refs[4]
    rows = N * CELLS
    per = N // groups
    steps = outs[0].shape[0]
    total_rows = kind_ref.shape[1]
    own_rows = total_rows // groups
    rank = rank_ref[0]
    sub = lax.broadcasted_iota(jnp.int32, (CELLS, TILE), 0)
    place = lax.broadcasted_iota(jnp.int32, kind_ref.shape, 1)
    lane = lax.broadcasted_iota(jnp.int32, density_ref.shape, 1)
    kinds, densities = kind_ref[...], density_ref[...]
    origin = rank * own_rows + first_row
    start = window(rank, own_rows, total_rows, first_row, steps)

    def cells_of(step):
        row = jnp.clip(origin + step, 0, total_rows - 1)
        return row - start, column_of(kinds, place, row), column_of(densities, lane, step + 1)

    def turned(value, at):
        straight, crossed = dot(value, matrix_ref[at]), dot(value, matrix_ref[at + 1])
        return jnp.concatenate([straight[:rows] + crossed[rows:], straight[rows:] - crossed[:rows]], 0)

    def prepare(step, moved_ref, spec_ref):
        now_at, kind, density = cells_of(step)
        past, ahead = cells_of(step - 1), cells_of(step + 1)
        for flip, source in enumerate(sources):
            owner = lax.bitwise_xor(rank, flip)
            positive = owner >= groups // 2
            other_at, other_kind, other_density = (jnp.where(positive, p, a) for p, a in zip(past, ahead))
            for i in range(per):
                line = owner * per + i
                table = tables_ref[line]
                for tile in range(2):
                    at = slice(TILE * tile, TILE * (tile + 1))
                    of = slice(PLANE * i + TILE * tile, PLANE * i + TILE * (tile + 1))
                    now = walled(kind, density, source[now_at, :, of], table, at)
                    other = walled(other_kind, other_density, source[other_at, :, of], table, at)
                    if tile:
                        near = jnp.where(sub == 0, before_ref[step * N + line], pltpu.roll(now, 1, 0))
                    else:
                        near = jnp.where(sub == CELLS - 1, after_ref[step * N + line], pltpu.roll(now, CELLS - 1, 0))
                    drift = table[0:1, at] * (now - other) + table[1:2, at] * (now - near)
                    moved_ref[line, :, at] = jnp.where(kind == 0.0, now - courant * drift, now)
        yield
        value = dot(matrix_ref[0, :, :rows], moved_ref[...].reshape(rows, PLANE).astype(bf16)).astype(bf16)
        yield
        value = turned(value, 1).astype(bf16)
        yield
        spec_ref[...] = turned(value, 3).astype(bf16).astype(f32)
        yield

    def finish(step, moved_ref, spec_ref, beside):
        def weighted(*pair):
            parts = [[] for _ in pair]
            for i in range(N):
                re_at, im_at = slice(CELLS * i, CELLS * (i + 1)), slice(rows + CELLS * i, rows + CELLS * (i + 1))
                low_re, top_re = spec_ref[re_at, :TILE], spec_ref[re_at, TILE:]
                low_im, top_im = spec_ref[im_at, :TILE], spec_ref[im_at, TILE:]
                for p, part in zip(pair, parts):
                    low, top = low_ref[i, p:p + 1, :], top_ref[i, p:p + 1, :]
                    part.append(low * low_re - top * top_im)
                    part.append(low * low_im + top * top_re)
            return jnp.concatenate([jnp.concatenate(part, 0) for part in parts], 1).astype(bf16)

        def along_i(*pair):
            value = dot(matrix_ref[5], weighted(*pair)).astype(bf16)
            return [jnp.concatenate([value[:rows, TILE * t:TILE * (t + 1)], value[rows:, TILE * t:TILE * (t + 1)]], 1)
                    for t in range(len(pair))]

        gain_ref[...] = jnp.zeros_like(gain_ref)
        for first in range(0, dirs, batch):
            stack = []
            for p in range(first, min(first + batch, dirs)):
                stack += along_i(p, dirs + p)
            value = dot(jnp.concatenate(stack, 0), matrix_ref[6])
            total = gain_ref[...]
            for at in range(0, value.shape[0], 2 * rows):
                total = total + value[at:at + rows] * value[at + rows:at + 2 * rows]
            gain_ref[...] = total
            next(beside, None)
        for _ in beside:
            pass
        loss = dot(along_i(2 * dirs)[0], matrix_ref[6])
        now = moved_ref[...]
        collision = (gain_ref[...] - now.reshape(rows, PLANE) * loss).reshape(N, CELLS, PLANE)
        moved_ref[...] = jnp.where(cells_of(step)[1] == 0.0, now + collision_timestep * collision, now)
        for flip, out_ref in enumerate(outs):
            at = lax.bitwise_xor(rank, flip) * per
            for i in range(per):
                out_ref[step, :, PLANE * i:PLANE * (i + 1)] = moved_ref[at + i]

    for _ in prepare(0, moved_refs[0], spec_refs[0]):
        pass

    def two_rows(pair, _):
        one, other = 2 * pair, jnp.minimum(2 * pair + 1, steps - 1)
        following = jnp.minimum(2 * pair + 2, steps - 1)
        finish(one, moved_refs[0], spec_refs[0], prepare(other, moved_refs[1], spec_refs[1]))
        finish(other, moved_refs[1], spec_refs[1], prepare(following, moved_refs[0], spec_refs[0]))
        return 0

    lax.fori_loop(0, (steps + 1) // 2, two_rows, 0)


def collide(rank, sources, before, after, density, kinds, tables, low, top, matrices, earlier, first_row, steps):
    groups = len(sources)
    dirs = low.shape[1] // 3
    _, cols, width = sources[0].shape
    vmem = pl.BlockSpec(memory_space=pltpu.VMEM)
    shape = jax.ShapeDtypeStruct((steps, cols, width), f32)
    operands = (*sources, before, after, density, kinds, tables, low, top, matrices, earlier)
    cells = pltpu.VMEM((N, CELLS, PLANE), f32)
    spec = pltpu.VMEM((2 * N * CELLS, PLANE), f32)
    return call(
        functools.partial(collide_body, groups, dirs, 4, first_row), (shape,) * groups, (rank, *operands),
        flops=steps * 2 * PLANE ** 3 * (2 * dirs + 6),
        scratch=[cells, cells, spec, spec, pltpu.VMEM((N * CELLS, PLANE), f32)],
        in_specs=[pl.BlockSpec(memory_space=pltpu.SMEM)] + [vmem] * (len(operands) - 1) + [pl.BlockSpec(memory_space=pl.ANY)],
        out_specs=(vmem,) * groups,
    )


def on_device(distribution, cell_type, first_kernel, second_kernel, loss_kernel):
    rows, cols, width = distribution.shape
    groups = lax.axis_size("vel")
    rank = lax.axis_index("vel")
    spots = lax.axis_size("cell")
    own_rows = rows // groups
    half = (own_rows // 4) * 2
    chunks = [(0, half), (half, own_rows - half)]
    rank_word = rank.astype(jnp.int32)[None]
    tables = jnp.asarray(velocity_tables())
    kinds = cell_type.astype(f32).T
    vmem = pl.BlockSpec(memory_space=pltpu.VMEM)
    smem = pl.BlockSpec(memory_space=pltpu.SMEM)
    anywhere = pl.BlockSpec(memory_space=pl.ANY)

    def swap(values):
        swapped = {0: values[0]}
        for flip in reversed(range(1, groups)):
            swapped[flip] = lax.ppermute(values[flip], "vel", [(i, i ^ flip) for i in range(groups)])
        return [swapped[flip] for flip in range(groups)]

    def cut(first_row, count, earlier, *columns):
        block = jax.ShapeDtypeStruct((count + 2 + len(columns), cols, width), f32)
        place = vmem
        return call(
            functools.partial(cut_body, groups, first_row), (block,) * groups, (rank_word, distribution, earlier, *columns),
            in_specs=[smem, anywhere, anywhere] + [vmem] * len(columns), out_specs=(place,) * groups,
            scratch=[pltpu.SemaphoreType.DMA((groups,))], limit=24 if columns else 52)

    def rims(first_row, count, sources, *passing):
        edge = jax.ShapeDtypeStruct((count * N, 1, TILE), f32)
        same = [jax.ShapeDtypeStruct(value.shape, f32) for value in passing]
        return call(
            functools.partial(edges_body, groups, first_row, len(passing)),
            (edge, edge, jax.ShapeDtypeStruct((cols, TILE), f32), *same),
            (rank_word, *sources, matrices, kinds, tables, *passing),
            in_specs=[smem] + [vmem] * groups + [anywhere, vmem, vmem] + [anywhere] * len(passing),
            out_specs=(vmem,) * 3 + (anywhere,) * len(passing),
            input_output_aliases={groups + 4 + at: 3 + at for at in range(len(passing))})

    def to_neighbours(first, last):
        return (lax.ppermute(last, "cell", [(i, i + 1) for i in range(spots - 1)]),
                lax.ppermute(first, "cell", [(i + 1, i) for i in range(spots - 1)]))

    (first_row, count), (next_row, next_count) = chunks
    cuts = cut(first_row, count, rank_word)
    sources = swap(cuts)
    low, top, matrices = setup(first_kernel, second_kernel, loss_kernel)
    column = jax.ShapeDtypeStruct((rows, 1, width // 2 + TILE), f32)
    columns = to_neighbours(*call(
        columns_body, (column, column), (distribution, kinds, cuts[0]), in_specs=[vmem, vmem, anywhere], out_specs=(vmem,) * 2))
    first, last, density = rims(first_row, count, sources)
    edges = to_neighbours(first, last)
    following = cut(next_row, next_count, sources[-1], *columns)
    done = collide(rank_word, sources, *edges, density, kinds, tables, low, top, matrices, following[0], first_row, count)
    sources = swap(following)
    after, before, density, *done = rims(next_row, next_count, sources, *done)
    home = swap(done)
    done = collide(rank_word, sources, before, after, density, kinds, tables, low, top, matrices, done[0], next_row, next_count)
    home = [home, swap(done)]
    updated = jnp.zeros((rows, cols, width), f32)
    for (first_row, count), blocks in zip(chunks, home):
        for flip, block in enumerate(blocks):
            updated = lax.dynamic_update_slice_in_dim(updated, block, (rank ^ flip) * own_rows + first_row, 0)
    return updated


def solution(mesh):
    return jax.shard_map(
        on_device,
        mesh=mesh,
        in_specs=(P(None, "cell", "vel"), P(None, "cell"), P(), P(), P()),
        out_specs=P(None, "cell", "vel"),
        check_vma=False,
    )
```

time: 116 us -> 84.3 us (0.73)
  starting transfers between devices: 35.6 us -> 21.7 us
  Pallas kernels: 50.5 us -> 38.2 us
  local copies, waits for them, and re-layouts: 15.8 us -> 5.56 us
  waiting for transfers between devices: 13.8 us -> 17.1 us
    ppermute x29 -> x16, starting transfers between devices: 35.6 us -> 21.7 us  [the longest x12 15.6 us: swap(): lax.ppermute(values[flip], 'vel', [(i, i ^ flip) for i in range(groups)])]
    pallas_call x8, Pallas kernels: 50.5 us -> 38.2 us  [call(): pl.pallas_call(kernel, out_shape=out_shape, scratch_shapes=list(scratch),...]
    unnamed x58 -> x36, local copies, waits for them, and re-layouts: 13.3 us -> 4.44 us
    ppermute x29 -> x16, waiting for transfers between devices: 13.8 us -> 17.1 us  [the longest x12 17.1 us: swap(): lax.ppermute(values[flip], 'vel', [(i, i ^ flip) for i in range(groups)])]
  transfers between devices with their start and end apart: 29 -> 16, of which waited for: 10 -> 6; matrix products, arithmetic and copies ran while one was open for 2% -> 1% of each run, Pallas kernels for 34% -> 44%
where the time goes in v2:
time: 84.3 us; the launch traced here: 83.7 us
  Pallas kernels  38.2 us (45%)
  starting transfers between devices  21.7 us (26%)
  waiting for transfers between devices  17.1 us (20%)
  local copies, waits for them, and re-layouts  5.56 us (7%)
    pallas_call x8, Pallas kernels, call(): pl.pallas_call(kernel, out_shape=out_shape, scratch_shapes=list(scratch),...  38.2 us
    ppermute x12, waiting for transfers between devices, swap(): lax.ppermute(values[flip], 'vel', [(i, i ^ flip) for i in range(groups)])  17.1 us
    ppermute x12, starting transfers between devices, swap(): lax.ppermute(values[flip], 'vel', [(i, i ^ flip) for i in range(groups)])  15.6 us
    unnamed x36, local copies, waits for them, and re-layouts  4.44 us
    ppermute x2, starting transfers between devices, to_neighbours(): lax.ppermute(last, 'cell', [(i, i + 1) for i in range(spots - 1)])  3.56 us
    ppermute x2, starting transfers between devices, to_neighbours(): lax.ppermute(first, 'cell', [(i + 1, i) for i in range(spots - 1)])  2.57 us
  transfers between devices with their start and end apart: 16, of which 6 were waited for; matrix products, arithmetic and copies ran while one was open for 1% of the time, Pallas kernels for 44%

profile of v2, /device:TPU:0, one launch (start us, length us, event | category | flops | bytes accessed | tf_op | source)
XLA Modules:
  0.0 83.7 jit_solution(1744138965229111390)
XLA Ops:
  0.0 1.5 %shard_map.82 = (f32[10,8,1024]{2,1,0:T(8,128)S(1)}, f32[10,8,1024]{2,1,0:T(8,128)S(1)}, f32[10,8,1024]{2,1,0:T(8,128)S(1)}, f32[10,8,1024]{2,1,0:T(8,128)S(1)}) custom-call(s32[1]{0:T(128)} %bitcast.rank_ref.after_ref, f32[64,8,1024]{2,1,0:T(8,128)} %cells_ref.5, s32[1]{0:T(128)} %bitcast.rank_ref.after_ref), custom_call_target="tpu_custom_call" | custom-call | bytes 3407880 | tf_op jit(solution)/shard_map/pallas_call | solution.py:77
  1.5 4.0 %collective-permute-start = (f32[10,8,1024]{2,1,0:T(8,128)S(1)}, f32[10,8,1024]{2,1,0:T(8,128)S(1)}, u32[]{:S(2)}, u32[]{:S(2)}) collective-permute-start(f32[10,8,1024]{2,1,0:T(8,128)S(1)} %get-tuple-element.36), channel_id=1, source_target_pairs={{0,3},{1,2},{2,1},{3,0},{4,7},{5,6},{6,5},{7,4},{8,11},{9,10},{10,... | collective-permute-start | bytes 983048 | tf_op jit(solution)/shard_map/ppermute | solution.py:358
  5.4 0.5 collective-permute-start.6
  6.1 0.7 convert_bitcast_fusion.kind_ref.refs_5_.refs_7_
  6.8 1.7 %shard_map.83 = (f32[64,1,640]{2,1,0:T(1,128)}, f32[64,1,640]{2,1,0:T(1,128)}) custom-call(f32[64,8,1024]{2,1,0:T(8,128)S(1)} %copy-done, f32[8,64]{1,0:T(8,128)S(1)} %convert_bitcast_fusion.kind_ref.refs_5_.refs_7_, f32[10,8,1024]{2,1,0:T(8,128)S(1)} %get-tuple-element.37.after_ref.refs_0_), custom_call_target="tpu_custom_call" | custom-call | bytes 2754560 | tf_op jit(solution)/shard_map/pallas_call | solution.py:77
  8.4 2.0 %collective-permute-start.1 = (f32[64,1,640]{2,1,0:T(1,128)}, f32[64,1,640]{2,1,0:T(1,128)}, u32[]{:S(2)}, u32[]{:S(2)}) collective-permute-start(f32[64,1,640]{2,1,0:T(1,128)} %get-tuple-element.38), channel_id=1, source_target_pairs={{0,4},{4,8},{8,12},{12,16},{16,20},{20,24},{24,28},{1,5},{5,9},{9,... | collective-permute-start | bytes 491528 | tf_op jit(solution)/shard_map/ppermute | solution.py:381
  10.4 1.3 %collective-permute-start.2 = (f32[64,1,640]{2,1,0:T(1,128)}, f32[64,1,640]{2,1,0:T(1,128)}, u32[]{:S(2)}, u32[]{:S(2)}) collective-permute-start(f32[64,1,640]{2,1,0:T(1,128)} %get-tuple-element.39), channel_id=1, source_target_pairs={{4,0},{8,4},{12,8},{16,12},{20,16},{24,20},{28,24},{5,1},{9,5},{13... | collective-permute-start | bytes 491528 | tf_op jit(solution)/shard_map/ppermute | solution.py:382
  11.7 0.9 %copy-done.10 = f32[16,4096]{1,0:T(8,128)S(1)} copy-done((f32[16,4096]{1,0:T(8,128)S(1)}, f32[16,4096]{1,0:T(8,128)}, u32[]{:S(2)}) %copy-start.10) | copy-done | bytes 262168
  12.7 0.9 %copy-done.11 = f32[16,4096]{1,0:T(8,128)S(1)} copy-done((f32[16,4096]{1,0:T(8,128)S(1)}, f32[16,4096]{1,0:T(8,128)}, u32[]{:S(2)}) %copy-start.11) | copy-done | bytes 262168
  13.6 0.7 copy-done.12
  14.3 0.9 %shard_map.85 = (f32[16,48,128]{2,1,0:T(8,128)S(1)}, f32[16,48,128]{2,1,0:T(8,128)S(1)}, bf16[7,256,256]{2,1,0:T(8,128)(2,1)S(1)}) custom-call(f32[16,4096]{1,0:T(8,128)S(1)} %copy-done.10, f32[16,4096]{1,0:T(8,128)S(1)} %copy-done.11, f32[1,4096]{1,0:T(1,128)S(1)} %bitcast.4, f32[256,512]{1,0:T(8,128)S(1)} %copy-done.4, f32[7,256,256]{2,1,0:T(8,128)S(1)} %copy-done.1), custom_call_target="tpu_custom_call" | custom-call | flops 603979776 | bytes 4603904 | tf_op jit(solution)/shard_map/pallas_call | solution.py:77
  15.2 5.2 %collective-permute-done.6.refs_1_ = f32[10,8,1024]{2,1,0:T(8,128)S(1)} collective-permute-done((f32[10,8,1024]{2,1,0:T(8,128)S(1)}, f32[10,8,1024]{2,1,0:T(8,128)S(1)}, u32[]{:S(2)}, u32[]{:S(2)}) %collective-permute-start.6) | collective-permute-done | bytes 327712 | tf_op jit(solution)/shard_map/ppermute | solution.py:358
  20.5 0.9 %shard_map.86 = (f32[128,1,128]{2,1,0:T(1,128)}, f32[128,1,128]{2,1,0:T(1,128)}, f32[8,128]{1,0:T(8,128)S(1)}) custom-call(s32[1]{0:T(128)} %bitcast.rank_ref.after_ref, f32[10,8,1024]{2,1,0:T(8,128)S(1)} %get-tuple-element.37.after_ref.refs_0_, f32[10,8,1024]{2,1,0:T(8,128)S(1)} %collective-permute-done.6.refs_1_, ...), custom_call_target="tpu_custom_call" | custom-call | bytes 2496516 | tf_op jit(solution)/shard_map/pallas_call | solution.py:77
  21.4 0.7 copy-done.2
  22.1 1.6 %collective-permute-start.8 = (f32[128,1,128]{2,1,0:T(1,128)}, f32[128,1,128]{2,1,0:T(1,128)S(1)}, u32[]{:S(2)}, u32[]{:S(2)}) collective-permute-start(f32[128,1,128]{2,1,0:T(1,128)} %get-tuple-element.47), channel_id=1, source_target_pairs={{0,4},{4,8},{8,12},{12,16},{16,20},{20,24},{24,28},{1,5},{5,9},{9,... | collective-permute-start | bytes 196616 | tf_op jit(solution)/shard_map/ppermute | solution.py:381
  23.7 1.3 %collective-permute-start.9 = (f32[128,1,128]{2,1,0:T(1,128)}, f32[128,1,128]{2,1,0:T(1,128)}, u32[]{:S(2)}, u32[]{:S(2)}) collective-permute-start(f32[128,1,128]{2,1,0:T(1,128)} %get-tuple-element.48), channel_id=1, source_target_pairs={{4,0},{8,4},{12,8},{16,12},{20,16},{24,20},{28,24},{5,1},{9,5},{13... | collective-permute-start | bytes 196616 | tf_op jit(solution)/shard_map/ppermute | solution.py:382
  25.1 1.0 %copy-done.3 = f32[10,8,1024]{2,1,0:T(8,128)S(1)} copy-done((f32[10,8,1024]{2,1,0:T(8,128)S(1)}, f32[10,8,1024]{2,1,0:T(8,128)}, u32[]{:S(2)}) %copy-start.3) | copy-done | bytes 327704
  26.1 1.6 %shard_map.84 = (f32[12,8,1024]{2,1,0:T(8,128)S(1)}, f32[12,8,1024]{2,1,0:T(8,128)S(1)}, f32[12,8,1024]{2,1,0:T(8,128)S(1)}, f32[12,8,1024]{2,1,0:T(8,128)S(1)}) custom-call(s32[1]{0:T(128)} %bitcast.rank_ref.after_ref, f32[64,8,1024]{2,1,0:T(8,128)S(1)} %copy-done, f32[10,8,1024]{2,1,0:T(8,128)S(1)} %copy-done.3, ...), custom_call_target="tpu_custom_call" | custom-call | bytes 4325380 | tf_op jit(solution)/shard_map/pallas_call | solution.py:77
  27.7 1.7 %collective-permute-start.3 = (f32[12,8,1024]{2,1,0:T(8,128)S(1)}, f32[12,8,1024]{2,1,0:T(8,128)S(1)}, u32[]{:S(2)}, u32[]{:S(2)}) collective-permute-start(f32[12,8,1024]{2,1,0:T(8,128)S(1)} %get-tuple-element.41), channel_id=1, source_target_pairs={{0,1},{1,0},{2,3},{3,2},{4,5},{5,4},{6,7},{7,6},{8,9},{9,8},{10,11... | collective-permute-start | bytes 1179656 | tf_op jit(solution)/shard_map/ppermute | solution.py:358
  29.5 1.5 %collective-permute-start.4 = (f32[12,8,1024]{2,1,0:T(8,128)S(1)}, f32[12,8,1024]{2,1,0:T(8,128)S(1)}, u32[]{:S(2)}, u32[]{:S(2)}) collective-permute-start(f32[12,8,1024]{2,1,0:T(8,128)S(1)} %get-tuple-element.42), channel_id=1, source_target_pairs={{0,2},{1,3},{2,0},{3,1},{4,6},{5,7},{6,4},{7,5},{8,10},{9,11},{10,... | collective-permute-start | bytes 1179656 | tf_op jit(solution)/shard_map/ppermute | solution.py:358
  31.3 16.1 %shard_map.87 = (f32[8,8,1024]{2,1,0:T(8,128)S(1)}, f32[8,8,1024]{2,1,0:T(8,128)S(1)}, f32[8,8,1024]{2,1,0:T(8,128)S(1)}, f32[8,8,1024]{2,1,0:T(8,128)S(1)}) custom-call(s32[1]{0:T(128)} %bitcast.rank_ref.after_ref, f32[10,8,1024]{2,1,0:T(8,128)S(1)} %get-tuple-element.37.after_ref.refs_0_, f32[10,8,1024]{2,1,0:T(8,128)S(1)} %copy-done.7, ...), custom_call_target="tpu_custom_call" | custom-call | flops 10200547328 | bytes 4724740 | tf_op jit(solution)/shard_map/pallas_call | solution.py:77
  48.3 1.5 %collective-permute-start.10 = (f32[8,8,1024]{2,1,0:T(8,128)S(1)}, f32[8,8,1024]{2,1,0:T(8,128)S(1)}, u32[]{:S(2)}, u32[]{:S(2)}) collective-permute-start(f32[8,8,1024]{2,1,0:T(8,128)S(1)} %get-tuple-element.57), channel_id=1, source_target_pairs={{0,1},{1,0},{2,3},{3,2},{4,5},{5,4},{6,7},{7,6},{8,9},{9,8},{10,11... | collective-permute-start | bytes 786440 | tf_op jit(solution)/shard_map/ppermute | solution.py:358
  49.8 1.2 %collective-permute-start.11 = (f32[8,8,1024]{2,1,0:T(8,128)S(1)}, f32[8,8,1024]{2,1,0:T(8,128)S(1)}, u32[]{:S(2)}, u32[]{:S(2)}) collective-permute-start(f32[8,8,1024]{2,1,0:T(8,128)S(1)} %get-tuple-element.58), channel_id=1, source_target_pairs={{0,2},{1,3},{2,0},{3,1},{4,6},{5,7},{6,4},{7,5},{8,10},{9,11},{10,... | collective-permute-start | bytes 786440 | tf_op jit(solution)/shard_map/ppermute | solution.py:358
  51.0 1.1 %collective-permute-start.12 = (f32[8,8,1024]{2,1,0:T(8,128)S(1)}, f32[8,8,1024]{2,1,0:T(8,128)S(1)}, u32[]{:S(2)}, u32[]{:S(2)}) collective-permute-start(f32[8,8,1024]{2,1,0:T(8,128)S(1)} %get-tuple-element.59), channel_id=1, source_target_pairs={{0,3},{1,2},{2,1},{3,0},{4,7},{5,6},{6,5},{7,4},{8,11},{9,10},{10,... | collective-permute-start | bytes 786440 | tf_op jit(solution)/shard_map/ppermute | solution.py:358
  52.1 15.3 %shard_map.89 = (f32[8,8,1024]{2,1,0:T(8,128)S(1)}, f32[8,8,1024]{2,1,0:T(8,128)S(1)}, f32[8,8,1024]{2,1,0:T(8,128)S(1)}, f32[8,8,1024]{2,1,0:T(8,128)S(1)}) custom-call(s32[1]{0:T(128)} %bitcast.rank_ref.after_ref, f32[12,8,1024]{2,1,0:T(8,128)S(1)} %get-tuple-element.40.refs_12_.refs_0_, f32[12,8,1024]{2,1,0:T(8,128)S(1)} %collective-permute-done.3.refs_1_, ...), custom_call_target="tpu_custom_call" | custom-call | flops 10200547328 | bytes 4855812 | tf_op jit(solution)/shard_map/pallas_call | solution.py:77
  67.5 1.2 %collective-permute-start.13 = (f32[8,8,1024]{2,1,0:T(8,128)S(1)}, f32[8,8,1024]{2,1,0:T(8,128)S(1)}, u32[]{:S(2)}, u32[]{:S(2)}) collective-permute-start(f32[8,8,1024]{2,1,0:T(8,128)S(1)} %get-tuple-element.64), channel_id=1, source_target_pairs={{0,1},{1,0},{2,3},{3,2},{4,5},{5,4},{6,7},{7,6},{8,9},{9,8},{10,11... | collective-permute-start | bytes 786440 | tf_op jit(solution)/shard_map/ppermute | solution.py:358
  68.7 1.2 %collective-permute-start.14 = (f32[8,8,1024]{2,1,0:T(8,128)S(1)}, f32[8,8,1024]{2,1,0:T(8,128)S(1)}, u32[]{:S(2)}, u32[]{:S(2)}) collective-permute-start(f32[8,8,1024]{2,1,0:T(8,128)S(1)} %get-tuple-element.65), channel_id=1, source_target_pairs={{0,2},{1,3},{2,0},{3,1},{4,6},{5,7},{6,4},{7,5},{8,10},{9,11},{10,... | collective-permute-start | bytes 786440 | tf_op jit(solution)/shard_map/ppermute | solution.py:358
  70.2 1.2 %collective-permute-start.15 = (f32[8,8,1024]{2,1,0:T(8,128)S(1)}, f32[8,8,1024]{2,1,0:T(8,128)S(1)}, u32[]{:S(2)}, u32[]{:S(2)}) collective-permute-start(f32[8,8,1024]{2,1,0:T(8,128)S(1)} %get-tuple-element.66), channel_id=1, source_target_pairs={{0,3},{1,2},{2,1},{3,0},{4,7},{5,6},{6,5},{7,4},{8,11},{9,10},{10,... | collective-permute-start | bytes 786440 | tf_op jit(solution)/shard_map/ppermute | solution.py:358
  71.5 5.1 %collective-permute-done.13 = f32[8,8,1024]{2,1,0:T(8,128)S(1)} collective-permute-done((f32[8,8,1024]{2,1,0:T(8,128)S(1)}, f32[8,8,1024]{2,1,0:T(8,128)S(1)}, u32[]{:S(2)}, u32[]{:S(2)}) %collective-permute-start.13) | collective-permute-done | bytes 262176 | tf_op jit(solution)/shard_map/ppermute | solution.py:358
  76.6 5.0 %collective-permute-done.14 = f32[8,8,1024]{2,1,0:T(8,128)S(1)} collective-permute-done((f32[8,8,1024]{2,1,0:T(8,128)S(1)}, f32[8,8,1024]{2,1,0:T(8,128)S(1)}, u32[]{:S(2)}, u32[]{:S(2)}) %collective-permute-start.14) | collective-permute-done | bytes 262176 | tf_op jit(solution)/shard_map/ppermute | solution.py:358
  81.7 1.2 %collective-permute-done.15 = f32[8,8,1024]{2,1,0:T(8,128)S(1)} collective-permute-done((f32[8,8,1024]{2,1,0:T(8,128)S(1)}, f32[8,8,1024]{2,1,0:T(8,128)S(1)}, u32[]{:S(2)}, u32[]{:S(2)}) %collective-permute-start.15) | collective-permute-done | bytes 262176 | tf_op jit(solution)/shard_map/ppermute | solution.py:358
  83.0 0.7 constant_dynamic-update-slice_fusion
  (54 shorter events, 1.8 us)
Async XLA Ops:
  0.0 6.8 %copy-start = (f32[64,8,1024]{2,1,0:T(8,128)S(1)}, f32[64,8,1024]{2,1,0:T(8,128)}, u32[]{:S(2)}) copy-start(f32[64,8,1024]{2,1,0:T(8,128)} %cells_ref.5) | copy-start | bytes 6291460
  0.0 11.7 %copy-start.1 = (f32[7,256,256]{2,1,0:T(8,128)S(1)}, f32[7,256,256]{2,1,0:T(8,128)}, u32[]{:S(2)}) copy-start(f32[7,256,256]{2,1,0:T(8,128)} %constant.33.clone.table_ref) | copy-start | bytes 5505028
  0.0 11.7 %copy-start.4 = (f32[256,512]{1,0:T(8,128)S(1)}, f32[256,512]{1,0:T(8,128)}, u32[]{:S(2)}) copy-start(f32[256,512]{1,0:T(8,128)} %constant.32.clone.pick_ref) | copy-start | bytes 1572868
  1.5 13.8 %collective-permute-start = (f32[10,8,1024]{2,1,0:T(8,128)S(1)}, f32[10,8,1024]{2,1,0:T(8,128)S(1)}, u32[]{:S(2)}, u32[]{:S(2)}) collective-permute-start(f32[10,8,1024]{2,1,0:T(8,128)S(1)} %get-tuple-element.36), channel_id=1, source_target_pairs={{0,3},{1,2},{2,1},{3,0},{4,7},{5,6},{6,5},{7,4},{8,11},{9,10},{10,... | collective-permute-start | bytes 983048 | tf_op jit(solution)/shard_map/ppermute | solution.py:358
  5.4 15.0 %collective-permute-start.6 = (f32[10,8,1024]{2,1,0:T(8,128)S(1)}, f32[10,8,1024]{2,1,0:T(8,128)S(1)}, u32[]{:S(2)}, u32[]{:S(2)}) collective-permute-start(f32[10,8,1024]{2,1,0:T(8,128)S(1)} %get-tuple-element.45), channel_id=1, source_target_pairs={{0,1},{1,0},{2,3},{3,2},{4,5},{5,4},{6,7},{7,6},{8,9},{9,8},{10,11... | collective-permute-start | bytes 983048 | tf_op jit(solution)/shard_map/ppermute | solution.py:358
  6.0 14.5 %collective-permute-start.7 = (f32[10,8,1024]{2,1,0:T(8,128)S(1)}, f32[10,8,1024]{2,1,0:T(8,128)S(1)}, u32[]{:S(2)}, u32[]{:S(2)}) collective-permute-start(f32[10,8,1024]{2,1,0:T(8,128)S(1)} %get-tuple-element.46), channel_id=1, source_target_pairs={{0,2},{1,3},{2,0},{3,1},{4,6},{5,7},{6,4},{7,5},{8,10},{9,11},{10,... | collective-permute-start | bytes 983048 | tf_op jit(solution)/shard_map/ppermute | solution.py:358
  6.8 13.7 %copy-start.5 = (f32[16,8,256]{2,1,0:T(8,128)S(1)}, f32[16,8,256]{2,1,0:T(8,128)}, u32[]{:S(2)}) copy-start(f32[16,8,256]{2,1,0:T(8,128)} %constant.31.clone.refs_6_.refs_8_) | copy-start | bytes 393220
  8.4 16.6 %collective-permute-start.1 = (f32[64,1,640]{2,1,0:T(1,128)}, f32[64,1,640]{2,1,0:T(1,128)}, u32[]{:S(2)}, u32[]{:S(2)}) collective-permute-start(f32[64,1,640]{2,1,0:T(1,128)} %get-tuple-element.38), channel_id=1, source_target_pairs={{0,4},{4,8},{8,12},{12,16},{16,20},{20,24},{24,28},{1,5},{5,9},{9,... | collective-permute-start | bytes 491528 | tf_op jit(solution)/shard_map/ppermute | solution.py:381
  10.4 14.7 %collective-permute-start.2 = (f32[64,1,640]{2,1,0:T(1,128)}, f32[64,1,640]{2,1,0:T(1,128)}, u32[]{:S(2)}, u32[]{:S(2)}) collective-permute-start(f32[64,1,640]{2,1,0:T(1,128)} %get-tuple-element.39), channel_id=1, source_target_pairs={{4,0},{8,4},{12,8},{16,12},{20,16},{24,20},{28,24},{5,1},{9,5},{13... | collective-permute-start | bytes 491528 | tf_op jit(solution)/shard_map/ppermute | solution.py:382
  11.7 1.0 %copy-start.10 = (f32[16,4096]{1,0:T(8,128)S(1)}, f32[16,4096]{1,0:T(8,128)}, u32[]{:S(2)}) copy-start(f32[16,4096]{1,0:T(8,128)} %first_ref.1) | copy-start | bytes 786436
  12.7 0.9 %copy-start.11 = (f32[16,4096]{1,0:T(8,128)S(1)}, f32[16,4096]{1,0:T(8,128)}, u32[]{:S(2)}) copy-start(f32[16,4096]{1,0:T(8,128)} %second_ref.1) | copy-start | bytes 786436
  15.2 8.5 %copy-start.13 = (f32[16,48,128]{2,1,0:T(8,128)}, f32[16,48,128]{2,1,0:T(8,128)S(1)}, u32[]{:S(2)}) copy-start(f32[16,48,128]{2,1,0:T(8,128)S(1)} %get-tuple-element.50.refs_9_) | copy-start | bytes 1179652
  15.2 8.5 %copy-start.15 = (f32[16,48,128]{2,1,0:T(8,128)}, f32[16,48,128]{2,1,0:T(8,128)S(1)}, u32[]{:S(2)}) copy-start(f32[16,48,128]{2,1,0:T(8,128)S(1)} %get-tuple-element.51.refs_10_) | copy-start | bytes 1179652
  20.5 0.9 %copy-start.6 = (f32[10,8,1024]{2,1,0:T(8,128)}, f32[10,8,1024]{2,1,0:T(8,128)S(1)}, u32[]{:S(2)}) copy-start(f32[10,8,1024]{2,1,0:T(8,128)S(1)} %collective-permute-done.6.refs_1_) | copy-start | bytes 983044
  20.5 1.6 %copy-start.8 = (f32[10,8,1024]{2,1,0:T(8,128)}, f32[10,8,1024]{2,1,0:T(8,128)S(1)}, u32[]{:S(2)}) copy-start(f32[10,8,1024]{2,1,0:T(8,128)S(1)} %collective-permute-done.7.refs_2_) | copy-start | bytes 983044
  22.1 9.2 %collective-permute-start.8 = (f32[128,1,128]{2,1,0:T(1,128)}, f32[128,1,128]{2,1,0:T(1,128)S(1)}, u32[]{:S(2)}, u32[]{:S(2)}) collective-permute-start(f32[128,1,128]{2,1,0:T(1,128)} %get-tuple-element.47), channel_id=1, source_target_pairs={{0,4},{4,8},{8,12},{12,16},{16,20},{20,24},{24,28},{1,5},{5,9},{9,... | collective-permute-start | bytes 196616 | tf_op jit(solution)/shard_map/ppermute | solution.py:381
  23.7 7.5 %collective-permute-start.9 = (f32[128,1,128]{2,1,0:T(1,128)}, f32[128,1,128]{2,1,0:T(1,128)}, u32[]{:S(2)}, u32[]{:S(2)}) collective-permute-start(f32[128,1,128]{2,1,0:T(1,128)} %get-tuple-element.48), channel_id=1, source_target_pairs={{4,0},{8,4},{12,8},{16,12},{20,16},{24,20},{28,24},{5,1},{9,5},{13... | collective-permute-start | bytes 196616 | tf_op jit(solution)/shard_map/ppermute | solution.py:382
  25.1 1.0 %copy-start.3 = (f32[10,8,1024]{2,1,0:T(8,128)S(1)}, f32[10,8,1024]{2,1,0:T(8,128)}, u32[]{:S(2)}) copy-start(f32[10,8,1024]{2,1,0:T(8,128)} %copy-done.2) | copy-start | bytes 983044
  26.1 5.2 %copy-start.7 = (f32[10,8,1024]{2,1,0:T(8,128)S(1)}, f32[10,8,1024]{2,1,0:T(8,128)}, u32[]{:S(2)}) copy-start(f32[10,8,1024]{2,1,0:T(8,128)} %copy-done.6) | copy-start | bytes 983044
  26.1 5.2 %copy-start.9 = (f32[10,8,1024]{2,1,0:T(8,128)S(1)}, f32[10,8,1024]{2,1,0:T(8,128)}, u32[]{:S(2)}) copy-start(f32[10,8,1024]{2,1,0:T(8,128)} %copy-done.8) | copy-start | bytes 983044
  26.1 5.2 %copy-start.14 = (f32[16,48,128]{2,1,0:T(8,128)S(1)}, f32[16,48,128]{2,1,0:T(8,128)}, u32[]{:S(2)}) copy-start(f32[16,48,128]{2,1,0:T(8,128)} %copy-done.13) | copy-start | bytes 1179652
  26.1 5.2 %copy-start.16 = (f32[16,48,128]{2,1,0:T(8,128)S(1)}, f32[16,48,128]{2,1,0:T(8,128)}, u32[]{:S(2)}) copy-start(f32[16,48,128]{2,1,0:T(8,128)} %copy-done.15) | copy-start | bytes 1179652
  27.7 19.7 %collective-permute-start.3 = (f32[12,8,1024]{2,1,0:T(8,128)S(1)}, f32[12,8,1024]{2,1,0:T(8,128)S(1)}, u32[]{:S(2)}, u32[]{:S(2)}) collective-permute-start(f32[12,8,1024]{2,1,0:T(8,128)S(1)} %get-tuple-element.41), channel_id=1, source_target_pairs={{0,1},{1,0},{2,3},{3,2},{4,5},{5,4},{6,7},{7,6},{8,9},{9,8},{10,11... | collective-permute-start | bytes 1179656 | tf_op jit(solution)/shard_map/ppermute | solution.py:358
  29.5 18.2 %collective-permute-start.4 = (f32[12,8,1024]{2,1,0:T(8,128)S(1)}, f32[12,8,1024]{2,1,0:T(8,128)S(1)}, u32[]{:S(2)}, u32[]{:S(2)}) collective-permute-start(f32[12,8,1024]{2,1,0:T(8,128)S(1)} %get-tuple-element.42), channel_id=1, source_target_pairs={{0,2},{1,3},{2,0},{3,1},{4,6},{5,7},{6,4},{7,5},{8,10},{9,11},{10,... | collective-permute-start | bytes 1179656 | tf_op jit(solution)/shard_map/ppermute | solution.py:358
  31.0 17.1 %collective-permute-start.5 = (f32[12,8,1024]{2,1,0:T(8,128)S(1)}, f32[12,8,1024]{2,1,0:T(8,128)S(1)}, u32[]{:S(2)}, u32[]{:S(2)}) collective-permute-start(f32[12,8,1024]{2,1,0:T(8,128)S(1)} %get-tuple-element.43), channel_id=1, source_target_pairs={{0,3},{1,2},{2,1},{3,0},{4,7},{5,6},{6,5},{7,4},{8,11},{9,10},{10,... | collective-permute-start | bytes 1179656 | tf_op jit(solution)/shard_map/ppermute | solution.py:358
  48.3 21.9 %collective-permute-start.10 = (f32[8,8,1024]{2,1,0:T(8,128)S(1)}, f32[8,8,1024]{2,1,0:T(8,128)S(1)}, u32[]{:S(2)}, u32[]{:S(2)}) collective-permute-start(f32[8,8,1024]{2,1,0:T(8,128)S(1)} %get-tuple-element.57), channel_id=1, source_target_pairs={{0,1},{1,0},{2,3},{3,2},{4,5},{5,4},{6,7},{7,6},{8,9},{9,8},{10,11... | collective-permute-start | bytes 786440 | tf_op jit(solution)/shard_map/ppermute | solution.py:358
  49.8 21.7 %collective-permute-start.11 = (f32[8,8,1024]{2,1,0:T(8,128)S(1)}, f32[8,8,1024]{2,1,0:T(8,128)S(1)}, u32[]{:S(2)}, u32[]{:S(2)}) collective-permute-start(f32[8,8,1024]{2,1,0:T(8,128)S(1)} %get-tuple-element.58), channel_id=1, source_target_pairs={{0,2},{1,3},{2,0},{3,1},{4,6},{5,7},{6,4},{7,5},{8,10},{9,11},{10,... | collective-permute-start | bytes 786440 | tf_op jit(solution)/shard_map/ppermute | solution.py:358
  51.0 20.5 %collective-permute-start.12 = (f32[8,8,1024]{2,1,0:T(8,128)S(1)}, f32[8,8,1024]{2,1,0:T(8,128)S(1)}, u32[]{:S(2)}, u32[]{:S(2)}) collective-permute-start(f32[8,8,1024]{2,1,0:T(8,128)S(1)} %get-tuple-element.59), channel_id=1, source_target_pairs={{0,3},{1,2},{2,1},{3,0},{4,7},{5,6},{6,5},{7,4},{8,11},{9,10},{10,... | collective-permute-start | bytes 786440 | tf_op jit(solution)/shard_map/ppermute | solution.py:358
  67.5 9.2 %collective-permute-start.13 = (f32[8,8,1024]{2,1,0:T(8,128)S(1)}, f32[8,8,1024]{2,1,0:T(8,128)S(1)}, u32[]{:S(2)}, u32[]{:S(2)}) collective-permute-start(f32[8,8,1024]{2,1,0:T(8,128)S(1)} %get-tuple-element.64), channel_id=1, source_target_pairs={{0,1},{1,0},{2,3},{3,2},{4,5},{5,4},{6,7},{7,6},{8,9},{9,8},{10,11... | collective-permute-start | bytes 786440 | tf_op jit(solution)/shard_map/ppermute | solution.py:358
  68.7 12.9 %collective-permute-start.14 = (f32[8,8,1024]{2,1,0:T(8,128)S(1)}, f32[8,8,1024]{2,1,0:T(8,128)S(1)}, u32[]{:S(2)}, u32[]{:S(2)}) collective-permute-start(f32[8,8,1024]{2,1,0:T(8,128)S(1)} %get-tuple-element.65), channel_id=1, source_target_pairs={{0,2},{1,3},{2,0},{3,1},{4,6},{5,7},{6,4},{7,5},{8,10},{9,11},{10,... | collective-permute-start | bytes 786440 | tf_op jit(solution)/shard_map/ppermute | solution.py:358
  70.2 12.7 %collective-permute-start.15 = (f32[8,8,1024]{2,1,0:T(8,128)S(1)}, f32[8,8,1024]{2,1,0:T(8,128)S(1)}, u32[]{:S(2)}, u32[]{:S(2)}) collective-permute-start(f32[8,8,1024]{2,1,0:T(8,128)S(1)} %get-tuple-element.66), channel_id=1, source_target_pairs={{0,3},{1,2},{2,1},{3,0},{4,7},{5,6},{6,5},{7,4},{8,11},{9,10},{10,... | collective-permute-start | bytes 786440 | tf_op jit(solution)/shard_map/ppermute | solution.py:358
  81.6 1.3 %copy-start.17 = (f32[64,8,1024]{2,1,0:T(8,128)}, f32[64,8,1024]{2,1,0:T(8,128)S(1)}, u32[]{:S(2)}) copy-start(f32[64,8,1024]{2,1,0:T(8,128)S(1)} %constant_dynamic-update-slice_fusion.1) | copy-start | bytes 6291460
  (2 other events, 1.4 us)

commit v3 on v2

--- a/solution.py
+++ b/solution.py
@@ -72,7 +72,7 @@
     return jnp.dot(left, right, preferred_element_type=f32)
 
 
-def call(kernel, out_shape, operands, flops=0, scratch=(), limit=24, **options):
+def call(kernel, out_shape, operands, flops=0, scratch=(), limit=2, **options):
     moved = sum(a.size * a.dtype.itemsize for a in list(operands) + jax.tree.leaves(out_shape))
     return pl.pallas_call(
         kernel, out_shape=out_shape, scratch_shapes=list(scratch),
@@ -216,6 +216,12 @@
     before_ref, after_ref, density_ref, kind_ref, tables_ref, low_ref, top_ref, matrix_ref, _ = refs[:9]
     outs, refs = refs[9:9 + groups], refs[9 + groups:]
     moved_refs, spec_refs, gain_ref = refs[:2], refs[2:4], refs[4]
+    given, kept, sems = (matrix_ref, low_ref, top_ref), refs[5:8], refs[8]
+    copies = [pltpu.make_async_copy(value, into, sems.at[at]) for at, (value, into) in enumerate(zip(given, kept))]
+    matrix_ref, low_ref, top_ref = kept
+    for copy in copies:
+        copy.start()
+    copies[0].wait()
     rows = N * CELLS
     per = N // groups
     steps = outs[0].shape[0]
@@ -308,6 +314,8 @@
 
     for _ in prepare(0, moved_refs[0], spec_refs[0]):
         pass
+    copies[1].wait()
+    copies[2].wait()
 
     def two_rows(pair, _):
         one, other = 2 * pair, jnp.minimum(2 * pair + 1, steps - 1)
@@ -317,6 +325,19 @@
         return 0
 
     lax.fori_loop(0, (steps + 1) // 2, two_rows, 0)
+
+
+def place_body(groups, starts, rank_ref, *refs):
+    pieces, (out_ref, sems) = refs[:-2], refs[-2:]
+    own_rows = out_ref.shape[0] // groups
+    copies = []
+    for at, piece in enumerate(pieces):
+        top = lax.bitwise_xor(rank_ref[0], at % groups) * own_rows + starts[at // groups]
+        copies.append(pltpu.make_async_copy(piece, out_ref.at[pl.ds(top, piece.shape[0])], sems.at[at]))
+    for copy in copies:
+        copy.start()
+    for copy in copies:
+        copy.wait()
 
 
 def collide(rank, sources, before, after, density, kinds, tables, low, top, matrices, earlier, first_row, steps):
@@ -330,8 +351,9 @@
     spec = pltpu.VMEM((2 * N * CELLS, PLANE), f32)
     return call(
         functools.partial(collide_body, groups, dirs, 4, first_row), (shape,) * groups, (rank, *operands),
-        flops=steps * 2 * PLANE ** 3 * (2 * dirs + 6),
-        scratch=[cells, cells, spec, spec, pltpu.VMEM((N * CELLS, PLANE), f32)],
+        flops=steps * 2 * PLANE ** 3 * (2 * dirs + 6), limit=6,
+        scratch=[cells, cells, spec, spec, pltpu.VMEM((N * CELLS, PLANE), f32)]
+        + [pltpu.VMEM(value.shape, value.dtype) for value in (matrices, low, top)] + [pltpu.SemaphoreType.DMA((3,))],
         in_specs=[pl.BlockSpec(memory_space=pltpu.SMEM)] + [vmem] * (len(operands) - 1) + [pl.BlockSpec(memory_space=pl.ANY)],
         out_specs=(vmem,) * groups,
     )
@@ -360,11 +382,10 @@
 
     def cut(first_row, count, earlier, *columns):
         block = jax.ShapeDtypeStruct((count + 2 + len(columns), cols, width), f32)
-        place = vmem
         return call(
             functools.partial(cut_body, groups, first_row), (block,) * groups, (rank_word, distribution, earlier, *columns),
-            in_specs=[smem, anywhere, anywhere] + [vmem] * len(columns), out_specs=(place,) * groups,
-            scratch=[pltpu.SemaphoreType.DMA((groups,))], limit=24 if columns else 52)
+            in_specs=[smem, anywhere, anywhere] + [vmem] * len(columns), out_specs=(vmem,) * groups,
+            scratch=[pltpu.SemaphoreType.DMA((groups,))])
 
     def rims(first_row, count, sources, *passing):
         edge = jax.ShapeDtypeStruct((count * N, 1, TILE), f32)
@@ -382,7 +403,8 @@
                 lax.ppermute(first, "cell", [(i + 1, i) for i in range(spots - 1)]))
 
     (first_row, count), (next_row, next_count) = chunks
-    cuts = cut(first_row, count, rank_word)
+    cuts = [lax.dynamic_slice_in_dim(distribution, window(rank ^ flip, own_rows, rows, first_row, count), count + 2, 0)
+            for flip in range(groups)]
     sources = swap(cuts)
     low, top, matrices = setup(first_kernel, second_kernel, loss_kernel)
     column = jax.ShapeDtypeStruct((rows, 1, width // 2 + TILE), f32)
@@ -390,18 +412,17 @@
         columns_body, (column, column), (distribution, kinds, cuts[0]), in_specs=[vmem, vmem, anywhere], out_specs=(vmem,) * 2))
     first, last, density = rims(first_row, count, sources)
     edges = to_neighbours(first, last)
-    following = cut(next_row, next_count, sources[-1], *columns)
+    following = cut(next_row, next_count, density, *columns)
     done = collide(rank_word, sources, *edges, density, kinds, tables, low, top, matrices, following[0], first_row, count)
     sources = swap(following)
     after, before, density, *done = rims(next_row, next_count, sources, *done)
     home = swap(done)
     done = collide(rank_word, sources, before, after, density, kinds, tables, low, top, matrices, done[0], next_row, next_count)
-    home = [home, swap(done)]
-    updated = jnp.zeros((rows, cols, width), f32)
-    for (first_row, count), blocks in zip(chunks, home):
-        for flip, block in enumerate(blocks):
-            updated = lax.dynamic_update_slice_in_dim(updated, block, (rank ^ flip) * own_rows + first_row, 0)
-    return updated
+    pieces = (*home, *swap(done))
+    return call(
+        functools.partial(place_body, groups, (first_row, next_row)), jax.ShapeDtypeStruct(distribution.shape, f32),
+        (rank_word, *pieces), in_specs=[smem] + [vmem] * len(pieces), out_specs=anywhere,
+        scratch=[pltpu.SemaphoreType.DMA((len(pieces),))])
 
 
 def solution(mesh):

time: 84.3 us -> 78.8 us (0.935)
  waiting for transfers between devices: 17.1 us -> 23.3 us
  Pallas kernels: 38.2 us -> 33.2 us
  local copies, waits for them, and re-layouts: 5.56 us -> 1.58 us
  starting transfers between devices: 21.7 us -> 20.4 us
    ppermute x12, waiting for transfers between devices: 17.1 us -> 23.3 us  [swap(): lax.ppermute(values[flip], 'vel', [(i, i ^ flip) for i in range(groups)])]
    pallas_call x8, Pallas kernels: 38.2 us -> 33.2 us  [call(): pl.pallas_call(kernel, out_shape=out_shape, scratch_shapes=list(scratch),...]
    unnamed x36 -> x16, local copies, waits for them, and re-layouts: 4.44 us -> 0.03 us
    dynamic_slice x0 -> x1, local copies, waits for them, and re-layouts: none -> 1.55 us  [on_device(): lax.dynamic_slice_in_dim(distribution, window(rank ^ flip, own_rows, rows...]
    ppermute x2, starting transfers between devices: 3.56 us -> 2.59 us  [to_neighbours(): lax.ppermute(last, 'cell', [(i, i + 1) for i in range(spots - 1)])]
    dynamic_update_slice x8 -> x0, local copies, waits for them, and re-layouts: 0.88 us -> none  [on_device(): lax.dynamic_update_slice_in_dim(updated, block, (rank ^ flip) * own_rows...]
  transfers between devices with their start and end apart: 16 -> 16, of which waited for: 6 -> 5; matrix products, arithmetic and copies ran while one was open for 1% -> 0% of each run, Pallas kernels for 44% -> 40%
where the time goes in v3:
time: 78.8 us; the launch traced here: 78.7 us
  Pallas kernels  33.2 us (42%)
  waiting for transfers between devices  23.3 us (30%)
  starting transfers between devices  20.4 us (26%)
  local copies, waits for them, and re-layouts  1.58 us (2%)
    pallas_call x8, Pallas kernels, call(): pl.pallas_call(kernel, out_shape=out_shape, scratch_shapes=list(scratch),...  33.2 us
    ppermute x12, waiting for transfers between devices, swap(): lax.ppermute(values[flip], 'vel', [(i, i ^ flip) for i in range(groups)])  23.3 us
    ppermute x12, starting transfers between devices, swap(): lax.ppermute(values[flip], 'vel', [(i, i ^ flip) for i in range(groups)])  15.2 us
    ppermute x2, starting transfers between devices, to_neighbours(): lax.ppermute(last, 'cell', [(i, i + 1) for i in range(spots - 1)])  2.59 us
    ppermute x2, starting transfers between devices, to_neighbours(): lax.ppermute(first, 'cell', [(i + 1, i) for i in range(spots - 1)])  2.58 us
  transfers between devices with their start and end apart: 16, of which 5 were waited for; matrix products, arithmetic and copies ran while one was open for 0% of the time, Pallas kernels for 40%

profile of v3, /device:TPU:0, one launch (start us, length us, event | category | flops | bytes accessed | tf_op | source)
XLA Modules:
  0.0 78.7 jit_solution(8925385793427264690)
XLA Ops:
  0.0 1.6 %constant_dynamic-slice_fusion = (f32[10,8,1024]{2,1,0:T(8,128)S(1)}, f32[10,8,1024]{2,1,0:T(8,128)S(1)}, f32[10,8,1024]{2,1,0:T(8,128)S(1)}, f32[10,8,1024]{2,1,0:T(8,128)S(1)}) fusion(f32[64,8,1024]{2,1,0:T(8,128)} %cells_ref.3, s32[]{:T(128)S(6)} %min.16, s32[]{:T(128)S(6)} %min.15, s32[]{:T(128)S(6)} %min.14, s32[]{:T(128)S(6)} %min.13), kind=kLoop, calls=%fused_computation.1 | loop fusion | bytes 2621456 | tf_op jit(solution)/shard_map/dynamic_slice | solution.py:406
  1.6 3.0 %collective-permute-start = (f32[10,8,1024]{2,1,0:T(8,128)S(1)}, f32[10,8,1024]{2,1,0:T(8,128)S(1)}, u32[]{:S(2)}, u32[]{:S(2)}) collective-permute-start(f32[10,8,1024]{2,1,0:T(8,128)S(1)} %get-tuple-element.61), channel_id=1, source_target_pairs={{0,1},{1,0},{2,3},{3,2},{4,5},{5,4},{6,7},{7,6},{8,9},{9,8},{10,11... | collective-permute-start | bytes 983048 | tf_op jit(solution)/shard_map/ppermute | solution.py:380
  4.6 1.5 %collective-permute-start.1 = (f32[10,8,1024]{2,1,0:T(8,128)S(1)}, f32[10,8,1024]{2,1,0:T(8,128)S(1)}, u32[]{:S(2)}, u32[]{:S(2)}) collective-permute-start(f32[10,8,1024]{2,1,0:T(8,128)S(1)} %get-tuple-element.60), channel_id=1, source_target_pairs={{0,2},{1,3},{2,0},{3,1},{4,6},{5,7},{6,4},{7,5},{8,10},{9,11},{10,... | collective-permute-start | bytes 983048 | tf_op jit(solution)/shard_map/ppermute | solution.py:380
  6.1 0.0 collective-permute-start.2
  6.2 1.0 %shard_map.84 = (f32[64,1,640]{2,1,0:T(1,128)S(1)}, f32[64,1,640]{2,1,0:T(1,128)S(1)}) custom-call(f32[64,8,1024]{2,1,0:T(8,128)S(1)} %copy-done, f32[8,64]{1,0:T(8,128)S(1)} %convert_bitcast_fusion.refs_5_.kind_ref.refs_7_, f32[10,8,1024]{2,1,0:T(8,128)S(1)} %get-tuple-element.62.refs_0_.after_ref), custom_call_target="tpu_custom_call" | custom-call | bytes 2754560 | tf_op jit(solution)/shard_map/pallas_call | solution.py:77
  7.1 1.3 %collective-permute-start.3 = (f32[64,1,640]{2,1,0:T(1,128)S(1)}, f32[64,1,640]{2,1,0:T(1,128)S(1)}, u32[]{:S(2)}, u32[]{:S(2)}) collective-permute-start(f32[64,1,640]{2,1,0:T(1,128)S(1)} %get-tuple-element.34), channel_id=1, source_target_pairs={{0,4},{4,8},{8,12},{12,16},{16,20},{20,24},{24,28},{1,5},{5,9},{9,... | collective-permute-start | bytes 491528 | tf_op jit(solution)/shard_map/ppermute | solution.py:402
  8.4 1.3 %collective-permute-start.4 = (f32[64,1,640]{2,1,0:T(1,128)S(1)}, f32[64,1,640]{2,1,0:T(1,128)S(1)}, u32[]{:S(2)}, u32[]{:S(2)}) collective-permute-start(f32[64,1,640]{2,1,0:T(1,128)S(1)} %get-tuple-element.35), channel_id=1, source_target_pairs={{4,0},{8,4},{12,8},{16,12},{20,16},{24,20},{28,24},{5,1},{9,5},{13... | collective-permute-start | bytes 491528 | tf_op jit(solution)/shard_map/ppermute | solution.py:403
  9.8 0.9 %shard_map.82 = (f32[16,48,128]{2,1,0:T(8,128)S(1)}, f32[16,48,128]{2,1,0:T(8,128)S(1)}, bf16[7,256,256]{2,1,0:T(8,128)(2,1)S(1)}) custom-call(f32[16,4096]{1,0:T(8,128)S(1)} %copy-done.4, f32[16,4096]{1,0:T(8,128)S(1)} %copy-done.5, f32[1,4096]{1,0:T(1,128)S(1)} %bitcast.4, f32[256,512]{1,0:T(8,128)S(1)} %copy-done.2, f32[7,256,256]{2,1,0:T(8,128)S(1)} %copy-done.1), custom_call_target="tpu_custom_call" | custom-call | flops 603979776 | bytes 4603904 | tf_op jit(solution)/shard_map/pallas_call | solution.py:77
  10.7 2.5 %collective-permute-done.refs_1_ = f32[10,8,1024]{2,1,0:T(8,128)S(1)} collective-permute-done((f32[10,8,1024]{2,1,0:T(8,128)S(1)}, f32[10,8,1024]{2,1,0:T(8,128)S(1)}, u32[]{:S(2)}, u32[]{:S(2)}) %collective-permute-start) | collective-permute-done | bytes 327712 | tf_op jit(solution)/shard_map/ppermute | solution.py:380
  13.2 7.7 %collective-permute-done.1.refs_2_ = f32[10,8,1024]{2,1,0:T(8,128)S(1)} collective-permute-done((f32[10,8,1024]{2,1,0:T(8,128)S(1)}, f32[10,8,1024]{2,1,0:T(8,128)S(1)}, u32[]{:S(2)}, u32[]{:S(2)}) %collective-permute-start.1) | collective-permute-done | bytes 327712 | tf_op jit(solution)/shard_map/ppermute | solution.py:380
  20.8 0.0 collective-permute-done.2.refs_3_
  20.8 0.3 shard_map.83
  21.1 1.3 %collective-permute-start.8 = (f32[128,1,128]{2,1,0:T(1,128)S(1)}, f32[128,1,128]{2,1,0:T(1,128)S(1)}, u32[]{:S(2)}, u32[]{:S(2)}) collective-permute-start(f32[128,1,128]{2,1,0:T(1,128)S(1)} %get-tuple-element.40), channel_id=1, source_target_pairs={{0,4},{4,8},{8,12},{12,16},{16,20},{20,24},{24,28},{1,5},{5,9},{9,... | collective-permute-start | bytes 196616 | tf_op jit(solution)/shard_map/ppermute | solution.py:402
  22.4 1.3 %collective-permute-start.9 = (f32[128,1,128]{2,1,0:T(1,128)S(1)}, f32[128,1,128]{2,1,0:T(1,128)S(1)}, u32[]{:S(2)}, u32[]{:S(2)}) collective-permute-start(f32[128,1,128]{2,1,0:T(1,128)S(1)} %get-tuple-element.41), channel_id=1, source_target_pairs={{4,0},{8,4},{12,8},{16,12},{20,16},{24,20},{28,24},{5,1},{9,5},{13... | collective-permute-start | bytes 196616 | tf_op jit(solution)/shard_map/ppermute | solution.py:403
  23.7 0.0 collective-permute-done.3.refs_0_
  23.7 0.5 shard_map.85
  24.2 1.3 %collective-permute-start.5 = (f32[12,8,1024]{2,1,0:T(8,128)S(1)}, f32[12,8,1024]{2,1,0:T(8,128)S(1)}, u32[]{:S(2)}, u32[]{:S(2)}) collective-permute-start(f32[12,8,1024]{2,1,0:T(8,128)S(1)} %get-tuple-element.37), channel_id=1, source_target_pairs={{0,1},{1,0},{2,3},{3,2},{4,5},{5,4},{6,7},{7,6},{8,9},{9,8},{10,11... | collective-permute-start | bytes 1179656 | tf_op jit(solution)/shard_map/ppermute | solution.py:380
  25.5 0.8 %collective-permute-start.6 = (f32[12,8,1024]{2,1,0:T(8,128)S(1)}, f32[12,8,1024]{2,1,0:T(8,128)S(1)}, u32[]{:S(2)}, u32[]{:S(2)}) collective-permute-start(f32[12,8,1024]{2,1,0:T(8,128)S(1)} %get-tuple-element.38), channel_id=1, source_target_pairs={{0,2},{1,3},{2,0},{3,1},{4,6},{5,7},{6,4},{7,5},{8,10},{9,11},{10,... | collective-permute-start | bytes 1179656 | tf_op jit(solution)/shard_map/ppermute | solution.py:380
  26.3 1.4 %collective-permute-start.7 = (f32[12,8,1024]{2,1,0:T(8,128)S(1)}, f32[12,8,1024]{2,1,0:T(8,128)S(1)}, u32[]{:S(2)}, u32[]{:S(2)}) collective-permute-start(f32[12,8,1024]{2,1,0:T(8,128)S(1)} %get-tuple-element.39), channel_id=1, source_target_pairs={{0,3},{1,2},{2,1},{3,0},{4,7},{5,6},{6,5},{7,4},{8,11},{9,10},{10,... | collective-permute-start | bytes 1179656 | tf_op jit(solution)/shard_map/ppermute | solution.py:380
  27.8 14.4 %shard_map.86 = (f32[8,8,1024]{2,1,0:T(8,128)S(1)}, f32[8,8,1024]{2,1,0:T(8,128)S(1)}, f32[8,8,1024]{2,1,0:T(8,128)S(1)}, f32[8,8,1024]{2,1,0:T(8,128)S(1)}) custom-call(s32[1]{0:T(128)} %bitcast.rank_ref, f32[10,8,1024]{2,1,0:T(8,128)S(1)} %get-tuple-element.62.refs_0_.after_ref, f32[10,8,1024]{2,1,0:T(8,128)S(1)} %collective-permute-done.refs_1_, ...), custom_call_target="tpu_custom_call" | custom-call | flops 10200547328 | bytes 4724740 | tf_op jit(solution)/shard_map/pallas_call | solution.py:77
  42.3 1.5 %collective-permute-done.7.refs_3_ = f32[12,8,1024]{2,1,0:T(8,128)S(1)} collective-permute-done((f32[12,8,1024]{2,1,0:T(8,128)S(1)}, f32[12,8,1024]{2,1,0:T(8,128)S(1)}, u32[]{:S(2)}, u32[]{:S(2)}) %collective-permute-start.7) | collective-permute-done | bytes 393248 | tf_op jit(solution)/shard_map/ppermute | solution.py:380
  43.7 0.3 shard_map.87
  44.0 0.6 collective-permute-start.10
  44.6 1.2 %collective-permute-start.11 = (f32[8,8,1024]{2,1,0:T(8,128)S(1)}, f32[8,8,1024]{2,1,0:T(8,128)S(1)}, u32[]{:S(2)}, u32[]{:S(2)}) collective-permute-start(f32[8,8,1024]{2,1,0:T(8,128)S(1)} %get-tuple-element.50), channel_id=1, source_target_pairs={{0,2},{1,3},{2,0},{3,1},{4,6},{5,7},{6,4},{7,5},{8,10},{9,11},{10,... | collective-permute-start | bytes 786440 | tf_op jit(solution)/shard_map/ppermute | solution.py:380
  45.8 1.8 %collective-permute-start.12 = (f32[8,8,1024]{2,1,0:T(8,128)S(1)}, f32[8,8,1024]{2,1,0:T(8,128)S(1)}, u32[]{:S(2)}, u32[]{:S(2)}) collective-permute-start(f32[8,8,1024]{2,1,0:T(8,128)S(1)} %get-tuple-element.51), channel_id=1, source_target_pairs={{0,3},{1,2},{2,1},{3,0},{4,7},{5,6},{6,5},{7,4},{8,11},{9,10},{10,... | collective-permute-start | bytes 786440 | tf_op jit(solution)/shard_map/ppermute | solution.py:380
  47.6 14.5 %shard_map.88 = (f32[8,8,1024]{2,1,0:T(8,128)S(1)}, f32[8,8,1024]{2,1,0:T(8,128)S(1)}, f32[8,8,1024]{2,1,0:T(8,128)S(1)}, f32[8,8,1024]{2,1,0:T(8,128)S(1)}) custom-call(s32[1]{0:T(128)} %bitcast.rank_ref, f32[12,8,1024]{2,1,0:T(8,128)S(1)} %get-tuple-element.36.refs_12_.refs_0_, f32[12,8,1024]{2,1,0:T(8,128)S(1)} %collective-permute-done.5.refs_1_, ...), custom_call_target="tpu_custom_call" | custom-call | flops 10200547328 | bytes 4855812 | tf_op jit(solution)/shard_map/pallas_call | solution.py:77
  62.1 0.6 collective-permute-start.13
  62.7 1.2 %collective-permute-start.14 = (f32[8,8,1024]{2,1,0:T(8,128)S(1)}, f32[8,8,1024]{2,1,0:T(8,128)S(1)}, u32[]{:S(2)}, u32[]{:S(2)}) collective-permute-start(f32[8,8,1024]{2,1,0:T(8,128)S(1)} %get-tuple-element.57), channel_id=1, source_target_pairs={{0,2},{1,3},{2,0},{3,1},{4,6},{5,7},{6,4},{7,5},{8,10},{9,11},{10,... | collective-permute-start | bytes 786440 | tf_op jit(solution)/shard_map/ppermute | solution.py:380
  63.9 1.8 %collective-permute-start.15 = (f32[8,8,1024]{2,1,0:T(8,128)S(1)}, f32[8,8,1024]{2,1,0:T(8,128)S(1)}, u32[]{:S(2)}, u32[]{:S(2)}) collective-permute-start(f32[8,8,1024]{2,1,0:T(8,128)S(1)} %get-tuple-element.58), channel_id=1, source_target_pairs={{0,3},{1,2},{2,1},{3,0},{4,7},{5,6},{6,5},{7,4},{8,11},{9,10},{10,... | collective-permute-start | bytes 786440 | tf_op jit(solution)/shard_map/ppermute | solution.py:380
  65.7 5.5 %collective-permute-done.13.refs_5_ = f32[8,8,1024]{2,1,0:T(8,128)S(1)} collective-permute-done((f32[8,8,1024]{2,1,0:T(8,128)S(1)}, f32[8,8,1024]{2,1,0:T(8,128)S(1)}, u32[]{:S(2)}, u32[]{:S(2)}) %collective-permute-start.13) | collective-permute-done | bytes 262176 | tf_op jit(solution)/shard_map/ppermute | solution.py:380
  71.1 6.2 %collective-permute-done.14.refs_6_ = f32[8,8,1024]{2,1,0:T(8,128)S(1)} collective-permute-done((f32[8,8,1024]{2,1,0:T(8,128)S(1)}, f32[8,8,1024]{2,1,0:T(8,128)S(1)}, u32[]{:S(2)}, u32[]{:S(2)}) %collective-permute-start.14) | collective-permute-done | bytes 262176 | tf_op jit(solution)/shard_map/ppermute | solution.py:380
  77.3 1.4 %shard_map.89 = f32[64,8,1024]{2,1,0:T(8,128)} custom-call(s32[1]{0:T(128)} %bitcast.rank_ref, f32[8,8,1024]{2,1,0:T(8,128)S(1)} %get-tuple-element.48.refs_12_.refs_0_, f32[8,8,1024]{2,1,0:T(8,128)S(1)} %collective-permute-done.10.refs_1_, f32[8,8,1024]{2,1,0:T(8,128)S(1)} %collective-permute-done.11.refs_2_, ...), custom_call_target="tpu_custom_call" | custom-call | bytes 4194308 | tf_op jit(solution)/shard_map/pallas_call | solution.py:77
  (26 shorter events, 0.1 us)
Async XLA Ops:
  0.0 6.2 %copy-start = (f32[64,8,1024]{2,1,0:T(8,128)S(1)}, f32[64,8,1024]{2,1,0:T(8,128)}, u32[]{:S(2)}) copy-start(f32[64,8,1024]{2,1,0:T(8,128)} %cells_ref.3) | copy-start | bytes 6291460
  0.0 6.2 %copy-start.7 = (s32[64,8]{0,1:T(8,128)S(1)}, s32[64,8]{0,1:T(8,128)}, u32[]{:S(2)}) copy-start(s32[64,8]{0,1:T(8,128)} %param.9) | copy-start | bytes 6148
  0.0 9.7 %copy-start.1 = (f32[7,256,256]{2,1,0:T(8,128)S(1)}, f32[7,256,256]{2,1,0:T(8,128)}, u32[]{:S(2)}) copy-start(f32[7,256,256]{2,1,0:T(8,128)} %constant.34.clone.table_ref) | copy-start | bytes 5505028
  0.0 9.7 %copy-start.2 = (f32[256,512]{1,0:T(8,128)S(1)}, f32[256,512]{1,0:T(8,128)}, u32[]{:S(2)}) copy-start(f32[256,512]{1,0:T(8,128)} %constant.33.clone.pick_ref) | copy-start | bytes 1572868
  0.0 9.7 %copy-start.4 = (f32[16,4096]{1,0:T(8,128)S(1)}, f32[16,4096]{1,0:T(8,128)}, u32[]{:S(2)}) copy-start(f32[16,4096]{1,0:T(8,128)} %first_ref.1) | copy-start | bytes 786436
  0.0 9.8 %copy-start.5 = (f32[16,4096]{1,0:T(8,128)S(1)}, f32[16,4096]{1,0:T(8,128)}, u32[]{:S(2)}) copy-start(f32[16,4096]{1,0:T(8,128)} %second_ref.1) | copy-start | bytes 786436
  0.0 9.8 %copy-start.6 = (f32[4096]{0:T(1024)S(1)}, f32[4096]{0:T(1024)}, u32[]{:S(2)}) copy-start(f32[4096]{0:T(1024)} %param.12) | copy-start | bytes 49156
  1.6 11.6 %collective-permute-start = (f32[10,8,1024]{2,1,0:T(8,128)S(1)}, f32[10,8,1024]{2,1,0:T(8,128)S(1)}, u32[]{:S(2)}, u32[]{:S(2)}) collective-permute-start(f32[10,8,1024]{2,1,0:T(8,128)S(1)} %get-tuple-element.61), channel_id=1, source_target_pairs={{0,1},{1,0},{2,3},{3,2},{4,5},{5,4},{6,7},{7,6},{8,9},{9,8},{10,11... | collective-permute-start | bytes 983048 | tf_op jit(solution)/shard_map/ppermute | solution.py:380
  4.6 16.2 %collective-permute-start.1 = (f32[10,8,1024]{2,1,0:T(8,128)S(1)}, f32[10,8,1024]{2,1,0:T(8,128)S(1)}, u32[]{:S(2)}, u32[]{:S(2)}) collective-permute-start(f32[10,8,1024]{2,1,0:T(8,128)S(1)} %get-tuple-element.60), channel_id=1, source_target_pairs={{0,2},{1,3},{2,0},{3,1},{4,6},{5,7},{6,4},{7,5},{8,10},{9,11},{10,... | collective-permute-start | bytes 983048 | tf_op jit(solution)/shard_map/ppermute | solution.py:380
  6.1 14.7 %collective-permute-start.2 = (f32[10,8,1024]{2,1,0:T(8,128)S(1)}, f32[10,8,1024]{2,1,0:T(8,128)S(1)}, u32[]{:S(2)}, u32[]{:S(2)}) collective-permute-start(f32[10,8,1024]{2,1,0:T(8,128)S(1)} %get-tuple-element.59), channel_id=1, source_target_pairs={{0,3},{1,2},{2,1},{3,0},{4,7},{5,6},{6,5},{7,4},{8,11},{9,10},{10,... | collective-permute-start | bytes 983048 | tf_op jit(solution)/shard_map/ppermute | solution.py:380
  6.2 14.6 %copy-start.3 = (f32[16,8,256]{2,1,0:T(8,128)S(1)}, f32[16,8,256]{2,1,0:T(8,128)}, u32[]{:S(2)}) copy-start(f32[16,8,256]{2,1,0:T(8,128)} %constant.32.clone.refs_6_.refs_8_) | copy-start | bytes 393220
  7.1 16.5 %collective-permute-start.3 = (f32[64,1,640]{2,1,0:T(1,128)S(1)}, f32[64,1,640]{2,1,0:T(1,128)S(1)}, u32[]{:S(2)}, u32[]{:S(2)}) collective-permute-start(f32[64,1,640]{2,1,0:T(1,128)S(1)} %get-tuple-element.34), channel_id=1, source_target_pairs={{0,4},{4,8},{8,12},{12,16},{16,20},{20,24},{24,28},{1,5},{5,9},{9,... | collective-permute-start | bytes 491528 | tf_op jit(solution)/shard_map/ppermute | solution.py:402
  8.4 15.3 %collective-permute-start.4 = (f32[64,1,640]{2,1,0:T(1,128)S(1)}, f32[64,1,640]{2,1,0:T(1,128)S(1)}, u32[]{:S(2)}, u32[]{:S(2)}) collective-permute-start(f32[64,1,640]{2,1,0:T(1,128)S(1)} %get-tuple-element.35), channel_id=1, source_target_pairs={{4,0},{8,4},{12,8},{16,12},{20,16},{24,20},{28,24},{5,1},{9,5},{13... | collective-permute-start | bytes 491528 | tf_op jit(solution)/shard_map/ppermute | solution.py:403
  21.1 6.7 %collective-permute-start.8 = (f32[128,1,128]{2,1,0:T(1,128)S(1)}, f32[128,1,128]{2,1,0:T(1,128)S(1)}, u32[]{:S(2)}, u32[]{:S(2)}) collective-permute-start(f32[128,1,128]{2,1,0:T(1,128)S(1)} %get-tuple-element.40), channel_id=1, source_target_pairs={{0,4},{4,8},{8,12},{12,16},{16,20},{20,24},{24,28},{1,5},{5,9},{9,... | collective-permute-start | bytes 196616 | tf_op jit(solution)/shard_map/ppermute | solution.py:402
  22.4 5.4 %collective-permute-start.9 = (f32[128,1,128]{2,1,0:T(1,128)S(1)}, f32[128,1,128]{2,1,0:T(1,128)S(1)}, u32[]{:S(2)}, u32[]{:S(2)}) collective-permute-start(f32[128,1,128]{2,1,0:T(1,128)S(1)} %get-tuple-element.41), channel_id=1, source_target_pairs={{4,0},{8,4},{12,8},{16,12},{20,16},{24,20},{28,24},{5,1},{9,5},{13... | collective-permute-start | bytes 196616 | tf_op jit(solution)/shard_map/ppermute | solution.py:403
  24.2 18.0 %collective-permute-start.5 = (f32[12,8,1024]{2,1,0:T(8,128)S(1)}, f32[12,8,1024]{2,1,0:T(8,128)S(1)}, u32[]{:S(2)}, u32[]{:S(2)}) collective-permute-start(f32[12,8,1024]{2,1,0:T(8,128)S(1)} %get-tuple-element.37), channel_id=1, source_target_pairs={{0,1},{1,0},{2,3},{3,2},{4,5},{5,4},{6,7},{7,6},{8,9},{9,8},{10,11... | collective-permute-start | bytes 1179656 | tf_op jit(solution)/shard_map/ppermute | solution.py:380
  25.5 16.7 %collective-permute-start.6 = (f32[12,8,1024]{2,1,0:T(8,128)S(1)}, f32[12,8,1024]{2,1,0:T(8,128)S(1)}, u32[]{:S(2)}, u32[]{:S(2)}) collective-permute-start(f32[12,8,1024]{2,1,0:T(8,128)S(1)} %get-tuple-element.38), channel_id=1, source_target_pairs={{0,2},{1,3},{2,0},{3,1},{4,6},{5,7},{6,4},{7,5},{8,10},{9,11},{10,... | collective-permute-start | bytes 1179656 | tf_op jit(solution)/shard_map/ppermute | solution.py:380
  26.3 17.4 %collective-permute-start.7 = (f32[12,8,1024]{2,1,0:T(8,128)S(1)}, f32[12,8,1024]{2,1,0:T(8,128)S(1)}, u32[]{:S(2)}, u32[]{:S(2)}) collective-permute-start(f32[12,8,1024]{2,1,0:T(8,128)S(1)} %get-tuple-element.39), channel_id=1, source_target_pairs={{0,3},{1,2},{2,1},{3,0},{4,7},{5,6},{6,5},{7,4},{8,11},{9,10},{10,... | collective-permute-start | bytes 1179656 | tf_op jit(solution)/shard_map/ppermute | solution.py:380
  44.0 19.9 %collective-permute-start.10 = (f32[8,8,1024]{2,1,0:T(8,128)S(1)}, f32[8,8,1024]{2,1,0:T(8,128)S(1)}, u32[]{:S(2)}, u32[]{:S(2)}) collective-permute-start(f32[8,8,1024]{2,1,0:T(8,128)S(1)} %get-tuple-element.49), channel_id=1, source_target_pairs={{0,1},{1,0},{2,3},{3,2},{4,5},{5,4},{6,7},{7,6},{8,9},{9,8},{10,11... | collective-permute-start | bytes 786440 | tf_op jit(solution)/shard_map/ppermute | solution.py:380
  44.6 21.1 %collective-permute-start.11 = (f32[8,8,1024]{2,1,0:T(8,128)S(1)}, f32[8,8,1024]{2,1,0:T(8,128)S(1)}, u32[]{:S(2)}, u32[]{:S(2)}) collective-permute-start(f32[8,8,1024]{2,1,0:T(8,128)S(1)} %get-tuple-element.50), channel_id=1, source_target_pairs={{0,2},{1,3},{2,0},{3,1},{4,6},{5,7},{6,4},{7,5},{8,10},{9,11},{10,... | collective-permute-start | bytes 786440 | tf_op jit(solution)/shard_map/ppermute | solution.py:380
  45.8 19.9 %collective-permute-start.12 = (f32[8,8,1024]{2,1,0:T(8,128)S(1)}, f32[8,8,1024]{2,1,0:T(8,128)S(1)}, u32[]{:S(2)}, u32[]{:S(2)}) collective-permute-start(f32[8,8,1024]{2,1,0:T(8,128)S(1)} %get-tuple-element.51), channel_id=1, source_target_pairs={{0,3},{1,2},{2,1},{3,0},{4,7},{5,6},{6,5},{7,4},{8,11},{9,10},{10,... | collective-permute-start | bytes 786440 | tf_op jit(solution)/shard_map/ppermute | solution.py:380
  62.1 9.0 %collective-permute-start.13 = (f32[8,8,1024]{2,1,0:T(8,128)S(1)}, f32[8,8,1024]{2,1,0:T(8,128)S(1)}, u32[]{:S(2)}, u32[]{:S(2)}) collective-permute-start(f32[8,8,1024]{2,1,0:T(8,128)S(1)} %get-tuple-element.56), channel_id=1, source_target_pairs={{0,1},{1,0},{2,3},{3,2},{4,5},{5,4},{6,7},{7,6},{8,9},{9,8},{10,11... | collective-permute-start | bytes 786440 | tf_op jit(solution)/shard_map/ppermute | solution.py:380
  62.7 14.6 %collective-permute-start.14 = (f32[8,8,1024]{2,1,0:T(8,128)S(1)}, f32[8,8,1024]{2,1,0:T(8,128)S(1)}, u32[]{:S(2)}, u32[]{:S(2)}) collective-permute-start(f32[8,8,1024]{2,1,0:T(8,128)S(1)} %get-tuple-element.57), channel_id=1, source_target_pairs={{0,2},{1,3},{2,0},{3,1},{4,6},{5,7},{6,4},{7,5},{8,10},{9,11},{10,... | collective-permute-start | bytes 786440 | tf_op jit(solution)/shard_map/ppermute | solution.py:380
  63.9 13.4 %collective-permute-start.15 = (f32[8,8,1024]{2,1,0:T(8,128)S(1)}, f32[8,8,1024]{2,1,0:T(8,128)S(1)}, u32[]{:S(2)}, u32[]{:S(2)}) collective-permute-start(f32[8,8,1024]{2,1,0:T(8,128)S(1)} %get-tuple-element.58), channel_id=1, source_target_pairs={{0,3},{1,2},{2,1},{3,0},{4,7},{5,6},{6,5},{7,4},{8,11},{9,10},{10,... | collective-permute-start | bytes 786440 | tf_op jit(solution)/shard_map/ppermute | solution.py:380

commit v4 on v3

--- a/solution.py
+++ b/solution.py
@@ -146,55 +146,74 @@
     lax.fori_loop(0, rows, one_row, 0, unroll=8)
 
 
-def cut_body(groups, first_row, rank_ref, cells_ref, after_ref, *refs):
+def later_window(taker, own_rows, total_rows, first_row, count):
+    return jnp.clip(taker * own_rows + first_row + 1, 0, total_rows - count)
+
+
+def cut_body(groups, first_row, count, rank_ref, cells_ref, after_ref, *refs):
     del after_ref
     columns, outs, sems = refs[:-1 - groups], refs[-1 - groups:-1], refs[-1]
     rows = cells_ref.shape[0]
-    extra = 2 if columns else 0
+    own_rows = rows // groups
     copies = []
     for flip, out_ref in enumerate(outs):
-        count = out_ref.shape[0] - extra
-        taker = lax.bitwise_xor(rank_ref[0], flip)
-        top = window(taker, rows // groups, rows, first_row, count - 2)
+        top = later_window(lax.bitwise_xor(rank_ref[0], flip), own_rows, rows, first_row, count)
         copies.append(pltpu.make_async_copy(cells_ref.at[pl.ds(top, count)], out_ref.at[pl.ds(0, count)], sems.at[flip]))
     for copy in copies:
         copy.start()
     for flip, out_ref in enumerate(outs):
-        count = out_ref.shape[0] - extra
-        top = lax.bitwise_xor(rank_ref[0], flip) * (rows // groups) + first_row
+        top = lax.bitwise_xor(rank_ref[0], flip) * own_rows + first_row
         for side, column in enumerate(columns):
             half = column.shape[2] - TILE
-            for step in range(count - 2):
+            for step in range(count):
                 out_ref[count, step:step + 1, half * side:half * (side + 1)] = column[top + step, :, :half]
                 out_ref[count + 1, step:step + 1, TILE * side:TILE * (side + 1)] = column[top + step, :, half:]
     for copy in copies:
         copy.wait()
 
 
-def edges_body(groups, first_row, passing, rank_ref, *refs):
+def reader(sources, carried, rank, own_rows, total_rows, first_row, count):
+    if not carried:
+        start = window(rank, own_rows, total_rows, first_row, count)
+        return lambda flip, row, of: sources[flip][row - start, :, of]
+    origin = rank * own_rows + first_row
+    start = later_window(rank, own_rows, total_rows, first_row, count)
+
+    def read(flip, row, of):
+        old = carried[flip][jnp.clip(row - origin + 1, 0, 1), :, of]
+        new = sources[flip][jnp.clip(row - start, 0, count - 1), :, of]
+        return jnp.where(row > origin, new, old)
+    return read
+
+
+def edges_body(groups, first_row, count, passing, later, rank_ref, *refs):
     sources, refs = refs[:groups], refs[groups:]
+    carried, refs = (refs[:groups], refs[groups:]) if later else ((), refs)
     kind_ref, tables_ref = refs[1:3]
     first_ref, last_ref, density_ref = refs[3 + passing:6 + passing]
+    keeps = () if later else refs[6 + passing:]
     cols, total_rows = kind_ref.shape
-    count = first_ref.shape[0] // N
-    carried = sources[0].shape[0] > count + 2
     half = sources[0].shape[2] // 2
     per = N // groups
     rank = rank_ref[0]
+    own_rows = total_rows // groups
     kinds = kind_ref[...]
     place = lax.broadcasted_iota(jnp.int32, kinds.shape, 1)
     lane = lax.broadcasted_iota(jnp.int32, density_ref.shape, 1)
-    start = window(rank, total_rows // groups, total_rows, first_row, count)
+    read = reader(sources, carried, rank, own_rows, total_rows, first_row, count)
+    for flip, keep in enumerate(keeps):
+        for at in range(2):
+            keep[at] = read(flip, rank * own_rows + first_row + count - 1 + at, slice(None))
     densities = jnp.zeros(density_ref.shape, f32)
     for step in range(count + 2):
-        row = jnp.clip(rank * (total_rows // groups) + first_row - 1 + step, 0, total_rows - 1)
-        values = [source[row - start] for source in sources]
+        row = jnp.clip(rank * own_rows + first_row - 1 + step, 0, total_rows - 1)
+        values = [read(flip, row, slice(None)) for flip in range(groups)]
         density = jnp.sum(sum(values), axis=1, keepdims=True)
         densities = jnp.where(lane == step, density, densities)
         if 0 < step <= count:
             kind = column_of(kinds, place, row)
             at = slice(step - 1, step)
-            tails = [[source[count + 3, at, TILE * side:TILE * (side + 1)] for source in sources] for side in range(2) if carried]
+            tails = [[source[count + 1, at, TILE * side:TILE * (side + 1)] for source in sources] for side in range(2) if later]
             known = [(column_of(tail[0], lane[:1], 1), column_of(sum(tail), lane[:1], 0)) for tail in tails]
             for flip, (value, source) in enumerate(zip(values, sources)):
                 for i in range(per):
@@ -202,8 +221,8 @@
                     table = tables_ref[at]
                     for tile, cell, out_ref in ((0, 0, first_ref), (1, cols - 1, last_ref)):
                         of = slice(TILE * tile, TILE * (tile + 1))
-                        if carried:
-                            raw = source[count + 2, step - 1:step, half * (1 - tile) + TILE * i:half * (1 - tile) + TILE * (i + 1)]
+                        if later:
+                            raw = source[count, step - 1:step, half * (1 - tile) + TILE * i:half * (1 - tile) + TILE * (i + 1)]
                             out_ref[(step - 1) * N + at] = walled(*known[1 - tile], raw, table, of)
                         else:
                             edge = walled(kind, density, value[:, PLANE * i + TILE * tile:PLANE * i + TILE * (tile + 1)], table, of)
@@ -211,8 +230,9 @@
     density_ref[...] = densities
 
 
-def collide_body(groups, dirs, batch, first_row, rank_ref, *refs):
+def collide_body(groups, dirs, batch, first_row, later, rank_ref, *refs):
     sources, refs = refs[:groups], refs[groups:]
+    carried, refs = (refs[:groups], refs[groups:]) if later else ((), refs)
     before_ref, after_ref, density_ref, kind_ref, tables_ref, low_ref, top_ref, matrix_ref, _ = refs[:9]
     outs, refs = refs[9:9 + groups], refs[9 + groups:]
     moved_refs, spec_refs, gain_ref = refs[:2], refs[2:4], refs[4]
@@ -221,7 +241,6 @@
     matrix_ref, low_ref, top_ref = kept
     for copy in copies:
         copy.start()
-    copies[0].wait()
     rows = N * CELLS
     per = N // groups
     steps = outs[0].shape[0]
@@ -233,11 +252,11 @@
     lane = lax.broadcasted_iota(jnp.int32, density_ref.shape, 1)
     kinds, densities = kind_ref[...], density_ref[...]
     origin = rank * own_rows + first_row
-    start = window(rank, own_rows, total_rows, first_row, steps)
+    read = reader(sources, carried, rank, own_rows, total_rows, first_row, steps)
 
     def cells_of(step):
         row = jnp.clip(origin + step, 0, total_rows - 1)
-        return row - start, column_of(kinds, place, row), column_of(densities, lane, step + 1)
+        return row, column_of(kinds, place, row), column_of(densities, lane, step + 1)
 
     def turned(value, at):
         straight, crossed = dot(value, matrix_ref[at]), dot(value, matrix_ref[at + 1])
@@ -256,8 +275,8 @@
                 for tile in range(2):
                     at = slice(TILE * tile, TILE * (tile + 1))
                     of = slice(PLANE * i + TILE * tile, PLANE * i + TILE * (tile + 1))
-                    now = walled(kind, density, source[now_at, :, of], table, at)
-                    other = walled(other_kind, other_density, source[other_at, :, of], table, at)
+                    now = walled(kind, density, read(flip, now_at, of), table, at)
+                    other = walled(other_kind, other_density, read(flip, other_at, of), table, at)
                     if tile:
                         near = jnp.where(sub == 0, before_ref[step * N + line], pltpu.roll(now, 1, 0))
                     else:
@@ -312,27 +331,33 @@
             for i in range(per):
                 out_ref[step, :, PLANE * i:PLANE * (i + 1)] = moved_ref[at + i]
 
-    for _ in prepare(0, moved_refs[0], spec_refs[0]):
+    opening = prepare(0, moved_refs[0], spec_refs[0])
+    next(opening)
+    copies[0].wait()
+    for _ in opening:
         pass
     copies[1].wait()
     copies[2].wait()
 
     def two_rows(pair, _):
-        one, other = 2 * pair, jnp.minimum(2 * pair + 1, steps - 1)
-        following = jnp.minimum(2 * pair + 2, steps - 1)
-        finish(one, moved_refs[0], spec_refs[0], prepare(other, moved_refs[1], spec_refs[1]))
-        finish(other, moved_refs[1], spec_refs[1], prepare(following, moved_refs[0], spec_refs[0]))
+        finish(2 * pair, moved_refs[0], spec_refs[0], prepare(2 * pair + 1, moved_refs[1], spec_refs[1]))
+        finish(2 * pair + 1, moved_refs[1], spec_refs[1], prepare(2 * pair + 2, moved_refs[0], spec_refs[0]))
         return 0
 
-    lax.fori_loop(0, (steps + 1) // 2, two_rows, 0)
-
-
-def place_body(groups, starts, rank_ref, *refs):
-    pieces, (out_ref, sems) = refs[:-2], refs[-2:]
+    lax.fori_loop(0, (steps - 1) // 2, two_rows, 0)
+    if steps % 2 == 0:
+        finish(steps - 2, moved_refs[0], spec_refs[0], prepare(steps - 1, moved_refs[1], spec_refs[1]))
+    last = (steps - 1) % 2
+    finish(steps - 1, moved_refs[last], spec_refs[last], iter(()))
+
+
+def place_body(groups, places, rank_ref, *refs):
+    pieces, refs = refs[:len(places)], refs[len(places):]
+    out_ref, sems = refs[-2:]
     own_rows = out_ref.shape[0] // groups
     copies = []
-    for at, piece in enumerate(pieces):
-        top = lax.bitwise_xor(rank_ref[0], at % groups) * own_rows + starts[at // groups]
+    for at, (piece, (flip, first_row)) in enumerate(zip(pieces, places)):
+        top = lax.bitwise_xor(rank_ref[0], flip) * own_rows + first_row
         copies.append(pltpu.make_async_copy(piece, out_ref.at[pl.ds(top, piece.shape[0])], sems.at[at]))
     for copy in copies:
         copy.start()
@@ -340,17 +365,17 @@
         copy.wait()
 
 
-def collide(rank, sources, before, after, density, kinds, tables, low, top, matrices, earlier, first_row, steps):
+def collide(rank, sources, carried, before, after, density, kinds, tables, low, top, matrices, earlier, first_row, steps):
     groups = len(sources)
     dirs = low.shape[1] // 3
     _, cols, width = sources[0].shape
     vmem = pl.BlockSpec(memory_space=pltpu.VMEM)
     shape = jax.ShapeDtypeStruct((steps, cols, width), f32)
-    operands = (*sources, before, after, density, kinds, tables, low, top, matrices, earlier)
+    operands = (*sources, *carried, before, after, density, kinds, tables, low, top, matrices, earlier)
     cells = pltpu.VMEM((N, CELLS, PLANE), f32)
     spec = pltpu.VMEM((2 * N * CELLS, PLANE), f32)
     return call(
-        functools.partial(collide_body, groups, dirs, 4, first_row), (shape,) * groups, (rank, *operands),
+        functools.partial(collide_body, groups, dirs, 4, first_row, bool(carried)), (shape,) * groups, (rank, *operands),
         flops=steps * 2 * PLANE ** 3 * (2 * dirs + 6), limit=6,
         scratch=[cells, cells, spec, spec, pltpu.VMEM((N * CELLS, PLANE), f32)]
         + [pltpu.VMEM(value.shape, value.dtype) for value in (matrices, low, top)] + [pltpu.SemaphoreType.DMA((3,))],
@@ -381,22 +406,24 @@
         return [swapped[flip] for flip in range(groups)]
 
     def cut(first_row, count, earlier, *columns):
-        block = jax.ShapeDtypeStruct((count + 2 + len(columns), cols, width), f32)
+        block = jax.ShapeDtypeStruct((count + 2, cols, width), f32)
         return call(
-            functools.partial(cut_body, groups, first_row), (block,) * groups, (rank_word, distribution, earlier, *columns),
+            functools.partial(cut_body, groups, first_row, count), (block,) * groups, (rank_word, distribution, earlier, *columns),
             in_specs=[smem, anywhere, anywhere] + [vmem] * len(columns), out_specs=(vmem,) * groups,
             scratch=[pltpu.SemaphoreType.DMA((groups,))])
 
-    def rims(first_row, count, sources, *passing):
+    def rims(first_row, count, sources, carried=(), passing=()):
         edge = jax.ShapeDtypeStruct((count * N, 1, TILE), f32)
         same = [jax.ShapeDtypeStruct(value.shape, f32) for value in passing]
+        keep = [] if carried else [jax.ShapeDtypeStruct((2, cols, width), f32)] * groups
+        before = 1 + len(sources) + len(carried) + 3
         return call(
-            functools.partial(edges_body, groups, first_row, len(passing)),
-            (edge, edge, jax.ShapeDtypeStruct((cols, TILE), f32), *same),
-            (rank_word, *sources, matrices, kinds, tables, *passing),
-            in_specs=[smem] + [vmem] * groups + [anywhere, vmem, vmem] + [anywhere] * len(passing),
-            out_specs=(vmem,) * 3 + (anywhere,) * len(passing),
-            input_output_aliases={groups + 4 + at: 3 + at for at in range(len(passing))})
+            functools.partial(edges_body, groups, first_row, count, len(passing), bool(carried)),
+            (edge, edge, jax.ShapeDtypeStruct((cols, TILE), f32), *same, *keep),
+            (rank_word, *sources, *carried, matrices, kinds, tables, *passing),
+            in_specs=[smem] + [vmem] * (before - 4) + [anywhere, vmem, vmem] + [anywhere] * len(passing),
+            out_specs=(vmem,) * 3 + (anywhere,) * len(passing) + (vmem,) * len(keep),
+            input_output_aliases={before + at: 3 + at for at in range(len(passing))})
 
     def to_neighbours(first, last):
         return (lax.ppermute(last, "cell", [(i, i + 1) for i in range(spots - 1)]),
@@ -410,17 +437,18 @@
     column = jax.ShapeDtypeStruct((rows, 1, width // 2 + TILE), f32)
     columns = to_neighbours(*call(
         columns_body, (column, column), (distribution, kinds, cuts[0]), in_specs=[vmem, vmem, anywhere], out_specs=(vmem,) * 2))
-    first, last, density = rims(first_row, count, sources)
+    first, last, density, *carried = rims(first_row, count, sources)
     edges = to_neighbours(first, last)
     following = cut(next_row, next_count, density, *columns)
-    done = collide(rank_word, sources, *edges, density, kinds, tables, low, top, matrices, following[0], first_row, count)
+    done = collide(rank_word, sources, (), *edges, density, kinds, tables, low, top, matrices, following[0], first_row, count)
     sources = swap(following)
-    after, before, density, *done = rims(next_row, next_count, sources, *done)
+    after, before, density, *done = rims(next_row, next_count, sources, carried, done)
     home = swap(done)
-    done = collide(rank_word, sources, before, after, density, kinds, tables, low, top, matrices, done[0], next_row, next_count)
+    done = collide(rank_word, sources, carried, before, after, density, kinds, tables, low, top, matrices, done[0], next_row, next_count)
     pieces = (*home, *swap(done))
+    places = [(flip, row) for row in (first_row, next_row) for flip in range(groups)]
     return call(
-        functools.partial(place_body, groups, (first_row, next_row)), jax.ShapeDtypeStruct(distribution.shape, f32),
+        functools.partial(place_body, groups, places), jax.ShapeDtypeStruct(distribution.shape, f32),
         (rank_word, *pieces), in_specs=[smem] + [vmem] * len(pieces), out_specs=anywhere,
         scratch=[pltpu.SemaphoreType.DMA((len(pieces),))])
 

time: 78.8 us -> 77.4 us (0.982); the launches traced: 78.7 us -> 76.3 us
  waiting for transfers between devices: 23.3 us -> 21.2 us
    ppermute x12, waiting for transfers between devices: 23.3 us -> 21.2 us  [swap(): lax.ppermute(values[flip], 'vel', [(i, i ^ flip) for i in range(groups)])]
  transfers between devices with their start and end apart: 16 -> 16, of which waited for: 5 -> 5; matrix products, arithmetic and copies ran while one was open for 0% -> 0% of each run, Pallas kernels for 40% -> 41%
where the time goes in v4:
time: 77.4 us; the launch traced here: 76.3 us
  Pallas kernels  32.8 us (42%)
  waiting for transfers between devices  21.2 us (27%)
  starting transfers between devices  20.4 us (26%)
  local copies, waits for them, and re-layouts  1.58 us (2%)
    pallas_call x8, Pallas kernels, call(): pl.pallas_call(kernel, out_shape=out_shape, scratch_shapes=list(scratch),...  32.8 us
    ppermute x12, waiting for transfers between devices, swap(): lax.ppermute(values[flip], 'vel', [(i, i ^ flip) for i in range(groups)])  21.2 us
    ppermute x12, starting transfers between devices, swap(): lax.ppermute(values[flip], 'vel', [(i, i ^ flip) for i in range(groups)])  15.2 us
    ppermute x2, starting transfers between devices, to_neighbours(): lax.ppermute(last, 'cell', [(i, i + 1) for i in range(spots - 1)])  2.59 us
    ppermute x2, starting transfers between devices, to_neighbours(): lax.ppermute(first, 'cell', [(i + 1, i) for i in range(spots - 1)])  2.58 us
    dynamic_slice x1, local copies, waits for them, and re-layouts, on_device(): lax.dynamic_slice_in_dim(distribution, window(rank ^ flip, own_rows, rows...  1.55 us
  transfers between devices with their start and end apart: 16, of which 5 were waited for; matrix products, arithmetic and copies ran while one was open for 0% of the time, Pallas kernels for 41%

profile of v4, /device:TPU:0, one launch (start us, length us, event | category | flops | bytes accessed | tf_op | source)
XLA Modules:
  0.0 76.3 jit_solution(1983487513894406655)
XLA Ops:
  0.0 1.6 %constant_dynamic-slice_fusion = (f32[10,8,1024]{2,1,0:T(8,128)S(1)}, f32[10,8,1024]{2,1,0:T(8,128)S(1)}, f32[10,8,1024]{2,1,0:T(8,128)S(1)}, f32[10,8,1024]{2,1,0:T(8,128)S(1)}) fusion(f32[64,8,1024]{2,1,0:T(8,128)} %cells_ref.3, s32[]{:T(128)S(6)} %min.16, s32[]{:T(128)S(6)} %min.15, s32[]{:T(128)S(6)} %min.14, s32[]{:T(128)S(6)} %min.13), kind=kLoop, calls=%fused_computation.1 | loop fusion | bytes 2621456 | tf_op jit(solution)/shard_map/dynamic_slice | solution.py:433
  1.6 3.0 %collective-permute-start = (f32[10,8,1024]{2,1,0:T(8,128)S(1)}, f32[10,8,1024]{2,1,0:T(8,128)S(1)}, u32[]{:S(2)}, u32[]{:S(2)}) collective-permute-start(f32[10,8,1024]{2,1,0:T(8,128)S(1)} %get-tuple-element.69), channel_id=1, source_target_pairs={{0,1},{1,0},{2,3},{3,2},{4,5},{5,4},{6,7},{7,6},{8,9},{9,8},{10,11... | collective-permute-start | bytes 983048 | tf_op jit(solution)/shard_map/ppermute | solution.py:405
  4.6 1.5 %collective-permute-start.1 = (f32[10,8,1024]{2,1,0:T(8,128)S(1)}, f32[10,8,1024]{2,1,0:T(8,128)S(1)}, u32[]{:S(2)}, u32[]{:S(2)}) collective-permute-start(f32[10,8,1024]{2,1,0:T(8,128)S(1)} %get-tuple-element.68), channel_id=1, source_target_pairs={{0,2},{1,3},{2,0},{3,1},{4,6},{5,7},{6,4},{7,5},{8,10},{9,11},{10,... | collective-permute-start | bytes 983048 | tf_op jit(solution)/shard_map/ppermute | solution.py:405
  6.1 0.0 collective-permute-start.2
  6.2 1.0 %shard_map.84 = (f32[64,1,640]{2,1,0:T(1,128)S(1)}, f32[64,1,640]{2,1,0:T(1,128)S(1)}) custom-call(f32[64,8,1024]{2,1,0:T(8,128)S(1)} %copy-done, f32[8,64]{1,0:T(8,128)S(1)} %convert_bitcast_fusion.refs_5_.kind_ref.refs_7_.refs_9_.refs_11_, f32[10,8,1024]{2,1,0:T(8,128)S(1)} %get-tuple-element.70.refs_0_.after_ref), custom_call_target="tpu_custom_call" | custom-call | bytes 2754560 | tf_op jit(solution)/shard_map/pallas_call | solution.py:77
  7.1 1.3 %collective-permute-start.3 = (f32[64,1,640]{2,1,0:T(1,128)S(1)}, f32[64,1,640]{2,1,0:T(1,128)S(1)}, u32[]{:S(2)}, u32[]{:S(2)}) collective-permute-start(f32[64,1,640]{2,1,0:T(1,128)S(1)} %get-tuple-element.38), channel_id=1, source_target_pairs={{0,4},{4,8},{8,12},{12,16},{16,20},{20,24},{24,28},{1,5},{5,9},{9,... | collective-permute-start | bytes 491528 | tf_op jit(solution)/shard_map/ppermute | solution.py:429
  8.4 1.3 %collective-permute-start.4 = (f32[64,1,640]{2,1,0:T(1,128)S(1)}, f32[64,1,640]{2,1,0:T(1,128)S(1)}, u32[]{:S(2)}, u32[]{:S(2)}) collective-permute-start(f32[64,1,640]{2,1,0:T(1,128)S(1)} %get-tuple-element.39), channel_id=1, source_target_pairs={{4,0},{8,4},{12,8},{16,12},{20,16},{24,20},{28,24},{5,1},{9,5},{13... | collective-permute-start | bytes 491528 | tf_op jit(solution)/shard_map/ppermute | solution.py:430
  9.8 0.9 %shard_map.82 = (f32[16,48,128]{2,1,0:T(8,128)S(1)}, f32[16,48,128]{2,1,0:T(8,128)S(1)}, bf16[7,256,256]{2,1,0:T(8,128)(2,1)S(1)}) custom-call(f32[16,4096]{1,0:T(8,128)S(1)} %copy-done.4, f32[16,4096]{1,0:T(8,128)S(1)} %copy-done.5, f32[1,4096]{1,0:T(1,128)S(1)} %bitcast.4, f32[256,512]{1,0:T(8,128)S(1)} %copy-done.2, f32[7,256,256]{2,1,0:T(8,128)S(1)} %copy-done.1), custom_call_target="tpu_custom_call" | custom-call | flops 603979776 | bytes 4603904 | tf_op jit(solution)/shard_map/pallas_call | solution.py:77
  10.7 2.5 %collective-permute-done.refs_1_ = f32[10,8,1024]{2,1,0:T(8,128)S(1)} collective-permute-done((f32[10,8,1024]{2,1,0:T(8,128)S(1)}, f32[10,8,1024]{2,1,0:T(8,128)S(1)}, u32[]{:S(2)}, u32[]{:S(2)}) %collective-permute-start) | collective-permute-done | bytes 327712 | tf_op jit(solution)/shard_map/ppermute | solution.py:405
  13.2 7.7 %collective-permute-done.1.refs_2_ = f32[10,8,1024]{2,1,0:T(8,128)S(1)} collective-permute-done((f32[10,8,1024]{2,1,0:T(8,128)S(1)}, f32[10,8,1024]{2,1,0:T(8,128)S(1)}, u32[]{:S(2)}, u32[]{:S(2)}) %collective-permute-start.1) | collective-permute-done | bytes 327712 | tf_op jit(solution)/shard_map/ppermute | solution.py:405
  20.8 0.0 collective-permute-done.2.refs_3_
  20.8 0.3 shard_map.83
  21.1 1.3 %collective-permute-start.8 = (f32[128,1,128]{2,1,0:T(1,128)S(1)}, f32[128,1,128]{2,1,0:T(1,128)S(1)}, u32[]{:S(2)}, u32[]{:S(2)}) collective-permute-start(f32[128,1,128]{2,1,0:T(1,128)S(1)} %get-tuple-element.48), channel_id=1, source_target_pairs={{0,4},{4,8},{8,12},{12,16},{16,20},{20,24},{24,28},{1,5},{5,9},{9,... | collective-permute-start | bytes 196616 | tf_op jit(solution)/shard_map/ppermute | solution.py:429
  22.4 1.3 %collective-permute-start.9 = (f32[128,1,128]{2,1,0:T(1,128)S(1)}, f32[128,1,128]{2,1,0:T(1,128)S(1)}, u32[]{:S(2)}, u32[]{:S(2)}) collective-permute-start(f32[128,1,128]{2,1,0:T(1,128)S(1)} %get-tuple-element.49), channel_id=1, source_target_pairs={{4,0},{8,4},{12,8},{16,12},{20,16},{24,20},{28,24},{5,1},{9,5},{13... | collective-permute-start | bytes 196616 | tf_op jit(solution)/shard_map/ppermute | solution.py:430
  23.7 0.0 collective-permute-done.4.refs_1_
  23.7 0.2 shard_map.85
  23.9 1.3 %collective-permute-start.5 = (f32[10,8,1024]{2,1,0:T(8,128)S(1)}, f32[10,8,1024]{2,1,0:T(8,128)S(1)}, u32[]{:S(2)}, u32[]{:S(2)}) collective-permute-start(f32[10,8,1024]{2,1,0:T(8,128)S(1)} %get-tuple-element.41), channel_id=1, source_target_pairs={{0,1},{1,0},{2,3},{3,2},{4,5},{5,4},{6,7},{7,6},{8,9},{9,8},{10,11... | collective-permute-start | bytes 983048 | tf_op jit(solution)/shard_map/ppermute | solution.py:405
  25.2 0.8 %collective-permute-start.6 = (f32[10,8,1024]{2,1,0:T(8,128)S(1)}, f32[10,8,1024]{2,1,0:T(8,128)S(1)}, u32[]{:S(2)}, u32[]{:S(2)}) collective-permute-start(f32[10,8,1024]{2,1,0:T(8,128)S(1)} %get-tuple-element.42), channel_id=1, source_target_pairs={{0,2},{1,3},{2,0},{3,1},{4,6},{5,7},{6,4},{7,5},{8,10},{9,11},{10,... | collective-permute-start | bytes 983048 | tf_op jit(solution)/shard_map/ppermute | solution.py:405
  26.0 1.4 %collective-permute-start.7 = (f32[10,8,1024]{2,1,0:T(8,128)S(1)}, f32[10,8,1024]{2,1,0:T(8,128)S(1)}, u32[]{:S(2)}, u32[]{:S(2)}) collective-permute-start(f32[10,8,1024]{2,1,0:T(8,128)S(1)} %get-tuple-element.43), channel_id=1, source_target_pairs={{0,3},{1,2},{2,1},{3,0},{4,7},{5,6},{6,5},{7,4},{8,11},{9,10},{10,... | collective-permute-start | bytes 983048 | tf_op jit(solution)/shard_map/ppermute | solution.py:405
  27.5 14.2 %shard_map.86 = (f32[8,8,1024]{2,1,0:T(8,128)S(1)}, f32[8,8,1024]{2,1,0:T(8,128)S(1)}, f32[8,8,1024]{2,1,0:T(8,128)S(1)}, f32[8,8,1024]{2,1,0:T(8,128)S(1)}) custom-call(s32[1]{0:T(128)} %bitcast.rank_ref, f32[10,8,1024]{2,1,0:T(8,128)S(1)} %get-tuple-element.70.refs_0_.after_ref, f32[10,8,1024]{2,1,0:T(8,128)S(1)} %collective-permute-done.refs_1_, ...), custom_call_target="tpu_custom_call" | custom-call | flops 10200547328 | bytes 4659204 | tf_op jit(solution)/shard_map/pallas_call | solution.py:77
  41.7 0.4 shard_map.87
  42.1 1.3 %collective-permute-start.10 = (f32[8,8,1024]{2,1,0:T(8,128)S(1)}, f32[8,8,1024]{2,1,0:T(8,128)S(1)}, u32[]{:S(2)}, u32[]{:S(2)}) collective-permute-start(f32[8,8,1024]{2,1,0:T(8,128)S(1)} %get-tuple-element.57), channel_id=1, source_target_pairs={{0,1},{1,0},{2,3},{3,2},{4,5},{5,4},{6,7},{7,6},{8,9},{9,8},{10,11... | collective-permute-start | bytes 786440 | tf_op jit(solution)/shard_map/ppermute | solution.py:405
  43.4 0.8 %collective-permute-start.11 = (f32[8,8,1024]{2,1,0:T(8,128)S(1)}, f32[8,8,1024]{2,1,0:T(8,128)S(1)}, u32[]{:S(2)}, u32[]{:S(2)}) collective-permute-start(f32[8,8,1024]{2,1,0:T(8,128)S(1)} %get-tuple-element.58), channel_id=1, source_target_pairs={{0,2},{1,3},{2,0},{3,1},{4,6},{5,7},{6,4},{7,5},{8,10},{9,11},{10,... | collective-permute-start | bytes 786440 | tf_op jit(solution)/shard_map/ppermute | solution.py:405
  44.2 1.4 %collective-permute-start.12 = (f32[8,8,1024]{2,1,0:T(8,128)S(1)}, f32[8,8,1024]{2,1,0:T(8,128)S(1)}, u32[]{:S(2)}, u32[]{:S(2)}) collective-permute-start(f32[8,8,1024]{2,1,0:T(8,128)S(1)} %get-tuple-element.59), channel_id=1, source_target_pairs={{0,3},{1,2},{2,1},{3,0},{4,7},{5,6},{6,5},{7,4},{8,11},{9,10},{10,... | collective-permute-start | bytes 786440 | tf_op jit(solution)/shard_map/ppermute | solution.py:405
  45.6 14.5 %shard_map.88 = (f32[8,8,1024]{2,1,0:T(8,128)S(1)}, f32[8,8,1024]{2,1,0:T(8,128)S(1)}, f32[8,8,1024]{2,1,0:T(8,128)S(1)}, f32[8,8,1024]{2,1,0:T(8,128)S(1)}) custom-call(s32[1]{0:T(128)} %bitcast.rank_ref, f32[10,8,1024]{2,1,0:T(8,128)S(1)} %get-tuple-element.40.refs_12_.refs_0_, f32[10,8,1024]{2,1,0:T(8,128)S(1)} %collective-permute-done.5.refs_1_, ...), custom_call_target="tpu_custom_call" | custom-call | flops 10200547328 | bytes 4855812 | tf_op jit(solution)/shard_map/pallas_call | solution.py:77
  60.2 1.3 %collective-permute-start.13 = (f32[8,8,1024]{2,1,0:T(8,128)S(1)}, f32[8,8,1024]{2,1,0:T(8,128)S(1)}, u32[]{:S(2)}, u32[]{:S(2)}) collective-permute-start(f32[8,8,1024]{2,1,0:T(8,128)S(1)} %get-tuple-element.64), channel_id=1, source_target_pairs={{0,1},{1,0},{2,3},{3,2},{4,5},{5,4},{6,7},{7,6},{8,9},{9,8},{10,11... | collective-permute-start | bytes 786440 | tf_op jit(solution)/shard_map/ppermute | solution.py:405
  61.5 0.8 %collective-permute-start.14 = (f32[8,8,1024]{2,1,0:T(8,128)S(1)}, f32[8,8,1024]{2,1,0:T(8,128)S(1)}, u32[]{:S(2)}, u32[]{:S(2)}) collective-permute-start(f32[8,8,1024]{2,1,0:T(8,128)S(1)} %get-tuple-element.65), channel_id=1, source_target_pairs={{0,2},{1,3},{2,0},{3,1},{4,6},{5,7},{6,4},{7,5},{8,10},{9,11},{10,... | collective-permute-start | bytes 786440 | tf_op jit(solution)/shard_map/ppermute | solution.py:405
  62.3 1.4 %collective-permute-start.15 = (f32[8,8,1024]{2,1,0:T(8,128)S(1)}, f32[8,8,1024]{2,1,0:T(8,128)S(1)}, u32[]{:S(2)}, u32[]{:S(2)}) collective-permute-start(f32[8,8,1024]{2,1,0:T(8,128)S(1)} %get-tuple-element.66), channel_id=1, source_target_pairs={{0,3},{1,2},{2,1},{3,0},{4,7},{5,6},{6,5},{7,4},{8,11},{9,10},{10,... | collective-permute-start | bytes 786440 | tf_op jit(solution)/shard_map/ppermute | solution.py:405
  63.8 4.3 %collective-permute-done.13.refs_5_ = f32[8,8,1024]{2,1,0:T(8,128)S(1)} collective-permute-done((f32[8,8,1024]{2,1,0:T(8,128)S(1)}, f32[8,8,1024]{2,1,0:T(8,128)S(1)}, u32[]{:S(2)}, u32[]{:S(2)}) %collective-permute-start.13) | collective-permute-done | bytes 262176 | tf_op jit(solution)/shard_map/ppermute | solution.py:405
  68.1 2.1 %collective-permute-done.14.refs_6_ = f32[8,8,1024]{2,1,0:T(8,128)S(1)} collective-permute-done((f32[8,8,1024]{2,1,0:T(8,128)S(1)}, f32[8,8,1024]{2,1,0:T(8,128)S(1)}, u32[]{:S(2)}, u32[]{:S(2)}) %collective-permute-start.14) | collective-permute-done | bytes 262176 | tf_op jit(solution)/shard_map/ppermute | solution.py:405
  70.2 4.6 %collective-permute-done.15.refs_7_ = f32[8,8,1024]{2,1,0:T(8,128)S(1)} collective-permute-done((f32[8,8,1024]{2,1,0:T(8,128)S(1)}, f32[8,8,1024]{2,1,0:T(8,128)S(1)}, u32[]{:S(2)}, u32[]{:S(2)}) %collective-permute-start.15) | collective-permute-done | bytes 262176 | tf_op jit(solution)/shard_map/ppermute | solution.py:405
  74.8 1.4 %shard_map.89 = f32[64,8,1024]{2,1,0:T(8,128)} custom-call(s32[1]{0:T(128)} %bitcast.rank_ref, f32[8,8,1024]{2,1,0:T(8,128)S(1)} %get-tuple-element.56.refs_16_.refs_0_, f32[8,8,1024]{2,1,0:T(8,128)S(1)} %collective-permute-done.10.refs_1_, f32[8,8,1024]{2,1,0:T(8,128)S(1)} %collective-permute-done.11.refs_2_, ...), custom_call_target="tpu_custom_call" | custom-call | bytes 4194308 | tf_op jit(solution)/shard_map/pallas_call | solution.py:77
  (26 shorter events, 0.1 us)
Async XLA Ops:
  0.0 6.2 %copy-start = (f32[64,8,1024]{2,1,0:T(8,128)S(1)}, f32[64,8,1024]{2,1,0:T(8,128)}, u32[]{:S(2)}) copy-start(f32[64,8,1024]{2,1,0:T(8,128)} %cells_ref.3) | copy-start | bytes 6291460
  0.0 6.2 %copy-start.7 = (s32[64,8]{0,1:T(8,128)S(1)}, s32[64,8]{0,1:T(8,128)}, u32[]{:S(2)}) copy-start(s32[64,8]{0,1:T(8,128)} %param.9) | copy-start | bytes 6148
  0.0 9.7 %copy-start.1 = (f32[7,256,256]{2,1,0:T(8,128)S(1)}, f32[7,256,256]{2,1,0:T(8,128)}, u32[]{:S(2)}) copy-start(f32[7,256,256]{2,1,0:T(8,128)} %constant.34.clone.table_ref) | copy-start | bytes 5505028
  0.0 9.7 %copy-start.2 = (f32[256,512]{1,0:T(8,128)S(1)}, f32[256,512]{1,0:T(8,128)}, u32[]{:S(2)}) copy-start(f32[256,512]{1,0:T(8,128)} %constant.33.clone.pick_ref) | copy-start | bytes 1572868
  0.0 9.7 %copy-start.4 = (f32[16,4096]{1,0:T(8,128)S(1)}, f32[16,4096]{1,0:T(8,128)}, u32[]{:S(2)}) copy-start(f32[16,4096]{1,0:T(8,128)} %first_ref.1) | copy-start | bytes 786436
  0.0 9.8 %copy-start.5 = (f32[16,4096]{1,0:T(8,128)S(1)}, f32[16,4096]{1,0:T(8,128)}, u32[]{:S(2)}) copy-start(f32[16,4096]{1,0:T(8,128)} %second_ref.1) | copy-start | bytes 786436
  0.0 9.8 %copy-start.6 = (f32[4096]{0:T(1024)S(1)}, f32[4096]{0:T(1024)}, u32[]{:S(2)}) copy-start(f32[4096]{0:T(1024)} %param.12) | copy-start | bytes 49156
  1.6 11.6 %collective-permute-start = (f32[10,8,1024]{2,1,0:T(8,128)S(1)}, f32[10,8,1024]{2,1,0:T(8,128)S(1)}, u32[]{:S(2)}, u32[]{:S(2)}) collective-permute-start(f32[10,8,1024]{2,1,0:T(8,128)S(1)} %get-tuple-element.69), channel_id=1, source_target_pairs={{0,1},{1,0},{2,3},{3,2},{4,5},{5,4},{6,7},{7,6},{8,9},{9,8},{10,11... | collective-permute-start | bytes 983048 | tf_op jit(solution)/shard_map/ppermute | solution.py:405
  4.6 16.2 %collective-permute-start.1 = (f32[10,8,1024]{2,1,0:T(8,128)S(1)}, f32[10,8,1024]{2,1,0:T(8,128)S(1)}, u32[]{:S(2)}, u32[]{:S(2)}) collective-permute-start(f32[10,8,1024]{2,1,0:T(8,128)S(1)} %get-tuple-element.68), channel_id=1, source_target_pairs={{0,2},{1,3},{2,0},{3,1},{4,6},{5,7},{6,4},{7,5},{8,10},{9,11},{10,... | collective-permute-start | bytes 983048 | tf_op jit(solution)/shard_map/ppermute | solution.py:405
  6.1 14.7 %collective-permute-start.2 = (f32[10,8,1024]{2,1,0:T(8,128)S(1)}, f32[10,8,1024]{2,1,0:T(8,128)S(1)}, u32[]{:S(2)}, u32[]{:S(2)}) collective-permute-start(f32[10,8,1024]{2,1,0:T(8,128)S(1)} %get-tuple-element.67), channel_id=1, source_target_pairs={{0,3},{1,2},{2,1},{3,0},{4,7},{5,6},{6,5},{7,4},{8,11},{9,10},{10,... | collective-permute-start | bytes 983048 | tf_op jit(solution)/shard_map/ppermute | solution.py:405
  6.2 14.6 %copy-start.3 = (f32[16,8,256]{2,1,0:T(8,128)S(1)}, f32[16,8,256]{2,1,0:T(8,128)}, u32[]{:S(2)}) copy-start(f32[16,8,256]{2,1,0:T(8,128)} %constant.32.clone.refs_6_.refs_8_.refs_10_.refs_12_) | copy-start | bytes 393220
  7.1 16.6 %collective-permute-start.3 = (f32[64,1,640]{2,1,0:T(1,128)S(1)}, f32[64,1,640]{2,1,0:T(1,128)S(1)}, u32[]{:S(2)}, u32[]{:S(2)}) collective-permute-start(f32[64,1,640]{2,1,0:T(1,128)S(1)} %get-tuple-element.38), channel_id=1, source_target_pairs={{0,4},{4,8},{8,12},{12,16},{16,20},{20,24},{24,28},{1,5},{5,9},{9,... | collective-permute-start | bytes 491528 | tf_op jit(solution)/shard_map/ppermute | solution.py:429
  8.4 15.3 %collective-permute-start.4 = (f32[64,1,640]{2,1,0:T(1,128)S(1)}, f32[64,1,640]{2,1,0:T(1,128)S(1)}, u32[]{:S(2)}, u32[]{:S(2)}) collective-permute-start(f32[64,1,640]{2,1,0:T(1,128)S(1)} %get-tuple-element.39), channel_id=1, source_target_pairs={{4,0},{8,4},{12,8},{16,12},{20,16},{24,20},{28,24},{5,1},{9,5},{13... | collective-permute-start | bytes 491528 | tf_op jit(solution)/shard_map/ppermute | solution.py:430
  21.1 6.4 %collective-permute-start.8 = (f32[128,1,128]{2,1,0:T(1,128)S(1)}, f32[128,1,128]{2,1,0:T(1,128)S(1)}, u32[]{:S(2)}, u32[]{:S(2)}) collective-permute-start(f32[128,1,128]{2,1,0:T(1,128)S(1)} %get-tuple-element.48), channel_id=1, source_target_pairs={{0,4},{4,8},{8,12},{12,16},{16,20},{20,24},{24,28},{1,5},{5,9},{9,... | collective-permute-start | bytes 196616 | tf_op jit(solution)/shard_map/ppermute | solution.py:429
  22.4 5.1 %collective-permute-start.9 = (f32[128,1,128]{2,1,0:T(1,128)S(1)}, f32[128,1,128]{2,1,0:T(1,128)S(1)}, u32[]{:S(2)}, u32[]{:S(2)}) collective-permute-start(f32[128,1,128]{2,1,0:T(1,128)S(1)} %get-tuple-element.49), channel_id=1, source_target_pairs={{4,0},{8,4},{12,8},{16,12},{20,16},{24,20},{28,24},{5,1},{9,5},{13... | collective-permute-start | bytes 196616 | tf_op jit(solution)/shard_map/ppermute | solution.py:430
  23.9 17.8 %collective-permute-start.5 = (f32[10,8,1024]{2,1,0:T(8,128)S(1)}, f32[10,8,1024]{2,1,0:T(8,128)S(1)}, u32[]{:S(2)}, u32[]{:S(2)}) collective-permute-start(f32[10,8,1024]{2,1,0:T(8,128)S(1)} %get-tuple-element.41), channel_id=1, source_target_pairs={{0,1},{1,0},{2,3},{3,2},{4,5},{5,4},{6,7},{7,6},{8,9},{9,8},{10,11... | collective-permute-start | bytes 983048 | tf_op jit(solution)/shard_map/ppermute | solution.py:405
  25.2 16.5 %collective-permute-start.6 = (f32[10,8,1024]{2,1,0:T(8,128)S(1)}, f32[10,8,1024]{2,1,0:T(8,128)S(1)}, u32[]{:S(2)}, u32[]{:S(2)}) collective-permute-start(f32[10,8,1024]{2,1,0:T(8,128)S(1)} %get-tuple-element.42), channel_id=1, source_target_pairs={{0,2},{1,3},{2,0},{3,1},{4,6},{5,7},{6,4},{7,5},{8,10},{9,11},{10,... | collective-permute-start | bytes 983048 | tf_op jit(solution)/shard_map/ppermute | solution.py:405
  26.0 15.7 %collective-permute-start.7 = (f32[10,8,1024]{2,1,0:T(8,128)S(1)}, f32[10,8,1024]{2,1,0:T(8,128)S(1)}, u32[]{:S(2)}, u32[]{:S(2)}) collective-permute-start(f32[10,8,1024]{2,1,0:T(8,128)S(1)} %get-tuple-element.43), channel_id=1, source_target_pairs={{0,3},{1,2},{2,1},{3,0},{4,7},{5,6},{6,5},{7,4},{8,11},{9,10},{10,... | collective-permute-start | bytes 983048 | tf_op jit(solution)/shard_map/ppermute | solution.py:405
  42.1 20.2 %collective-permute-start.10 = (f32[8,8,1024]{2,1,0:T(8,128)S(1)}, f32[8,8,1024]{2,1,0:T(8,128)S(1)}, u32[]{:S(2)}, u32[]{:S(2)}) collective-permute-start(f32[8,8,1024]{2,1,0:T(8,128)S(1)} %get-tuple-element.57), channel_id=1, source_target_pairs={{0,1},{1,0},{2,3},{3,2},{4,5},{5,4},{6,7},{7,6},{8,9},{9,8},{10,11... | collective-permute-start | bytes 786440 | tf_op jit(solution)/shard_map/ppermute | solution.py:405
  43.4 20.4 %collective-permute-start.11 = (f32[8,8,1024]{2,1,0:T(8,128)S(1)}, f32[8,8,1024]{2,1,0:T(8,128)S(1)}, u32[]{:S(2)}, u32[]{:S(2)}) collective-permute-start(f32[8,8,1024]{2,1,0:T(8,128)S(1)} %get-tuple-element.58), channel_id=1, source_target_pairs={{0,2},{1,3},{2,0},{3,1},{4,6},{5,7},{6,4},{7,5},{8,10},{9,11},{10,... | collective-permute-start | bytes 786440 | tf_op jit(solution)/shard_map/ppermute | solution.py:405
  44.2 19.5 %collective-permute-start.12 = (f32[8,8,1024]{2,1,0:T(8,128)S(1)}, f32[8,8,1024]{2,1,0:T(8,128)S(1)}, u32[]{:S(2)}, u32[]{:S(2)}) collective-permute-start(f32[8,8,1024]{2,1,0:T(8,128)S(1)} %get-tuple-element.59), channel_id=1, source_target_pairs={{0,3},{1,2},{2,1},{3,0},{4,7},{5,6},{6,5},{7,4},{8,11},{9,10},{10,... | collective-permute-start | bytes 786440 | tf_op jit(solution)/shard_map/ppermute | solution.py:405
  60.2 7.9 %collective-permute-start.13 = (f32[8,8,1024]{2,1,0:T(8,128)S(1)}, f32[8,8,1024]{2,1,0:T(8,128)S(1)}, u32[]{:S(2)}, u32[]{:S(2)}) collective-permute-start(f32[8,8,1024]{2,1,0:T(8,128)S(1)} %get-tuple-element.64), channel_id=1, source_target_pairs={{0,1},{1,0},{2,3},{3,2},{4,5},{5,4},{6,7},{7,6},{8,9},{9,8},{10,11... | collective-permute-start | bytes 786440 | tf_op jit(solution)/shard_map/ppermute | solution.py:405
  61.5 8.7 %collective-permute-start.14 = (f32[8,8,1024]{2,1,0:T(8,128)S(1)}, f32[8,8,1024]{2,1,0:T(8,128)S(1)}, u32[]{:S(2)}, u32[]{:S(2)}) collective-permute-start(f32[8,8,1024]{2,1,0:T(8,128)S(1)} %get-tuple-element.65), channel_id=1, source_target_pairs={{0,2},{1,3},{2,0},{3,1},{4,6},{5,7},{6,4},{7,5},{8,10},{9,11},{10,... | collective-permute-start | bytes 786440 | tf_op jit(solution)/shard_map/ppermute | solution.py:405
  62.3 12.4 %collective-permute-start.15 = (f32[8,8,1024]{2,1,0:T(8,128)S(1)}, f32[8,8,1024]{2,1,0:T(8,128)S(1)}, u32[]{:S(2)}, u32[]{:S(2)}) collective-permute-start(f32[8,8,1024]{2,1,0:T(8,128)S(1)} %get-tuple-element.66), channel_id=1, source_target_pairs={{0,3},{1,2},{2,1},{3,0},{4,7},{5,6},{6,5},{7,4},{8,11},{9,10},{10,... | collective-permute-start | bytes 786440 | tf_op jit(solution)/shard_map/ppermute | solution.py:405

commit v5 on v4

--- a/solution.py
+++ b/solution.py
@@ -309,22 +309,21 @@
             return [jnp.concatenate([value[:rows, TILE * t:TILE * (t + 1)], value[rows:, TILE * t:TILE * (t + 1)]], 1)
                     for t in range(len(pair))]
 
-        gain_ref[...] = jnp.zeros_like(gain_ref)
         for first in range(0, dirs, batch):
-            stack = []
+            stack = along_i(2 * dirs) if first == 0 else []
             for p in range(first, min(first + batch, dirs)):
                 stack += along_i(p, dirs + p)
             value = dot(jnp.concatenate(stack, 0), matrix_ref[6])
-            total = gain_ref[...]
-            for at in range(0, value.shape[0], 2 * rows):
+            skip = rows if first == 0 else 0
+            total = gain_ref[...] if first else -moved_ref[...].reshape(rows, PLANE) * value[:rows]
+            for at in range(skip, value.shape[0], 2 * rows):
                 total = total + value[at:at + rows] * value[at + rows:at + 2 * rows]
             gain_ref[...] = total
             next(beside, None)
         for _ in beside:
             pass
-        loss = dot(along_i(2 * dirs)[0], matrix_ref[6])
         now = moved_ref[...]
-        collision = (gain_ref[...] - now.reshape(rows, PLANE) * loss).reshape(N, CELLS, PLANE)
+        collision = gain_ref[...].reshape(N, CELLS, PLANE)
         moved_ref[...] = jnp.where(cells_of(step)[1] == 0.0, now + collision_timestep * collision, now)
         for flip, out_ref in enumerate(outs):
             at = lax.bitwise_xor(rank, flip) * per

time: 77.4 us -> 77.9 us (level)
  no operation moved by 1% of the time
where the time goes in v5:
time: 77.9 us; the launch traced here: 76.8 us
  Pallas kernels  33.2 us (43%)
  waiting for transfers between devices  21.2 us (27%)
  starting transfers between devices  20.4 us (26%)
  local copies, waits for them, and re-layouts  1.58 us (2%)
    pallas_call x8, Pallas kernels, call(): pl.pallas_call(kernel, out_shape=out_shape, scratch_shapes=list(scratch),...  33.2 us
    ppermute x12, waiting for transfers between devices, swap(): lax.ppermute(values[flip], 'vel', [(i, i ^ flip) for i in range(groups)])  21.2 us
    ppermute x12, starting transfers between devices, swap(): lax.ppermute(values[flip], 'vel', [(i, i ^ flip) for i in range(groups)])  15.2 us
    ppermute x2, starting transfers between devices, to_neighbours(): lax.ppermute(last, 'cell', [(i, i + 1) for i in range(spots - 1)])  2.59 us
    ppermute x2, starting transfers between devices, to_neighbours(): lax.ppermute(first, 'cell', [(i + 1, i) for i in range(spots - 1)])  2.58 us
  transfers between devices with their start and end apart: 16, of which 5 were waited for; matrix products, arithmetic and copies ran while one was open for 0% of the time, Pallas kernels for 41%

profile of v5, /device:TPU:0, one launch (start us, length us, event | category | flops | bytes accessed | tf_op | source)
XLA Modules:
  0.0 76.8 jit_solution(13515408456419531652)
XLA Ops:
  0.0 1.6 %constant_dynamic-slice_fusion = (f32[10,8,1024]{2,1,0:T(8,128)S(1)}, f32[10,8,1024]{2,1,0:T(8,128)S(1)}, f32[10,8,1024]{2,1,0:T(8,128)S(1)}, f32[10,8,1024]{2,1,0:T(8,128)S(1)}) fusion(f32[64,8,1024]{2,1,0:T(8,128)} %cells_ref.3, s32[]{:T(128)S(6)} %min.16, s32[]{:T(128)S(6)} %min.15, s32[]{:T(128)S(6)} %min.14, s32[]{:T(128)S(6)} %min.13), kind=kLoop, calls=%fused_computation.1 | loop fusion | bytes 2621456 | tf_op jit(solution)/shard_map/dynamic_slice | solution.py:432
  1.6 3.0 %collective-permute-start = (f32[10,8,1024]{2,1,0:T(8,128)S(1)}, f32[10,8,1024]{2,1,0:T(8,128)S(1)}, u32[]{:S(2)}, u32[]{:S(2)}) collective-permute-start(f32[10,8,1024]{2,1,0:T(8,128)S(1)} %get-tuple-element.69), channel_id=1, source_target_pairs={{0,1},{1,0},{2,3},{3,2},{4,5},{5,4},{6,7},{7,6},{8,9},{9,8},{10,11... | collective-permute-start | bytes 983048 | tf_op jit(solution)/shard_map/ppermute | solution.py:404
  4.6 1.5 %collective-permute-start.1 = (f32[10,8,1024]{2,1,0:T(8,128)S(1)}, f32[10,8,1024]{2,1,0:T(8,128)S(1)}, u32[]{:S(2)}, u32[]{:S(2)}) collective-permute-start(f32[10,8,1024]{2,1,0:T(8,128)S(1)} %get-tuple-element.68), channel_id=1, source_target_pairs={{0,2},{1,3},{2,0},{3,1},{4,6},{5,7},{6,4},{7,5},{8,10},{9,11},{10,... | collective-permute-start | bytes 983048 | tf_op jit(solution)/shard_map/ppermute | solution.py:404
  6.1 0.0 collective-permute-start.2
  6.2 1.0 %shard_map.84 = (f32[64,1,640]{2,1,0:T(1,128)S(1)}, f32[64,1,640]{2,1,0:T(1,128)S(1)}) custom-call(f32[64,8,1024]{2,1,0:T(8,128)S(1)} %copy-done, f32[8,64]{1,0:T(8,128)S(1)} %convert_bitcast_fusion.refs_5_.kind_ref.refs_7_.refs_9_.refs_11_, f32[10,8,1024]{2,1,0:T(8,128)S(1)} %get-tuple-element.70.refs_0_.after_ref), custom_call_target="tpu_custom_call" | custom-call | bytes 2754560 | tf_op jit(solution)/shard_map/pallas_call | solution.py:77
  7.1 1.3 %collective-permute-start.3 = (f32[64,1,640]{2,1,0:T(1,128)S(1)}, f32[64,1,640]{2,1,0:T(1,128)S(1)}, u32[]{:S(2)}, u32[]{:S(2)}) collective-permute-start(f32[64,1,640]{2,1,0:T(1,128)S(1)} %get-tuple-element.38), channel_id=1, source_target_pairs={{0,4},{4,8},{8,12},{12,16},{16,20},{20,24},{24,28},{1,5},{5,9},{9,... | collective-permute-start | bytes 491528 | tf_op jit(solution)/shard_map/ppermute | solution.py:428
  8.4 1.3 %collective-permute-start.4 = (f32[64,1,640]{2,1,0:T(1,128)S(1)}, f32[64,1,640]{2,1,0:T(1,128)S(1)}, u32[]{:S(2)}, u32[]{:S(2)}) collective-permute-start(f32[64,1,640]{2,1,0:T(1,128)S(1)} %get-tuple-element.39), channel_id=1, source_target_pairs={{4,0},{8,4},{12,8},{16,12},{20,16},{24,20},{28,24},{5,1},{9,5},{13... | collective-permute-start | bytes 491528 | tf_op jit(solution)/shard_map/ppermute | solution.py:429
  9.8 0.9 %shard_map.82 = (f32[16,48,128]{2,1,0:T(8,128)S(1)}, f32[16,48,128]{2,1,0:T(8,128)S(1)}, bf16[7,256,256]{2,1,0:T(8,128)(2,1)S(1)}) custom-call(f32[16,4096]{1,0:T(8,128)S(1)} %copy-done.4, f32[16,4096]{1,0:T(8,128)S(1)} %copy-done.5, f32[1,4096]{1,0:T(1,128)S(1)} %bitcast.4, f32[256,512]{1,0:T(8,128)S(1)} %copy-done.2, f32[7,256,256]{2,1,0:T(8,128)S(1)} %copy-done.1), custom_call_target="tpu_custom_call" | custom-call | flops 603979776 | bytes 4603904 | tf_op jit(solution)/shard_map/pallas_call | solution.py:77
  10.7 2.5 %collective-permute-done.refs_1_ = f32[10,8,1024]{2,1,0:T(8,128)S(1)} collective-permute-done((f32[10,8,1024]{2,1,0:T(8,128)S(1)}, f32[10,8,1024]{2,1,0:T(8,128)S(1)}, u32[]{:S(2)}, u32[]{:S(2)}) %collective-permute-start) | collective-permute-done | bytes 327712 | tf_op jit(solution)/shard_map/ppermute | solution.py:404
  13.2 7.7 %collective-permute-done.1.refs_2_ = f32[10,8,1024]{2,1,0:T(8,128)S(1)} collective-permute-done((f32[10,8,1024]{2,1,0:T(8,128)S(1)}, f32[10,8,1024]{2,1,0:T(8,128)S(1)}, u32[]{:S(2)}, u32[]{:S(2)}) %collective-permute-start.1) | collective-permute-done | bytes 327712 | tf_op jit(solution)/shard_map/ppermute | solution.py:404
  20.8 0.3 shard_map.83
  21.1 1.3 %collective-permute-start.8 = (f32[128,1,128]{2,1,0:T(1,128)S(1)}, f32[128,1,128]{2,1,0:T(1,128)S(1)}, u32[]{:S(2)}, u32[]{:S(2)}) collective-permute-start(f32[128,1,128]{2,1,0:T(1,128)S(1)} %get-tuple-element.48), channel_id=1, source_target_pairs={{0,4},{4,8},{8,12},{12,16},{16,20},{20,24},{24,28},{1,5},{5,9},{9,... | collective-permute-start | bytes 196616 | tf_op jit(solution)/shard_map/ppermute | solution.py:428
  22.4 1.3 %collective-permute-start.9 = (f32[128,1,128]{2,1,0:T(1,128)S(1)}, f32[128,1,128]{2,1,0:T(1,128)S(1)}, u32[]{:S(2)}, u32[]{:S(2)}) collective-permute-start(f32[128,1,128]{2,1,0:T(1,128)S(1)} %get-tuple-element.49), channel_id=1, source_target_pairs={{4,0},{8,4},{12,8},{16,12},{20,16},{24,20},{28,24},{5,1},{9,5},{13... | collective-permute-start | bytes 196616 | tf_op jit(solution)/shard_map/ppermute | solution.py:429
  23.7 0.0 collective-permute-done.3.refs_0_
  23.7 0.2 shard_map.85
  23.9 1.3 %collective-permute-start.5 = (f32[10,8,1024]{2,1,0:T(8,128)S(1)}, f32[10,8,1024]{2,1,0:T(8,128)S(1)}, u32[]{:S(2)}, u32[]{:S(2)}) collective-permute-start(f32[10,8,1024]{2,1,0:T(8,128)S(1)} %get-tuple-element.41), channel_id=1, source_target_pairs={{0,1},{1,0},{2,3},{3,2},{4,5},{5,4},{6,7},{7,6},{8,9},{9,8},{10,11... | collective-permute-start | bytes 983048 | tf_op jit(solution)/shard_map/ppermute | solution.py:404
  25.2 0.8 %collective-permute-start.6 = (f32[10,8,1024]{2,1,0:T(8,128)S(1)}, f32[10,8,1024]{2,1,0:T(8,128)S(1)}, u32[]{:S(2)}, u32[]{:S(2)}) collective-permute-start(f32[10,8,1024]{2,1,0:T(8,128)S(1)} %get-tuple-element.42), channel_id=1, source_target_pairs={{0,2},{1,3},{2,0},{3,1},{4,6},{5,7},{6,4},{7,5},{8,10},{9,11},{10,... | collective-permute-start | bytes 983048 | tf_op jit(solution)/shard_map/ppermute | solution.py:404
  26.0 1.4 %collective-permute-start.7 = (f32[10,8,1024]{2,1,0:T(8,128)S(1)}, f32[10,8,1024]{2,1,0:T(8,128)S(1)}, u32[]{:S(2)}, u32[]{:S(2)}) collective-permute-start(f32[10,8,1024]{2,1,0:T(8,128)S(1)} %get-tuple-element.43), channel_id=1, source_target_pairs={{0,3},{1,2},{2,1},{3,0},{4,7},{5,6},{6,5},{7,4},{8,11},{9,10},{10,... | collective-permute-start | bytes 983048 | tf_op jit(solution)/shard_map/ppermute | solution.py:404
  27.5 0.0 collective-permute-done.8.refs_4_
  27.5 14.4 %shard_map.86 = (f32[8,8,1024]{2,1,0:T(8,128)S(1)}, f32[8,8,1024]{2,1,0:T(8,128)S(1)}, f32[8,8,1024]{2,1,0:T(8,128)S(1)}, f32[8,8,1024]{2,1,0:T(8,128)S(1)}) custom-call(s32[1]{0:T(128)} %bitcast.rank_ref, f32[10,8,1024]{2,1,0:T(8,128)S(1)} %get-tuple-element.70.refs_0_.after_ref, f32[10,8,1024]{2,1,0:T(8,128)S(1)} %collective-permute-done.refs_1_, ...), custom_call_target="tpu_custom_call" | custom-call | flops 10200547328 | bytes 4659204 | tf_op jit(solution)/shard_map/pallas_call | solution.py:77
  41.9 0.4 shard_map.87
  42.3 1.3 %collective-permute-start.10 = (f32[8,8,1024]{2,1,0:T(8,128)S(1)}, f32[8,8,1024]{2,1,0:T(8,128)S(1)}, u32[]{:S(2)}, u32[]{:S(2)}) collective-permute-start(f32[8,8,1024]{2,1,0:T(8,128)S(1)} %get-tuple-element.57), channel_id=1, source_target_pairs={{0,1},{1,0},{2,3},{3,2},{4,5},{5,4},{6,7},{7,6},{8,9},{9,8},{10,11... | collective-permute-start | bytes 786440 | tf_op jit(solution)/shard_map/ppermute | solution.py:404
  43.6 0.8 %collective-permute-start.11 = (f32[8,8,1024]{2,1,0:T(8,128)S(1)}, f32[8,8,1024]{2,1,0:T(8,128)S(1)}, u32[]{:S(2)}, u32[]{:S(2)}) collective-permute-start(f32[8,8,1024]{2,1,0:T(8,128)S(1)} %get-tuple-element.58), channel_id=1, source_target_pairs={{0,2},{1,3},{2,0},{3,1},{4,6},{5,7},{6,4},{7,5},{8,10},{9,11},{10,... | collective-permute-start | bytes 786440 | tf_op jit(solution)/shard_map/ppermute | solution.py:404
  44.5 1.4 %collective-permute-start.12 = (f32[8,8,1024]{2,1,0:T(8,128)S(1)}, f32[8,8,1024]{2,1,0:T(8,128)S(1)}, u32[]{:S(2)}, u32[]{:S(2)}) collective-permute-start(f32[8,8,1024]{2,1,0:T(8,128)S(1)} %get-tuple-element.59), channel_id=1, source_target_pairs={{0,3},{1,2},{2,1},{3,0},{4,7},{5,6},{6,5},{7,4},{8,11},{9,10},{10,... | collective-permute-start | bytes 786440 | tf_op jit(solution)/shard_map/ppermute | solution.py:404
  45.9 14.8 %shard_map.88 = (f32[8,8,1024]{2,1,0:T(8,128)S(1)}, f32[8,8,1024]{2,1,0:T(8,128)S(1)}, f32[8,8,1024]{2,1,0:T(8,128)S(1)}, f32[8,8,1024]{2,1,0:T(8,128)S(1)}) custom-call(s32[1]{0:T(128)} %bitcast.rank_ref, f32[10,8,1024]{2,1,0:T(8,128)S(1)} %get-tuple-element.40.refs_12_.refs_0_, f32[10,8,1024]{2,1,0:T(8,128)S(1)} %collective-permute-done.5.refs_1_, ...), custom_call_target="tpu_custom_call" | custom-call | flops 10200547328 | bytes 4855812 | tf_op jit(solution)/shard_map/pallas_call | solution.py:77
  60.6 1.3 %collective-permute-start.13 = (f32[8,8,1024]{2,1,0:T(8,128)S(1)}, f32[8,8,1024]{2,1,0:T(8,128)S(1)}, u32[]{:S(2)}, u32[]{:S(2)}) collective-permute-start(f32[8,8,1024]{2,1,0:T(8,128)S(1)} %get-tuple-element.64), channel_id=1, source_target_pairs={{0,1},{1,0},{2,3},{3,2},{4,5},{5,4},{6,7},{7,6},{8,9},{9,8},{10,11... | collective-permute-start | bytes 786440 | tf_op jit(solution)/shard_map/ppermute | solution.py:404
  62.0 0.9 %collective-permute-start.14 = (f32[8,8,1024]{2,1,0:T(8,128)S(1)}, f32[8,8,1024]{2,1,0:T(8,128)S(1)}, u32[]{:S(2)}, u32[]{:S(2)}) collective-permute-start(f32[8,8,1024]{2,1,0:T(8,128)S(1)} %get-tuple-element.65), channel_id=1, source_target_pairs={{0,2},{1,3},{2,0},{3,1},{4,6},{5,7},{6,4},{7,5},{8,10},{9,11},{10,... | collective-permute-start | bytes 786440 | tf_op jit(solution)/shard_map/ppermute | solution.py:404
  62.8 1.4 %collective-permute-start.15 = (f32[8,8,1024]{2,1,0:T(8,128)S(1)}, f32[8,8,1024]{2,1,0:T(8,128)S(1)}, u32[]{:S(2)}, u32[]{:S(2)}) collective-permute-start(f32[8,8,1024]{2,1,0:T(8,128)S(1)} %get-tuple-element.66), channel_id=1, source_target_pairs={{0,3},{1,2},{2,1},{3,0},{4,7},{5,6},{6,5},{7,4},{8,11},{9,10},{10,... | collective-permute-start | bytes 786440 | tf_op jit(solution)/shard_map/ppermute | solution.py:404
  64.2 4.3 %collective-permute-done.13.refs_5_ = f32[8,8,1024]{2,1,0:T(8,128)S(1)} collective-permute-done((f32[8,8,1024]{2,1,0:T(8,128)S(1)}, f32[8,8,1024]{2,1,0:T(8,128)S(1)}, u32[]{:S(2)}, u32[]{:S(2)}) %collective-permute-start.13) | collective-permute-done | bytes 262176 | tf_op jit(solution)/shard_map/ppermute | solution.py:404
  68.6 2.2 %collective-permute-done.14.refs_6_ = f32[8,8,1024]{2,1,0:T(8,128)S(1)} collective-permute-done((f32[8,8,1024]{2,1,0:T(8,128)S(1)}, f32[8,8,1024]{2,1,0:T(8,128)S(1)}, u32[]{:S(2)}, u32[]{:S(2)}) %collective-permute-start.14) | collective-permute-done | bytes 262176 | tf_op jit(solution)/shard_map/ppermute | solution.py:404
  70.7 4.5 %collective-permute-done.15.refs_7_ = f32[8,8,1024]{2,1,0:T(8,128)S(1)} collective-permute-done((f32[8,8,1024]{2,1,0:T(8,128)S(1)}, f32[8,8,1024]{2,1,0:T(8,128)S(1)}, u32[]{:S(2)}, u32[]{:S(2)}) %collective-permute-start.15) | collective-permute-done | bytes 262176 | tf_op jit(solution)/shard_map/ppermute | solution.py:404
  75.3 1.4 %shard_map.89 = f32[64,8,1024]{2,1,0:T(8,128)} custom-call(s32[1]{0:T(128)} %bitcast.rank_ref, f32[8,8,1024]{2,1,0:T(8,128)S(1)} %get-tuple-element.56.refs_16_.refs_0_, f32[8,8,1024]{2,1,0:T(8,128)S(1)} %collective-permute-done.10.refs_1_, f32[8,8,1024]{2,1,0:T(8,128)S(1)} %collective-permute-done.11.refs_2_, ...), custom_call_target="tpu_custom_call" | custom-call | bytes 4194308 | tf_op jit(solution)/shard_map/pallas_call | solution.py:77
  (26 shorter events, 0.1 us)
Async XLA Ops:
  0.0 6.2 %copy-start = (f32[64,8,1024]{2,1,0:T(8,128)S(1)}, f32[64,8,1024]{2,1,0:T(8,128)}, u32[]{:S(2)}) copy-start(f32[64,8,1024]{2,1,0:T(8,128)} %cells_ref.3) | copy-start | bytes 6291460
  0.0 6.2 %copy-start.7 = (s32[64,8]{0,1:T(8,128)S(1)}, s32[64,8]{0,1:T(8,128)}, u32[]{:S(2)}) copy-start(s32[64,8]{0,1:T(8,128)} %param.9) | copy-start | bytes 6148
  0.0 9.7 %copy-start.1 = (f32[7,256,256]{2,1,0:T(8,128)S(1)}, f32[7,256,256]{2,1,0:T(8,128)}, u32[]{:S(2)}) copy-start(f32[7,256,256]{2,1,0:T(8,128)} %constant.34.clone.table_ref) | copy-start | bytes 5505028
  0.0 9.7 %copy-start.2 = (f32[256,512]{1,0:T(8,128)S(1)}, f32[256,512]{1,0:T(8,128)}, u32[]{:S(2)}) copy-start(f32[256,512]{1,0:T(8,128)} %constant.33.clone.pick_ref) | copy-start | bytes 1572868
  0.0 9.7 %copy-start.4 = (f32[16,4096]{1,0:T(8,128)S(1)}, f32[16,4096]{1,0:T(8,128)}, u32[]{:S(2)}) copy-start(f32[16,4096]{1,0:T(8,128)} %first_ref.1) | copy-start | bytes 786436
  0.0 9.8 %copy-start.5 = (f32[16,4096]{1,0:T(8,128)S(1)}, f32[16,4096]{1,0:T(8,128)}, u32[]{:S(2)}) copy-start(f32[16,4096]{1,0:T(8,128)} %second_ref.1) | copy-start | bytes 786436
  0.0 9.8 %copy-start.6 = (f32[4096]{0:T(1024)S(1)}, f32[4096]{0:T(1024)}, u32[]{:S(2)}) copy-start(f32[4096]{0:T(1024)} %param.12) | copy-start | bytes 49156
  1.6 11.6 %collective-permute-start = (f32[10,8,1024]{2,1,0:T(8,128)S(1)}, f32[10,8,1024]{2,1,0:T(8,128)S(1)}, u32[]{:S(2)}, u32[]{:S(2)}) collective-permute-start(f32[10,8,1024]{2,1,0:T(8,128)S(1)} %get-tuple-element.69), channel_id=1, source_target_pairs={{0,1},{1,0},{2,3},{3,2},{4,5},{5,4},{6,7},{7,6},{8,9},{9,8},{10,11... | collective-permute-start | bytes 983048 | tf_op jit(solution)/shard_map/ppermute | solution.py:404
  4.6 16.2 %collective-permute-start.1 = (f32[10,8,1024]{2,1,0:T(8,128)S(1)}, f32[10,8,1024]{2,1,0:T(8,128)S(1)}, u32[]{:S(2)}, u32[]{:S(2)}) collective-permute-start(f32[10,8,1024]{2,1,0:T(8,128)S(1)} %get-tuple-element.68), channel_id=1, source_target_pairs={{0,2},{1,3},{2,0},{3,1},{4,6},{5,7},{6,4},{7,5},{8,10},{9,11},{10,... | collective-permute-start | bytes 983048 | tf_op jit(solution)/shard_map/ppermute | solution.py:404
  6.1 14.7 %collective-permute-start.2 = (f32[10,8,1024]{2,1,0:T(8,128)S(1)}, f32[10,8,1024]{2,1,0:T(8,128)S(1)}, u32[]{:S(2)}, u32[]{:S(2)}) collective-permute-start(f32[10,8,1024]{2,1,0:T(8,128)S(1)} %get-tuple-element.67), channel_id=1, source_target_pairs={{0,3},{1,2},{2,1},{3,0},{4,7},{5,6},{6,5},{7,4},{8,11},{9,10},{10,... | collective-permute-start | bytes 983048 | tf_op jit(solution)/shard_map/ppermute | solution.py:404
  6.2 14.6 %copy-start.3 = (f32[16,8,256]{2,1,0:T(8,128)S(1)}, f32[16,8,256]{2,1,0:T(8,128)}, u32[]{:S(2)}) copy-start(f32[16,8,256]{2,1,0:T(8,128)} %constant.32.clone.refs_6_.refs_8_.refs_10_.refs_12_) | copy-start | bytes 393220
  7.1 16.6 %collective-permute-start.3 = (f32[64,1,640]{2,1,0:T(1,128)S(1)}, f32[64,1,640]{2,1,0:T(1,128)S(1)}, u32[]{:S(2)}, u32[]{:S(2)}) collective-permute-start(f32[64,1,640]{2,1,0:T(1,128)S(1)} %get-tuple-element.38), channel_id=1, source_target_pairs={{0,4},{4,8},{8,12},{12,16},{16,20},{20,24},{24,28},{1,5},{5,9},{9,... | collective-permute-start | bytes 491528 | tf_op jit(solution)/shard_map/ppermute | solution.py:428
  8.4 15.3 %collective-permute-start.4 = (f32[64,1,640]{2,1,0:T(1,128)S(1)}, f32[64,1,640]{2,1,0:T(1,128)S(1)}, u32[]{:S(2)}, u32[]{:S(2)}) collective-permute-start(f32[64,1,640]{2,1,0:T(1,128)S(1)} %get-tuple-element.39), channel_id=1, source_target_pairs={{4,0},{8,4},{12,8},{16,12},{20,16},{24,20},{28,24},{5,1},{9,5},{13... | collective-permute-start | bytes 491528 | tf_op jit(solution)/shard_map/ppermute | solution.py:429
  21.1 6.4 %collective-permute-start.8 = (f32[128,1,128]{2,1,0:T(1,128)S(1)}, f32[128,1,128]{2,1,0:T(1,128)S(1)}, u32[]{:S(2)}, u32[]{:S(2)}) collective-permute-start(f32[128,1,128]{2,1,0:T(1,128)S(1)} %get-tuple-element.48), channel_id=1, source_target_pairs={{0,4},{4,8},{8,12},{12,16},{16,20},{20,24},{24,28},{1,5},{5,9},{9,... | collective-permute-start | bytes 196616 | tf_op jit(solution)/shard_map/ppermute | solution.py:428
  22.4 5.1 %collective-permute-start.9 = (f32[128,1,128]{2,1,0:T(1,128)S(1)}, f32[128,1,128]{2,1,0:T(1,128)S(1)}, u32[]{:S(2)}, u32[]{:S(2)}) collective-permute-start(f32[128,1,128]{2,1,0:T(1,128)S(1)} %get-tuple-element.49), channel_id=1, source_target_pairs={{4,0},{8,4},{12,8},{16,12},{20,16},{24,20},{28,24},{5,1},{9,5},{13... | collective-permute-start | bytes 196616 | tf_op jit(solution)/shard_map/ppermute | solution.py:429
  23.9 18.0 %collective-permute-start.5 = (f32[10,8,1024]{2,1,0:T(8,128)S(1)}, f32[10,8,1024]{2,1,0:T(8,128)S(1)}, u32[]{:S(2)}, u32[]{:S(2)}) collective-permute-start(f32[10,8,1024]{2,1,0:T(8,128)S(1)} %get-tuple-element.41), channel_id=1, source_target_pairs={{0,1},{1,0},{2,3},{3,2},{4,5},{5,4},{6,7},{7,6},{8,9},{9,8},{10,11... | collective-permute-start | bytes 983048 | tf_op jit(solution)/shard_map/ppermute | solution.py:404
  25.2 16.7 %collective-permute-start.6 = (f32[10,8,1024]{2,1,0:T(8,128)S(1)}, f32[10,8,1024]{2,1,0:T(8,128)S(1)}, u32[]{:S(2)}, u32[]{:S(2)}) collective-permute-start(f32[10,8,1024]{2,1,0:T(8,128)S(1)} %get-tuple-element.42), channel_id=1, source_target_pairs={{0,2},{1,3},{2,0},{3,1},{4,6},{5,7},{6,4},{7,5},{8,10},{9,11},{10,... | collective-permute-start | bytes 983048 | tf_op jit(solution)/shard_map/ppermute | solution.py:404
  26.0 15.9 %collective-permute-start.7 = (f32[10,8,1024]{2,1,0:T(8,128)S(1)}, f32[10,8,1024]{2,1,0:T(8,128)S(1)}, u32[]{:S(2)}, u32[]{:S(2)}) collective-permute-start(f32[10,8,1024]{2,1,0:T(8,128)S(1)} %get-tuple-element.43), channel_id=1, source_target_pairs={{0,3},{1,2},{2,1},{3,0},{4,7},{5,6},{6,5},{7,4},{8,11},{9,10},{10,... | collective-permute-start | bytes 983048 | tf_op jit(solution)/shard_map/ppermute | solution.py:404
  42.3 20.5 %collective-permute-start.10 = (f32[8,8,1024]{2,1,0:T(8,128)S(1)}, f32[8,8,1024]{2,1,0:T(8,128)S(1)}, u32[]{:S(2)}, u32[]{:S(2)}) collective-permute-start(f32[8,8,1024]{2,1,0:T(8,128)S(1)} %get-tuple-element.57), channel_id=1, source_target_pairs={{0,1},{1,0},{2,3},{3,2},{4,5},{5,4},{6,7},{7,6},{8,9},{9,8},{10,11... | collective-permute-start | bytes 786440 | tf_op jit(solution)/shard_map/ppermute | solution.py:404
  43.6 20.6 %collective-permute-start.11 = (f32[8,8,1024]{2,1,0:T(8,128)S(1)}, f32[8,8,1024]{2,1,0:T(8,128)S(1)}, u32[]{:S(2)}, u32[]{:S(2)}) collective-permute-start(f32[8,8,1024]{2,1,0:T(8,128)S(1)} %get-tuple-element.58), channel_id=1, source_target_pairs={{0,2},{1,3},{2,0},{3,1},{4,6},{5,7},{6,4},{7,5},{8,10},{9,11},{10,... | collective-permute-start | bytes 786440 | tf_op jit(solution)/shard_map/ppermute | solution.py:404
  44.5 19.8 %collective-permute-start.12 = (f32[8,8,1024]{2,1,0:T(8,128)S(1)}, f32[8,8,1024]{2,1,0:T(8,128)S(1)}, u32[]{:S(2)}, u32[]{:S(2)}) collective-permute-start(f32[8,8,1024]{2,1,0:T(8,128)S(1)} %get-tuple-element.59), channel_id=1, source_target_pairs={{0,3},{1,2},{2,1},{3,0},{4,7},{5,6},{6,5},{7,4},{8,11},{9,10},{10,... | collective-permute-start | bytes 786440 | tf_op jit(solution)/shard_map/ppermute | solution.py:404
  60.6 7.9 %collective-permute-start.13 = (f32[8,8,1024]{2,1,0:T(8,128)S(1)}, f32[8,8,1024]{2,1,0:T(8,128)S(1)}, u32[]{:S(2)}, u32[]{:S(2)}) collective-permute-start(f32[8,8,1024]{2,1,0:T(8,128)S(1)} %get-tuple-element.64), channel_id=1, source_target_pairs={{0,1},{1,0},{2,3},{3,2},{4,5},{5,4},{6,7},{7,6},{8,9},{9,8},{10,11... | collective-permute-start | bytes 786440 | tf_op jit(solution)/shard_map/ppermute | solution.py:404
  62.0 8.8 %collective-permute-start.14 = (f32[8,8,1024]{2,1,0:T(8,128)S(1)}, f32[8,8,1024]{2,1,0:T(8,128)S(1)}, u32[]{:S(2)}, u32[]{:S(2)}) collective-permute-start(f32[8,8,1024]{2,1,0:T(8,128)S(1)} %get-tuple-element.65), channel_id=1, source_target_pairs={{0,2},{1,3},{2,0},{3,1},{4,6},{5,7},{6,4},{7,5},{8,10},{9,11},{10,... | collective-permute-start | bytes 786440 | tf_op jit(solution)/shard_map/ppermute | solution.py:404
  62.8 12.4 %collective-permute-start.15 = (f32[8,8,1024]{2,1,0:T(8,128)S(1)}, f32[8,8,1024]{2,1,0:T(8,128)S(1)}, u32[]{:S(2)}, u32[]{:S(2)}) collective-permute-start(f32[8,8,1024]{2,1,0:T(8,128)S(1)} %get-tuple-element.66), channel_id=1, source_target_pairs={{0,3},{1,2},{2,1},{3,0},{4,7},{5,6},{6,5},{7,4},{8,11},{9,10},{10,... | collective-permute-start | bytes 786440 | tf_op jit(solution)/shard_map/ppermute | solution.py:404
